TPU v7x, 32 devices: a whole 2x2x4 slice. The times are simulated.
32 devices in a mesh: exp: 8 (over y, x, core), tp: 4 (over z).
Axes of the slice: x: 2, y: 2, z: 4, core: 2. Of those that a mesh axis runs over, the one named last changes fastest.
Arguments:
- tokens: bfloat16 [8192, 1024], P(('exp', 'tp')), may hold values from -6 to 6
- norm1_gain: float32 [1024], replicated, may hold values from 0.5 to 1.5
- w_query: bfloat16 [1024, 1024], P(None, 'tp'), may hold values from -0.1875 to 0.1875
- w_key_value: bfloat16 [1024, 8, 128], P(None, 'tp'), may hold values from -0.1875 to 0.1875
- w_out: bfloat16 [1024, 1024], P('tp'), may hold values from -2 to 2
- norm2_gain: float32 [1024], replicated, may hold values from 0.5 to 1.5
- w_router: bfloat16 [1024, 32], replicated, may hold values from -0.09375 to 0.09375
- w_gate_up: bfloat16 [32, 1024, 1024], P('exp'), may hold values from -0.1875 to 0.1875
- w_down: bfloat16 [32, 512, 1024], P('exp'), may hold values from -0.75 to 0.75
- routes: int32 [8192, 8], P(('exp', 'tp')), may hold values from 0 to 31, all different within a row; in each aligned block of 256 rows (0 to 255, 256 to 511, ...) at most 80 rows name the same one
- prefix: int32 [8], P('exp'), may hold values from 102 to 512
- cotangent: bfloat16 [8192, 1024], P(('exp', 'tp')), may hold values from -6 to 6
Outputs:
- layer_out: bfloat16 [8192, 1024], P(('exp', 'tp'))
- input_grad: float32 [8192, 1024], P(('exp', 'tp'))
- norm1_grad: float32 [1024], replicated
- query_grad: float32 [1024, 1024], P(None, 'tp')
- key_value_grad: float32 [1024, 8, 128], P(None, 'tp')
- out_grad: float32 [1024, 1024], P('tp')
- norm2_grad: float32 [1024], replicated
- router_grad: float32 [1024, 32], replicated
- gate_up_grad: float32 [32, 1024, 1024], P('exp')
- down_grad: float32 [32, 512, 1024], P('exp')
Inputs may be any that keep to these rules, and one draw needn't show every extreme that they name: `routes`: each row names 8 different experts; in each aligned block of 256 rows (the rows of one device) no expert is named by more than 80 rows, a bound that some block reaches.
All inputs are finite; a program needn't handle non-finite values.
Results may differ from a plain program's by a relative error of at most 0.024.
Values may be sent and summed in bfloat16 or wider, within the bound.
A program may use at most 192 MiB of HBM per device.

v0:
```python
import jax
import jax.numpy as jnp
from jax import lax
from jax.sharding import PartitionSpec as P

D = 1024
H = 16
KVH = 8
HD = 64
FF = 512


epsilon = 1e-06
masked_score = -1e30


def row_scaling(values):
    inverse = lax.rsqrt(jnp.mean(values * values, axis=-1, keepdims=True) + epsilon)
    return (values * inverse, inverse)


def norm_backward(gradient, scaled, inverse, gain_vector):
    weighted = gradient * gain_vector
    inner_mean = jnp.mean(weighted * scaled, axis=-1, keepdims=True)
    return (inverse * (weighted - scaled * inner_mean), jnp.sum(gradient * scaled, axis=0))


def attention_shapes(queries, key_value, prefix):
    seq_count = prefix.shape[0]
    length = queries.shape[0] // seq_count
    block_rows = min(512, length)
    kv_local = key_value.shape[1] // (2 * HD)
    return (seq_count, length, block_rows, length // block_rows, kv_local)


def block_inputs(queries, key_value, prefix, block_index, length, block_rows, block_count):
    sequence = block_index // block_count
    first_row = block_index % block_count * block_rows
    query_block = lax.dynamic_slice_in_dim(queries, sequence * length + first_row, block_rows, 0)
    prefix_len = lax.dynamic_index_in_dim(prefix, sequence, 0, keepdims=False)
    row_ids = first_row + jnp.arange(block_rows, dtype=jnp.int32)
    col_ids = jnp.arange(length, dtype=jnp.int32)
    visible = (col_ids[None, :] <= row_ids[:, None]) | (col_ids[None, :] < prefix_len)
    return (query_block, key_value, visible, first_row)


def head_scores(query_head, key_head, visible):
    scores = lax.dot_general(
        query_head, key_head, (((1,), (1,)), ((), ())), preferred_element_type=jnp.float32
    ) * HD ** (-0.5)
    return jnp.where(visible, scores, masked_score)


def attention_forward(queries, key_value, prefix):
    seq_count, length, block_rows, block_count, kv_local = attention_shapes(
        queries, key_value, prefix
    )
    head_groups = H // KVH

    def one_block(block_index):
        query_block, pair_seq, visible, first_row = block_inputs(
            queries, key_value, prefix, block_index, length, block_rows, block_count
        )
        outputs = []
        totals = []
        for kv_head in range(kv_local):
            key_head = pair_seq[:, kv_head * 2 * HD : kv_head * 2 * HD + HD]
            value_head = pair_seq[:, kv_head * 2 * HD + HD : (kv_head + 1) * 2 * HD]
            for group in range(head_groups):
                head = kv_head * head_groups + group
                query_head = query_block[:, head * HD : (head + 1) * HD]
                scores = head_scores(query_head, key_head, visible)
                row_max = jnp.max(scores, axis=-1, keepdims=True)
                exp_scores = jnp.exp(scores - row_max)
                row_total = jnp.sum(exp_scores, axis=-1, keepdims=True)
                probs_low = (exp_scores / row_total).astype(jnp.bfloat16)
                mixed_head = jnp.dot(probs_low, value_head, preferred_element_type=jnp.float32)
                outputs.append(mixed_head.astype(jnp.bfloat16))
                totals.append((row_max + jnp.log(row_total))[:, 0])
        return (jnp.concatenate(outputs, axis=-1), jnp.stack(totals, axis=0))

    mixed_heads, log_totals = lax.map(
        one_block, jnp.arange(seq_count * block_count, dtype=jnp.int32)
    )
    return (mixed_heads.reshape(queries.shape[0], -1), log_totals)


def attention_backward(queries, key_value, prefix, dmixed, log_totals):
    seq_count, length, block_rows, block_count, kv_local = attention_shapes(
        queries, key_value, prefix
    )
    head_groups = H // KVH
    score_scale = HD ** (-0.5)

    def one_block(block_index):
        query_block, pair_seq, visible, first_row = block_inputs(
            queries, key_value, prefix, block_index, length, block_rows, block_count
        )
        sequence = block_index // block_count
        grad_block = lax.dynamic_slice_in_dim(dmixed, sequence * length + first_row, block_rows, 0)
        block_totals = lax.dynamic_index_in_dim(log_totals, block_index, 0, keepdims=False)
        dquery_parts = []
        dpair_parts = []
        for kv_head in range(kv_local):
            key_head = pair_seq[:, kv_head * 2 * HD : kv_head * 2 * HD + HD]
            value_head = pair_seq[:, kv_head * 2 * HD + HD : (kv_head + 1) * 2 * HD]
            dkeys = jnp.zeros((length, HD), jnp.float32)
            dvalues = jnp.zeros((length, HD), jnp.float32)
            for group in range(head_groups):
                head = kv_head * head_groups + group
                query_head = query_block[:, head * HD : (head + 1) * HD]
                grad_head = grad_block[:, head * HD : (head + 1) * HD]
                scores = head_scores(query_head, key_head, visible)
                probs = jnp.exp(scores - block_totals[head][:, None])
                dprobs = lax.dot_general(
                    grad_head,
                    value_head,
                    (((1,), (1,)), ((), ())),
                    preferred_element_type=jnp.float32,
                )
                dscores = (
                    probs * (dprobs - jnp.sum(probs * dprobs, axis=-1, keepdims=True))
                ).astype(jnp.bfloat16)
                dquery_parts.append(
                    jnp.dot(dscores, key_head, preferred_element_type=jnp.float32) * score_scale
                )
                dkeys = (
                    dkeys
                    + lax.dot_general(
                        dscores,
                        query_head,
                        (((0,), (0,)), ((), ())),
                        preferred_element_type=jnp.float32,
                    )
                    * score_scale
                )
                dvalues = dvalues + lax.dot_general(
                    probs.astype(jnp.bfloat16),
                    grad_head,
                    (((0,), (0,)), ((), ())),
                    preferred_element_type=jnp.float32,
                )
            dpair_parts.append(dkeys)
            dpair_parts.append(dvalues)
        return (jnp.concatenate(dquery_parts, axis=-1), jnp.concatenate(dpair_parts, axis=-1))

    dquery, dpairs = lax.map(one_block, jnp.arange(seq_count * block_count, dtype=jnp.int32))
    dquery = dquery.reshape(queries.shape).astype(jnp.bfloat16)
    dpairs = jnp.sum(dpairs.reshape(seq_count, block_count, length, dpairs.shape[-1]), axis=1)
    return (dquery, dpairs.reshape(key_value.shape).astype(jnp.bfloat16))


def local(
    tokens,
    norm1_gain,
    w_query,
    w_key_value,
    w_out,
    norm2_gain,
    w_router,
    w_gate_up,
    w_down,
    routes,
    prefix,
    cotangent,
):
    own_rows = tokens.shape[0]
    experts = w_router.shape[1]
    top_k = routes.shape[1]
    capacity = own_rows * top_k * 5 // (experts * 4)
    local_experts = w_gate_up.shape[0]
    pair_weight = w_key_value.reshape(w_key_value.shape[0], -1)
    token_values = tokens.astype(jnp.float32)
    scaled1, inverse1 = row_scaling(token_values)
    normed1 = (scaled1 * norm1_gain).astype(jnp.bfloat16)
    gathered = lax.all_gather(normed1, "tp", axis=0, tiled=True)
    queries = jnp.dot(gathered, w_query, preferred_element_type=jnp.float32).astype(jnp.bfloat16)
    key_value = jnp.dot(gathered, pair_weight, preferred_element_type=jnp.float32).astype(
        jnp.bfloat16
    )
    mixed, log_totals = attention_forward(queries, key_value, prefix)
    summed = lax.psum(
        jnp.dot(mixed, w_out, preferred_element_type=jnp.float32).astype(jnp.bfloat16), "tp"
    ).astype(jnp.float32)
    attended = lax.dynamic_slice_in_dim(summed, lax.axis_index("tp") * own_rows, own_rows, 0)
    hidden = token_values + attended
    scaled2, inverse2 = row_scaling(hidden)
    normed_moe = (scaled2 * norm2_gain).astype(jnp.bfloat16)
    logits = jnp.dot(normed_moe, w_router, preferred_element_type=jnp.float32)
    chosen = jnp.take_along_axis(logits, routes, axis=1)
    gate_weights = jax.nn.softmax(chosen, axis=-1)
    assign_count = own_rows * top_k
    flat_routes = routes.reshape(assign_count)
    matches = (flat_routes[:, None] == jnp.arange(experts, dtype=jnp.int32)[None, :]).astype(
        jnp.int32
    )
    position = jnp.sum((jnp.cumsum(matches, axis=0) - matches) * matches, axis=1)
    slot_index = flat_routes * capacity + position
    sources = jnp.full((experts * capacity,), assign_count, jnp.int32)
    sources = sources.at[slot_index].set(jnp.arange(assign_count, dtype=jnp.int32))
    padded = jnp.concatenate([normed_moe, jnp.zeros((1, D), jnp.bfloat16)], axis=0)
    outgoing = padded[sources // top_k].reshape(experts, capacity, D)
    received = lax.all_to_all(outgoing, "exp", split_axis=0, concat_axis=0, tiled=True)
    source_count = received.shape[0] // local_experts
    block_slots = received.shape[1]
    grouped = received.reshape(source_count, local_experts, block_slots, D)
    units = jnp.einsum("nscd,sdf->nscf", grouped, w_gate_up, preferred_element_type=jnp.float32)
    active = (jax.nn.silu(units[..., :FF]) * units[..., FF:]).astype(jnp.bfloat16)
    produced = jnp.einsum("nscf,sfd->nscd", active, w_down, preferred_element_type=jnp.float32)
    produced = produced.astype(jnp.bfloat16).reshape(received.shape)
    returned = lax.all_to_all(produced, "exp", split_axis=0, concat_axis=0, tiled=True)
    results = (returned, received)
    returned = results[0]
    received = results[1]
    picked = (
        returned.reshape(experts * capacity, D)[slot_index]
        .reshape(own_rows, top_k, D)
        .astype(jnp.float32)
    )
    mixture = jnp.sum(gate_weights[:, :, None] * picked, axis=1)
    layer_out = (hidden + mixture).astype(jnp.bfloat16)
    upstream = cotangent.astype(jnp.float32)
    dgates = jnp.sum(upstream[:, None, :] * picked, axis=-1)
    dchosen = gate_weights * (dgates - jnp.sum(gate_weights * dgates, axis=-1, keepdims=True))
    onehot = (routes[:, :, None] == jnp.arange(experts, dtype=jnp.int32)[None, None, :]).astype(
        jnp.float32
    )
    dlogits = jnp.sum(onehot * dchosen[:, :, None], axis=1).astype(jnp.bfloat16)
    dexpert_out = (
        (gate_weights[:, :, None] * upstream[:, None, :])
        .astype(jnp.bfloat16)
        .reshape(assign_count, D)
    )
    grad_padded = jnp.concatenate([dexpert_out, jnp.zeros((1, D), jnp.bfloat16)], axis=0)
    grad_outgoing = grad_padded[sources].reshape(experts, capacity, D)
    grad_received = lax.all_to_all(grad_outgoing, "exp", split_axis=0, concat_axis=0, tiled=True)
    source_count = received.shape[0] // local_experts
    split_shape = (source_count, local_experts, capacity, D)
    expert_in = received.reshape(split_shape)
    expert_dout = grad_received.reshape(split_shape)
    units = jnp.einsum("nscd,sdf->nscf", expert_in, w_gate_up, preferred_element_type=jnp.float32)
    gate_part = units[..., :FF]
    up_part = units[..., FF:]
    sigmoid = jax.nn.sigmoid(gate_part)
    silu_gate = gate_part * sigmoid
    active = (silu_gate * up_part).astype(jnp.bfloat16)
    down_grad = jnp.einsum(
        "nscf,nscd->sfd", active, expert_dout, preferred_element_type=jnp.float32
    )
    dactive = jnp.einsum("nscd,sfd->nscf", expert_dout, w_down, preferred_element_type=jnp.float32)
    dgate = dactive * up_part * sigmoid * (1.0 + gate_part * (1.0 - sigmoid))
    dunits = jnp.concatenate([dgate, dactive * silu_gate], axis=-1).astype(jnp.bfloat16)
    gate_up_grad = jnp.einsum(
        "nscd,nscf->sdf", expert_in, dunits, preferred_element_type=jnp.float32
    )
    dexpert_in = jnp.einsum("nscf,sdf->nscd", dunits, w_gate_up, preferred_element_type=jnp.float32)
    dexpert_in = dexpert_in.astype(jnp.bfloat16).reshape(received.shape)
    grad_back = lax.all_to_all(dexpert_in, "exp", split_axis=0, concat_axis=0, tiled=True)
    from_experts = grad_back.reshape(experts * capacity, D)[slot_index].reshape(own_rows, top_k, D)
    dnormed2 = jnp.sum(from_experts.astype(jnp.float32), axis=1)
    dnormed2 = dnormed2 + jnp.einsum(
        "te,de->td", dlogits, w_router, preferred_element_type=jnp.float32
    )
    router_grad = jnp.einsum("td,te->de", normed_moe, dlogits, preferred_element_type=jnp.float32)
    dhidden_norm, norm2_part = norm_backward(dnormed2, scaled2, inverse2, norm2_gain)
    dhidden = upstream + dhidden_norm
    dhidden_low = dhidden.astype(jnp.bfloat16)
    dfull = lax.all_gather(dhidden_low, "tp", axis=0, tiled=True)
    out_grad = jnp.einsum("tf,td->fd", mixed, dfull, preferred_element_type=jnp.float32)
    dmixed = jnp.einsum("td,fd->tf", dfull, w_out, preferred_element_type=jnp.float32).astype(
        jnp.bfloat16
    )
    dqueries, dkey_value = attention_backward(queries, key_value, prefix, dmixed, log_totals)
    query_grad = jnp.einsum("td,tf->df", gathered, dqueries, preferred_element_type=jnp.float32)
    key_value_grad = jnp.einsum(
        "td,tf->df", gathered, dkey_value, preferred_element_type=jnp.float32
    )
    key_value_grad = key_value_grad.reshape(w_key_value.shape)
    rows_query = lax.slice_in_dim(dqueries, 0, own_rows * lax.axis_size("tp"), axis=0)
    from_query = jnp.einsum("tf,df->td", rows_query, w_query, preferred_element_type=jnp.float32)
    from_pair = jnp.einsum("tf,df->td", dkey_value, pair_weight, preferred_element_type=jnp.float32)
    dnormed1 = lax.psum_scatter(
        (from_query + from_pair).astype(jnp.bfloat16), "tp", scatter_dimension=0, tiled=True
    ).astype(jnp.float32)
    dtokens_norm, norm1_part = norm_backward(dnormed1, scaled1, inverse1, norm1_gain)
    input_grad = dhidden + dtokens_norm
    query_grad, key_value_grad, out_grad = (
        lax.psum(query_grad.astype(jnp.bfloat16), "exp").astype(jnp.float32),
        lax.psum(key_value_grad.astype(jnp.bfloat16), "exp").astype(jnp.float32),
        lax.psum(out_grad.astype(jnp.bfloat16), "exp").astype(jnp.float32),
    )
    gate_up_grad, down_grad = (
        lax.psum(gate_up_grad.astype(jnp.bfloat16), "tp").astype(jnp.float32),
        lax.psum(down_grad.astype(jnp.bfloat16), "tp").astype(jnp.float32),
    )
    router_grad, norm1_grad, norm2_grad = lax.psum(
        (router_grad, norm1_part, norm2_part), ("exp", "tp")
    )
    return (
        layer_out,
        input_grad,
        norm1_grad,
        query_grad,
        key_value_grad,
        out_grad,
        norm2_grad,
        router_grad,
        gate_up_grad,
        down_grad,
    )


def solution(mesh):
    return jax.shard_map(
        local,
        mesh=mesh,
        in_specs=(
            P(("exp", "tp"), None),
            P(),
            P(None, "tp"),
            P(None, "tp", None),
            P("tp", None),
            P(),
            P(),
            P("exp", None, None),
            P("exp", None, None),
            P(("exp", "tp"), None),
            P("exp"),
            P(("exp", "tp"), None),
        ),
        out_specs=(
            P(("exp", "tp"), None),
            P(("exp", "tp"), None),
            P(),
            P(None, "tp"),
            P(None, "tp", None),
            P("tp", None),
            P(),
            P(),
            P("exp", None, None),
            P("exp", None, None),
        ),
        check_vma=False,
    )
```

profile of v0, /device:TPU:8, one launch (start us, length us, event | category | flops | bytes accessed | tf_op | source)
XLA Modules:
  0.0 1286.6 jit_solution(9288011412051385500)
XLA Ops:
  9.1 2.0 fusion.111
  11.3 45.6 %all-gather.3.cloned.1.call-done = bf16[1024,1024]{1,0:T(8,128)(2,1)} async-done(((bf16[256,1024]{1,0:T(8,128)(2,1)}), bf16[1024,1024]{1,0:T(8,128)(2,1)}) %all-gather.3.cloned.1.call-update) | async-done | bytes 2097168 | tf_op jit(solution)/shard_map/all_gather | solution.py:176
  56.8 2.5 convolution_convert_fusion.8
  60.8 32.1 %while.28 = (s32[]{:T(128)}, bf16[2,512,256]{2,1,0:T(8,128)(2,1)S(1)}, f32[2,4,512]{2,1,0:T(4,128)S(1)}, s32[2]{0:T(128)S(1)}, s32[1]{0:T(128)}, /*index=5*/bf16...) while((s32[]{:T(128)}, ...), condition=%wide.region_10.11_spmd, body=%wide.region_1.10_spmd.sunk | while | flops 559027712 | bytes 29720056 | solution.py:82
  93.0 2.0 convolution_convert_fusion.4
  95.7 9.1 reduce-window.6
  105.7 8.5 scatter_custom_fusion
  114.2 66.7 %all-reduce.10.cloned.1.call-done = bf16[1024,1024]{1,0:T(8,128)(2,1)} async-done(((bf16[1024,1024]{1,0:T(8,128)(2,1)}), bf16[1024,1024]{1,0:T(8,128)(2,1)}) %all-reduce.10.cloned.1.call-update) | async-done | bytes 2097168 | tf_op jit(solution)/shard_map/psum | solution.py:182
  183.6 8.8 gather_fusion
  192.4 4.8 all-to-all-start
  197.9 16.8 %gather_fusion.4 = f32[2048]{0:T(1024)S(1)} fusion(f32[256,32]{0,1:T(8,128)S(1)} %fusion.139, s32[2048]{0:T(1024)S(1)} %reshape.403), kind=kCustom, calls=%fused_computation.4 | custom fusion | bytes 32768 | tf_op jit(solution)/shard_map/jit(take_along_axis)/gather | solution.py:190
  215.8 2.5 concatenate.29
  218.3 14.8 %gather_fusion.2 = bf16[2560,1024]{1,0:T(8,128)(2,1)} fusion(bf16[2049,1024]{1,0:T(8,128)(2,1)} %concatenate.29, s32[3072]{0:T(1024)S(1)} %pad_clamp_fusion), kind=kCustom, calls=%fused_computation.2 | custom fusion | bytes 10496000 | tf_op jit(solution)/shard_map/gather | solution.py:235
  233.1 24.5 %all-to-all-done = bf16[32,80,1024]{2,1,0:T(8,128)(2,1)} async-done(((bf16[32,80,1024]{2,1,0:T(8,128)(2,1)}), bf16[32,80,1024]{2,1,0:T(8,128)(2,1)}, u32[]{:S(2)}, u32[]{:S(2)}) %all-to-all-start) | async-done | bytes 5242912 | tf_op jit(solution)/shard_map/all_to_all | solution.py:203
  257.6 4.7 all-to-all-start.2
  262.2 12.3 fusion.88
  274.6 48.0 %all-to-all-done.2 = bf16[32,80,1024]{2,1,0:T(8,128)(2,1)} async-done(((bf16[32,80,1024]{2,1,0:T(8,128)(2,1)}), bf16[32,80,1024]{2,1,0:T(8,128)(2,1)}, u32[]{:S(2)}, u32[]{:S(2)}) %all-to-all-start.2) | async-done | bytes 5242912 | tf_op jit(solution)/shard_map/all_to_all | solution.py:236
  322.6 11.6 fusion.76
  334.2 10.0 convert_bitcast_fusion
  344.3 3.0 copy.101
  347.3 4.6 all-to-all-start.3
  351.9 5.9 convert_bitcast_fusion.1
  357.8 3.1 copy.98
  360.9 51.4 %all-to-all-done.3 = bf16[32,80,1024]{2,1,0:T(8,128)(2,1)} async-done(((bf16[32,80,1024]{2,1,0:T(8,128)(2,1)}), bf16[32,80,1024]{2,1,0:T(8,128)(2,1)}, u32[]{:S(2)}, u32[]{:S(2)}) %all-to-all-start.3) | async-done | bytes 5242912 | tf_op jit(solution)/shard_map/all_to_all | solution.py:258
  412.3 4.7 all-to-all-start.1
  417.2 14.1 %gather_fusion.3 = bf16[2048,1024]{1,0:T(8,128)(2,1)} fusion(bf16[2560,1024]{1,0:T(8,128)(2,1)} %bitcast.42, s32[2048]{0:T(1024)S(1)} %broadcast_clamp_fusion), kind=kCustom, calls=%fused_computation.3 | custom fusion | bytes 8396800 | tf_op jit(solution)/shard_map/gather | solution.py:259
  431.3 6.4 convert_reduce_fusion
  437.7 39.6 %all-to-all-done.1 = bf16[32,80,1024]{2,1,0:T(8,128)(2,1)} async-done(((bf16[32,80,1024]{2,1,0:T(8,128)(2,1)}), bf16[32,80,1024]{2,1,0:T(8,128)(2,1)}, u32[]{:S(2)}, u32[]{:S(2)}) %all-to-all-start.1) | async-done | bytes 5242912 | tf_op jit(solution)/shard_map/all_to_all | solution.py:211
  477.3 14.1 %gather_fusion.1 = bf16[2048,1024]{1,0:T(8,128)(2,1)} fusion(bf16[2560,1024]{1,0:T(8,128)(2,1)} %bitcast.32, s32[2048]{0:T(1024)S(1)} %broadcast_clamp_fusion), kind=kCustom, calls=%fused_computation.1 | custom fusion | bytes 8396800 | tf_op jit(solution)/shard_map/gather | solution.py:216
  491.4 6.1 fusion.68
  500.7 2.2 fusion.134
  503.2 42.8 %all-gather.5.cloned.1.call-done = bf16[1024,1024]{1,0:T(8,128)(2,1)} async-done(((bf16[256,1024]{1,0:T(8,128)(2,1)}), bf16[1024,1024]{1,0:T(8,128)(2,1)}) %all-gather.5.cloned.1.call-update) | async-done | bytes 2097168 | tf_op jit(solution)/shard_map/all_gather | solution.py:268
  546.0 2.3 convolution_convert_fusion.7
  548.4 57.3 %while.29 = (s32[]{:T(128)}, bf16[2,512,256]{2,1,0:T(8,128)(2,1)}, f32[2,1024,256]{1,2,0:T(8,128)}, s32[2]{0:T(128)S(1)}, s32[1]{0:T(128)}, /*index=5*/bf16[1024...) while((s32[]{:T(128)}, bf16[2,512,256]{2,1,0:T(8,128)(2,1)}, ...), condition=%wide.region_30.31_spmd, body=%wide.region_25.30_spmd.sunk | while | flops 1367735808 | bytes 75292352 | solution.py:147
  607.6 3.3 convolution_convert_fusion.5
  615.0 2.1 add_convert_fusion
  617.3 9.1 bitcast_convert_fusion.1
  626.4 11.6 bitcast_convert_fusion
  639.9 34.1 %all-reduce.14.cloned.1.call-done = (bf16[1024,256]{1,0:T(8,128)(2,1)}, bf16[1024,2,128]{2,0,1:T(8,128)(2,1)}, bf16[256,1024]{1,0:T(8,128)(2,1)}) async-done(((bf16[1024,256]{1,0:T(8,128)(2,1)}, bf16[1024,2,128]{2,0,1:T(8,128)(2,1)}, bf16[256,1024]{1,0:T(8,128)(2,1)}), (bf16[1024,256]{1,0:T(8,128)(2,1)}, bf16[1024,2,128]{2,0,1:T(8,128)(2,1)}, bf16[256,1024]{1,0:T(8,128)(2,1)})) %all-reduce.14.cloned.1.call-update) | async-done | bytes 1572880 | tf_op jit(solution)/shard_map/psum | solution.py:288
  674.1 2.1 convert_element_type.260
  676.2 2.7 copy.108
  680.0 37.0 %reduce-scatter.2.cloned.1.call-done = bf16[256,1024]{1,0:T(8,128)(2,1)} async-done(((bf16[1024,1024]{1,0:T(8,128)(2,1)}), bf16[256,1024]{1,0:T(8,128)(2,1)}) %reduce-scatter.2.cloned.1.call-update) | async-done | bytes 524304 | tf_op jit(solution)/shard_map/reduce_scatter | solution.py:282
  718.5 3.4 fusion.110
  721.9 47.1 %all-reduce.2 = (f32[1024]{0:T(1024)}, f32[1024]{0:T(1024)}) all-reduce(f32[1024]{0:T(1024)S(1)} %get-tuple-element.278, f32[1024]{0:T(1024)S(1)} %get-tuple-element.276), channel_id=1, replica_groups=mesh['exp'=8,'tp'=4] {'exp','tp'}, use_global_device_ids=true, to_apply=%region_35.36 | all-reduce | flops 2048 | bytes 16384 | tf_op jit(solution)/shard_map/psum | solution.py:296
  769.1 378.3 %all-reduce.16.cloned.1.call-done = (bf16[4,1024,1024]{2,1,0:T(8,128)(2,1)}, bf16[4,512,1024]{2,1,0:T(8,128)(2,1)}) async-done(((bf16[4,1024,1024]{2,1,0:T(8,128)(2,1)}, bf16[4,512,1024]{2,1,0:T(8,128)(2,1)}), (bf16[4,1024,1024]{2,1,0:T(8,128)(2,1)}, bf16[4,512,1024]{2,1,0:T(8,128)(2,1)})) %all-reduce.16.cloned.1.call-update) | async-done | bytes 12582928 | tf_op jit(solution)/shard_map/psum | solution.py:293
  1147.4 11.9 convert_element_type.267
  1159.2 4.4 convert_element_type.269
  1163.7 114.4 %all-reduce.12.cloned.1.call-done = f32[1024,32]{0,1:T(8,128)} async-done(((f32[1024,32]{0,1:T(8,128)}), f32[1024,32]{0,1:T(8,128)}) %all-reduce.12.cloned.1.call-update) | async-done | bytes 131088 | tf_op jit(solution)/shard_map/psum | solution.py:296
  (253 shorter events, 100.5 us)
Async XLA Ops:
  7.2 85.8 %copy-start = (bf16[256,1024]{1,0:T(8,128)(2,1)S(1)}, bf16[256,1024]{1,0:T(8,128)(2,1)}, u32[]{:S(2)}) copy-start(bf16[256,1024]{1,0:T(8,128)(2,1)} %param.20) | copy-start | bytes 1572868
  7.2 49.7 %copy-start.14 = (bf16[1024,2,128]{2,1,0:T(2,128)(2,1)S(1)}, bf16[1024,2,128]{2,1,0:T(2,128)(2,1)}, u32[]{:S(2)}) copy-start(bf16[1024,2,128]{2,1,0:T(2,128)(2,1)} %param.19) | copy-start | bytes 1572868
  7.2 49.6 %all-gather.3.cloned.1.call-start = ((), (), s32[]{:S(2)}) async-start(), calls=%async_computation.5 | async-start | bytes 2621440 | tf_op jit(solution)/shard_map/all_gather | solution.py:176
  8.6 0.6 copy-start.29
  11.2 48.1 %copy-start.16 = (bf16[1024,256]{1,0:T(8,128)(2,1)S(1)}, bf16[1024,256]{1,0:T(8,128)(2,1)}, u32[]{:S(2)}) copy-start(bf16[1024,256]{1,0:T(8,128)(2,1)} %param.18) | copy-start | bytes 1572868
  11.2 169.8 %all-reduce.10.cloned.1.call-start = ((), (), s32[]{:S(2)}) async-start(), calls=%async_computation.6 | async-start | bytes 4194304 | tf_op jit(solution)/shard_map/psum | solution.py:182
  56.8 2.5 copy-start.31
  92.9 2.1 copy-start.1
  92.9 2.1 copy-start.12
  92.9 2.1 copy-start.22
  92.9 2.1 copy-start.20
  95.0 85.9 %copy-start.3 = (bf16[256,1024]{1,0:T(8,128)(2,1)S(1)}, bf16[256,1024]{1,0:T(8,128)(2,1)}, u32[]{:S(2)}) copy-start(bf16[256,1024]{1,0:T(8,128)(2,1)} %param.16) | copy-start | bytes 1572868
  95.2 87.1 %copy-start.24 = (f32[1024]{0:T(1024)S(1)}, f32[1024]{0:T(1024)}, u32[]{:S(2)}) copy-start(f32[1024]{0:T(1024)} %param.21) | copy-start | bytes 12292
  182.3 10.1 copy-start.27
  183.6 14.0 %copy-start.7 = (bf16[256,1024]{1,0:T(8,128)(2,1)}, bf16[256,1024]{1,0:T(8,128)(2,1)S(1)}, u32[]{:S(2)}) copy-start(bf16[256,1024]{1,0:T(8,128)(2,1)S(1)} %multiply_convert_fusion.5) | copy-start | bytes 1572868
  192.4 5.1 copy-start.9
  192.4 5.2 copy-start.21
  192.4 65.2 %all-to-all-start = ((bf16[32,80,1024]{2,1,0:T(8,128)(2,1)}), bf16[32,80,1024]{2,1,0:T(8,128)(2,1)}, u32[]{:S(2)}, u32[]{:S(2)}) async-start(bf16[32,80,1024]{2,1,0:T(8,128)(2,1)} %bitcast.210), calls=%async_computation | async-start | bytes 10485760 | tf_op jit(solution)/shard_map/all_to_all | solution.py:203
  257.6 65.0 %all-to-all-start.2 = ((bf16[32,80,1024]{2,1,0:T(8,128)(2,1)}), bf16[32,80,1024]{2,1,0:T(8,128)(2,1)}, u32[]{:S(2)}, u32[]{:S(2)}) async-start(bf16[32,80,1024]{2,1,0:T(8,128)(2,1)} %bitcast.211), calls=%async_computation.2 | async-start | bytes 10485760 | tf_op jit(solution)/shard_map/all_to_all | solution.py:236
  347.3 65.0 %all-to-all-start.3 = ((bf16[32,80,1024]{2,1,0:T(8,128)(2,1)}), bf16[32,80,1024]{2,1,0:T(8,128)(2,1)}, u32[]{:S(2)}, u32[]{:S(2)}) async-start(bf16[32,80,1024]{2,1,0:T(8,128)(2,1)} %bitcast.213), calls=%async_computation.3 | async-start | bytes 10485760 | tf_op jit(solution)/shard_map/all_to_all | solution.py:258
  412.3 65.0 %all-to-all-start.1 = ((bf16[32,80,1024]{2,1,0:T(8,128)(2,1)}), bf16[32,80,1024]{2,1,0:T(8,128)(2,1)}, u32[]{:S(2)}, u32[]{:S(2)}) async-start(bf16[32,80,1024]{2,1,0:T(8,128)(2,1)} %bitcast.212), calls=%async_computation.1 | async-start | bytes 10485760 | tf_op jit(solution)/shard_map/all_to_all | solution.py:211
  417.0 129.0 %all-gather.5.cloned.1.call-start = ((), (), s32[]{:S(2)}) async-start(), calls=%async_computation.7 | async-start | bytes 2621440 | tf_op jit(solution)/shard_map/all_gather | solution.py:268
  491.4 6.3 copy-start.4
  491.4 6.3 copy-start.25
  491.4 6.3 copy-start.28
  499.7 1.0 copy-start.5
  502.9 171.1 %all-reduce.14.cloned.1.call-start = ((), (), s32[]{:S(2)}) async-start(), calls=%async_computation.10 | async-start | bytes 3145728 | tf_op jit(solution)/shard_map/psum | solution.py:288
  503.2 45.2 %copy-start.2 = (bf16[1024,256]{1,0:T(8,128)(2,1)S(1)}, bf16[1024,256]{1,0:T(8,128)(2,1)}, u32[]{:S(2)}) copy-start(bf16[1024,256]{1,0:T(8,128)(2,1)} %copy-done.1) | copy-start | bytes 1572868
  503.2 45.2 %copy-start.23 = (f32[2,4,512]{2,1,0:T(4,128)S(1)}, f32[2,4,512]{2,1,0:T(4,128)}, u32[]{:S(2)}) copy-start(f32[2,4,512]{2,1,0:T(4,128)} %copy-done.22) | copy-start | bytes 49156
  605.7 1.9 copy-start.13
  607.6 3.3 copy-start.32
  610.8 1.6 copy-start.19
  612.4 1.6 copy-start.17
  614.0 1.0 copy-start.15
  614.0 103.0 %reduce-scatter.2.cloned.1.call-start = ((), (), s32[]{:S(2)}) async-start(), calls=%async_computation.8 | async-start | bytes 2621440 | tf_op jit(solution)/shard_map/reduce_scatter | solution.py:282
  617.2 530.2 %all-reduce.16.cloned.1.call-start = ((), (), s32[]{:S(2)}) async-start(), calls=%async_computation.11 | async-start | bytes 25165824 | tf_op jit(solution)/shard_map/psum | solution.py:293
  617.2 9.1 copy-start.33
  617.3 9.1 copy-start.34
  638.0 1.0 copy-start.8
  638.0 640.0 %all-reduce.12.cloned.1.call-start = ((), (), s32[]{:S(2)}) async-start(), calls=%async_computation.9 | async-start | bytes 262144 | tf_op jit(solution)/shard_map/psum | solution.py:296
  674.0 4.8 copy-start.18
  674.0 42.9 %copy-start.26 = (f32[1024]{0:T(1024)S(1)}, f32[1024]{0:T(1024)}, u32[]{:S(2)}) copy-start(f32[1024]{0:T(1024)} %param.17) | copy-start | bytes 12292
  674.1 42.9 %copy-start.30 = (f32[256]{0:T(256)S(1)}, f32[256]{0:T(256)}, u32[]{:S(2)}) copy-start(f32[256]{0:T(256)} %copy-done.29) | copy-start | bytes 3076
  676.2 42.3 %copy-start.6 = (f32[256,1024]{1,0:T(8,128)S(1)}, f32[256,1024]{1,0:T(8,128)}, u32[]{:S(2)}) copy-start(f32[256,1024]{1,0:T(8,128)} %copy-done.5) | copy-start | bytes 3145732
  676.2 42.3 %copy-start.10 = (bf16[256,1024]{1,0:T(8,128)(2,1)S(1)}, bf16[256,1024]{1,0:T(8,128)(2,1)}, u32[]{:S(2)}) copy-start(bf16[256,1024]{1,0:T(8,128)(2,1)} %param.27) | copy-start | bytes 1572868
  1147.4 11.9 copy-start.11
Sparse Core Ops, SparseCore 0:
  11.3 45.4 all-gather.2
  95.1 85.8 all-reduce.9
  503.1 42.9 all-gather.4
  614.1 59.8 all-reduce.13
  676.2 40.7 reduce-scatter.1
  720.2 427.1 all-reduce.15
  1154.4 123.5 all-reduce.11
where the time goes:
time: 1300 us; the launch traced here: 1290 us
  waiting for transfers between devices  883 us (68%)
  matrix products  138 us (11%)
  local copies, waits for them, and re-layouts  102 us (8%)
  other arithmetic  68.5 us (5%)
  blocking collectives  47.1 us (4%)
  starting transfers between devices  19.6 us (2%)
  between operations  15 us (1%)
  loops' own time  13.9 us (1%)
    psum x1, waiting for transfers between devices, local(): lax.psum(gate_up_grad.astype(jnp.bfloat16), 'tp').astype(jnp.float32)  378 us
    psum x1, waiting for transfers between devices, local(): lax.psum((router_grad, norm1_part, norm2_part), ('exp', 'tp'))  114 us
    psum x1, waiting for transfers between devices, local(): lax.psum(jnp.dot(mixed, w_out, preferred_element_type=jnp.float32).astype...  66.7 us
    all_to_all x1, waiting for transfers between devices, local(): lax.all_to_all(dexpert_in, 'exp', split_axis=0, concat_axis=0, tiled=True)  51.4 us
    all_to_all x1, waiting for transfers between devices, local(): lax.all_to_all(grad_outgoing, 'exp', split_axis=0, concat_axis=0, tiled=T...  48 us
    psum x1, blocking collectives, local(): lax.psum((router_grad, norm1_part, norm2_part), ('exp', 'tp'))  47.1 us
    all_gather x1, waiting for transfers between devices, local(): gathered = lax.all_gather(normed1, 'tp', axis=0, tiled=True)  45.6 us
    all_gather x1, waiting for transfers between devices, local(): dfull = lax.all_gather(dhidden_low, 'tp', axis=0, tiled=True)  42.8 us
  transfers between devices with their start and end apart: 11, of which 11 were waited for; matrix products, arithmetic and copies ran while one was open for 12% of the time, Pallas kernels for 0%

commit v1 on v0

v1 whole, which is shorter than its diff:
```python
import functools

import jax
import jax.numpy as jnp
from jax import lax
from jax.experimental import pallas as pl
from jax.experimental.pallas import tpu as pltpu
from jax.sharding import PartitionSpec as P

D = 1024
H = 16
KVH = 8
HD = 64
FF = 512
LANES = 128
XW = D + LANES
GROUP = 4

EPS = 1e-06
MASKED = -1e30
MESH = pl.DeviceIdType.MESH
BF = jnp.bfloat16
F32 = jnp.float32
VMEM = pltpu.VMEM
MIB = 1 << 20


def mm(a, b):
    return jnp.dot(a, b, preferred_element_type=F32)


def mm_nt(a, b):
    return lax.dot_general(a, b, (((1,), (1,)), ((), ())), preferred_element_type=F32)


def mm_tn(a, b):
    return lax.dot_general(a, b, (((0,), (0,)), ((), ())), preferred_element_type=F32)


def row_scaling(values):
    inverse = lax.rsqrt(jnp.mean(values * values, axis=-1, keepdims=True) + EPS)
    return values * inverse, inverse


def norm_backward(gradient, scaled, inverse, gain):
    weighted = gradient * gain
    inner = jnp.mean(weighted * scaled, axis=-1, keepdims=True)
    return inverse * (weighted - scaled * inner)


def block(ref, index, rows):
    return ref.at[pl.ds(pl.multiple_of(index * rows, rows), rows)]


def line_order(n):
    orders = []
    for z in range(n):
        right = list(range(n - 1, z, -1))
        left = list(range(z))
        first, second = (right, left) if len(right) >= len(left) else (left, right)
        order = []
        while first or second:
            if len(first) >= len(second):
                order.append(first.pop(0))
            else:
                order.append(second.pop(0))
        orders.append(order + [z])
    return orders


def lookup(table, z, j):
    value = jnp.int32(table[0][0])
    for a, row in enumerate(table):
        for b, entry in enumerate(row):
            value = jnp.where((z == a) & (j == b), jnp.int32(entry), value)
    return value


def greet_line(e, z, n):
    barrier = pltpu.get_barrier_semaphore()

    @pl.when(z > 0)
    def _():
        pl.semaphore_signal(barrier, inc=1, device_id=(e, z - 1), device_id_type=MESH)

    @pl.when(z < n - 1)
    def _():
        pl.semaphore_signal(barrier, inc=1, device_id=(e, z + 1), device_id_type=MESH)

    neighbours = jnp.where(z > 0, 1, 0) + jnp.where(z < n - 1, 1, 0)
    pl.semaphore_wait(barrier, neighbours)


def line_gather(e, z, n, rows, held, right_sems, left_sems, work):
    def copy(step, way):
        send, recv = right_sems if way > 0 else left_sems
        there = block(held, z - way * step, rows)
        return pltpu.make_async_remote_copy(
            src_ref=there,
            dst_ref=there,
            send_sem=send.at[step],
            recv_sem=recv.at[step],
            device_id=(e, z + way),
            device_id_type=MESH,
        )

    def arrived(step, way):
        send, recv = right_sems if way > 0 else left_sems
        there = block(held, z - way * step, rows)
        return pltpu.make_async_remote_copy(
            src_ref=there,
            dst_ref=there,
            send_sem=send.at[step],
            recv_sem=recv.at[step - 1],
            device_id=(e, z + way),
            device_id_type=MESH,
        )

    from_here = {1: z < n - 1, -1: z > 0}
    for way in (1, -1):

        @pl.when(from_here[way])
        def _():
            copy(0, way).start()

    work(z)
    for step in range(1, n):
        has = {1: z >= step, -1: z + step < n}
        for way in (1, -1):

            @pl.when(has[way])
            def _():
                arrived(step, way).wait_recv()

            @pl.when(has[way] & from_here[way])
            def _():
                copy(step, way).start()

        def one(way, carry):
            @pl.when(jnp.where(way > 0, has[-1], has[1]))
            def _():
                work(jnp.where(way > 0, z + step, z - step))

            return carry

        lax.fori_loop(0, 2, one, 0)

    def drain():
        for step in range(n - 1):
            has = {1: z >= step, -1: z + step < n}
            for way in (1, -1):

                @pl.when(has[way] & from_here[way])
                def _():
                    copy(step, way).wait_send()

    return drain


def line_scatter(e, z, n, sent, landed, sems, part, between=None):
    send, recv = sems
    table = line_order(n)

    def copy(way, slot):
        return pltpu.make_async_remote_copy(
            src_ref=sent.at[way, slot],
            dst_ref=landed.at[way, slot],
            send_sem=send.at[way, slot],
            recv_sem=recv.at[way, slot],
            device_id=(e, jnp.where(way == 0, z + 1, z - 1)),
            device_id_type=MESH,
        )

    def one(j, carry):
        d = lookup(table, z, j)
        way = jnp.where(d > z, 0, 1)
        slot = jnp.where(d > z, n - 1 - d, d)
        value = part(d)
        upstream = jnp.where(d > z, z > 0, z < n - 1)

        @pl.when(upstream)
        def _():
            copy(way, slot).wait_recv()
            sent[way, slot] = (value + landed[way, slot].astype(F32)).astype(BF)

        @pl.when(jnp.logical_not(upstream))
        def _():
            sent[way, slot] = value.astype(BF)

        copy(way, slot).start()
        return carry

    lax.fori_loop(0, n - 1, one, 0)
    own = part(z)
    if between is not None:
        between()

    def finish(total_ref):
        total_ref[...] = own

        @pl.when(z > 0)
        def _():
            copy(0, n - 1 - z).wait_recv()
            total_ref[...] += landed[0, n - 1 - z].astype(F32)

        @pl.when(z < n - 1)
        def _():
            copy(1, z).wait_recv()
            total_ref[...] += landed[1, z].astype(F32)

        for slot in range(n):

            @pl.when(slot < n - 1 - z)
            def _():
                copy(0, slot).wait_send()

            @pl.when(slot < z)
            def _():
                copy(1, slot).wait_send()

    return finish


def visible_mask(d, rows, length, prefix):
    row_ids = d * rows + lax.broadcasted_iota(jnp.int32, (rows, length), 0)
    col_ids = lax.broadcasted_iota(jnp.int32, (rows, length), 1)
    return (col_ids <= row_ids) | (col_ids < prefix)


def halves(pair, low):
    pair = pair.astype(F32)
    zero = jnp.zeros_like(pair)
    return jnp.where(low, pair, zero), jnp.where(low, pltpu.roll(pair, HD, 1), zero)


def attention_forward_kernel(
    n,
    tokens,
    gain1,
    w_query,
    w_pair,
    w_out,
    gain2,
    w_router,
    routes,
    prefix,
    hidden,
    ext,
    held,
    queries,
    pairs,
    mixed,
    totals,
    sent,
    landed,
    ag_rs,
    ag_rr,
    ag_ls,
    ag_lr,
    rs_s,
    rs_r,
):
    e, z = lax.axis_index("exp"), lax.axis_index("tp")
    rows = tokens.shape[0]
    length = rows * n
    kv_local = pairs.shape[1] // LANES
    low = lax.broadcasted_iota(jnp.int32, (rows, LANES), 1) < HD
    greet_line(e, z, n)
    scaled, _ = row_scaling(tokens[...].astype(F32))
    held[pl.ds(pl.multiple_of(z * rows, rows), rows)] = (scaled * gain1[...]).astype(BF)

    def project(d):
        at = pl.ds(pl.multiple_of(d * rows, rows), rows)
        normed = held[at]
        queries[at] = mm(normed, w_query[...]).astype(BF)
        pairs[at] = mm(normed, w_pair[...]).astype(BF)

    drain = line_gather(e, z, n, rows, held, (ag_rs, ag_rr), (ag_ls, ag_lr), project)

    def part(d):
        at = pl.ds(pl.multiple_of(d * rows, rows), rows)
        seen = visible_mask(d, rows, length, prefix[0])
        lane = lax.broadcasted_iota(jnp.int32, (rows, LANES), 1)
        stats = jnp.zeros((rows, LANES), F32)
        for kv in range(kv_local):
            span = slice(kv * LANES, (kv + 1) * LANES)
            pair = pairs[:, span]
            outs = []
            for h, head in enumerate(halves(queries[at, span], low)):
                scores = mm_nt((head * HD**-0.5).astype(BF), pair)
                scores = jnp.where(seen, scores, MASKED)
                top = jnp.max(scores, axis=-1, keepdims=True)
                grown = jnp.exp(scores - top)
                total = jnp.sum(grown, axis=-1, keepdims=True)
                probs = (grown / total).astype(BF)
                outs.append(mm(probs, pair))
                stats = jnp.where(lane == 2 * kv + h, top + jnp.log(total), stats)
            both = jnp.where(low, pltpu.roll(outs[0], HD, 1), outs[1])
            mixed[at, span] = both.astype(BF)
        totals[at] = stats
        return mm(mixed[at], w_out[...])

    finish = line_scatter(e, z, n, sent, landed, (rs_s, rs_r), part)
    finish(hidden)
    hid = tokens[...].astype(F32) + hidden[...]
    hidden[...] = hid
    scaled2, _ = row_scaling(hid)
    normed2 = (scaled2 * gain2[...]).astype(BF)
    ext[:, :D] = normed2
    experts = w_router.shape[1]
    logits = mm(normed2, w_router[...])
    lane = lax.broadcasted_iota(jnp.int32, (rows, experts), 1)
    chosen = lane == routes[:, 0:1]
    for k in range(1, routes.shape[1]):
        chosen = chosen | (lane == routes[:, k : k + 1])
    logits = jnp.where(chosen, logits, MASKED)
    grown = jnp.exp(logits - jnp.max(logits, axis=-1, keepdims=True))
    grown = jnp.where(chosen, grown, 0.0)
    gates = grown / jnp.sum(grown, axis=-1, keepdims=True)
    high = gates.astype(BF)
    low_part = (gates - high.astype(F32)).astype(BF)
    mask = jnp.where(chosen, 1.0, 0.0).astype(BF)
    pad = jnp.zeros((rows, LANES - 3 * experts), BF)
    ext[:, D:] = jnp.concatenate([high, low_part, mask, pad], axis=1)
    drain()


def attention_forward(n, tokens, gain1, w_query, w_pair, w_out, gain2, w_router, routes, prefix):
    rows = tokens.shape[0]
    length = rows * n
    qw, pw = w_query.shape[1], w_pair.shape[1]
    v = pl.BlockSpec(memory_space=VMEM)
    sem = pltpu.SemaphoreType.DMA
    return pl.pallas_call(
        functools.partial(attention_forward_kernel, n),
        out_shape=(
            jax.ShapeDtypeStruct((rows, D), F32),
            jax.ShapeDtypeStruct((rows, XW), BF),
            jax.ShapeDtypeStruct((length, D), BF),
            jax.ShapeDtypeStruct((length, qw), BF),
            jax.ShapeDtypeStruct((length, pw), BF),
            jax.ShapeDtypeStruct((length, qw), BF),
            jax.ShapeDtypeStruct((length, LANES), F32),
        ),
        in_specs=[v] * 8 + [pl.BlockSpec(memory_space=pltpu.SMEM)],
        out_specs=[v] * 7,
        scratch_shapes=[
            pltpu.VMEM((2, n, rows, D), BF),
            pltpu.VMEM((2, n, rows, D), BF),
            sem((n,)),
            sem((n,)),
            sem((n,)),
            sem((n,)),
            sem((2, n)),
            sem((2, n)),
        ],
        compiler_params=pltpu.CompilerParams(
            collective_id=1, has_side_effects=True, vmem_limit_bytes=48 * MIB
        ),
        cost_estimate=pl.CostEstimate(
            flops=2 * length * D * 4 * qw, bytes_accessed=300 * MIB, transcendentals=0
        ),
    )(tokens, gain1, w_query, w_pair, w_out, gain2, w_router, routes, prefix)


def slot_rows(rows, top_k, experts):
    capacity = rows * top_k * 5 // (experts * 4)
    return -(-capacity // 16) * 16


def selection(extra, first, local_experts, slots):
    rows = extra.shape[0]
    pick = lax.broadcasted_iota(jnp.int32, (8, LANES), 1) == (
        64 + first + lax.broadcasted_iota(jnp.int32, (8, LANES), 0)
    )
    named = mm_nt(jnp.where(pick, 1.0, 0.0).astype(BF), extra)
    earlier = lax.broadcasted_iota(jnp.int32, (rows, rows), 0) < lax.broadcasted_iota(
        jnp.int32, (rows, rows), 1
    )
    place = mm(named.astype(BF), jnp.where(earlier, 1.0, 0.0).astype(BF))
    place = jnp.where(named > 0.5, place, -1.0).astype(jnp.int32)
    slot = lax.broadcasted_iota(jnp.int32, (slots, rows), 0)
    parts = [
        jnp.where(slot == place[k : k + 1, :], 1.0, 0.0) for k in range(local_experts)
    ]
    return jnp.concatenate(parts, axis=0).astype(BF)


def own_gate(extra, expert):
    lane = lax.broadcasted_iota(jnp.int32, extra.shape, 1)
    mine = (lane == expert) | (lane == 32 + expert)
    return jnp.sum(jnp.where(mine, extra.astype(F32), 0.0), axis=-1, keepdims=True)


def sigmoid(v):
    return 1.0 / (1.0 + jnp.exp(-v))


def own_experts_kernel(
    n_exp,
    local_experts,
    ext,
    cot,
    cot_all,
    w_gate_up,
    w_down,
    hidden,
    w_router,
    gain2,
    layer_out,
    dhidden,
    dhidden_low,
    router_part,
    norm2_part,
    xg,
    cg,
    wgu,
    wd,
    sel,
    xs,
    cs,
    core_in,
    chip_out,
    chip_in,
    mix_core_in,
    mix_out,
    mix_in,
    total,
    cot_sem,
    w_sem,
    ag_s,
    ag_r,
    fw_s,
    fw_r,
    core_s,
    core_r,
    chip_s,
    chip_r,
    mcore_s,
    mcore_r,
    mchip_s,
    mchip_r,
):
    e, z = lax.axis_index("exp"), lax.axis_index("tp")
    rows = ext.shape[0]
    chips = n_exp // 2
    chip, core = e // 2, lax.rem(e, 2)
    partner = 2 * chip + 1 - core
    slots = sel.shape[1] // local_experts
    first = e * local_experts
    experts = w_router.shape[1]

    loads = [
        pltpu.make_async_copy(w_gate_up, wgu, w_sem.at[0]),
        pltpu.make_async_copy(w_down, wd, w_sem.at[1]),
    ]
    for b in range(n_exp):
        loads.append(pltpu.make_async_copy(cot_all.at[b, z], cg.at[b], cot_sem.at[b]))
    for load in loads:
        load.start()

    def there(k):
        return 2 * (chip ^ k) + core

    barrier = pltpu.get_barrier_semaphore()
    pl.semaphore_signal(barrier, inc=1, device_id=(partner, z), device_id_type=MESH)
    for k in range(1, chips):
        pl.semaphore_signal(barrier, inc=1, device_id=(there(k), z), device_id_type=MESH)
    xg[e] = ext[...]
    pl.semaphore_wait(barrier, chips)

    def push(k):
        return pltpu.make_async_remote_copy(
            src_ref=xg.at[e],
            dst_ref=xg.at[e],
            send_sem=ag_s.at[k],
            recv_sem=ag_r.at[k],
            device_id=(there(k), z),
            device_id_type=MESH,
        )

    def forward(k):
        return pltpu.make_async_remote_copy(
            src_ref=xg.at[there(k)],
            dst_ref=xg.at[there(k)],
            send_sem=fw_s.at[k],
            recv_sem=fw_r.at[k],
            device_id=(partner, z),
            device_id_type=MESH,
        )

    def pushed(k):
        return pltpu.make_async_remote_copy(
            src_ref=xg.at[there(k)],
            dst_ref=xg.at[there(k)],
            send_sem=ag_s.at[k],
            recv_sem=ag_r.at[k],
            device_id=(there(k), z),
            device_id_type=MESH,
        )

    def forwarded(k):
        b = 2 * (chip ^ k) + 1 - core
        return pltpu.make_async_remote_copy(
            src_ref=xg.at[b],
            dst_ref=xg.at[b],
            send_sem=fw_s.at[k],
            recv_sem=fw_r.at[k],
            device_id=(partner, z),
            device_id_type=MESH,
        )

    for k in range(1, chips):
        push(k).start()
    forward(0).start()
    for load in loads[2:]:
        load.wait()

    def gather(b):
        s = selection(xg[b, :, D:], first, local_experts, slots)
        sel[b] = s
        xs[b] = mm(s, xg[b]).astype(BF)
        cs[b] = mm(s, cg[b]).astype(BF)

    gather(e)
    for k in range(1, chips):
        pushed(k).wait_recv()
        forward(k).start()
    lax.fori_loop(1, chips, lambda k, c: (gather(there(k)), c)[1], 0)
    for k in range(chips):
        forwarded(k).wait_recv()
    lax.fori_loop(0, chips, lambda k, c: (gather(2 * (chip ^ k) + 1 - core), c)[1], 0)
    for load in loads[:2]:
        load.wait()
    for k in range(1, chips):
        push(k).wait_send()
    for k in range(chips):
        forward(k).wait_send()

    groups = n_exp // GROUP

    def expert_step(step, carry):
        k = step // groups
        b0 = lax.rem(step, groups) * GROUP
        at = pl.ds(pl.multiple_of(k * slots, slots), slots)
        wide = jnp.concatenate([xs[b0 + i, at] for i in range(GROUP)], axis=0)
        gate_value = own_gate(wide[:, D:], first + k)
        units = mm(wide[:, :D], wgu[k])
        gate, up = units[:, :FF], units[:, FF:]
        sig = sigmoid(gate)
        silu = gate * sig
        active = (silu * up).astype(BF)
        made = mm(active, wd[k]).astype(BF).astype(F32)
        upstream = jnp.concatenate([cs[b0 + i, at] for i in range(GROUP)], axis=0).astype(F32)
        dgate_value = jnp.sum(upstream * made, axis=-1, keepdims=True)
        share = (gate_value * made).astype(BF)
        dmade = (gate_value * upstream).astype(BF)
        dactive = mm_nt(dmade, wd[k])
        dgate = dactive * up * sig * (1.0 + gate * (1.0 - sig))
        dunits = jnp.concatenate([dgate, dactive * silu], axis=1).astype(BF)
        dx = mm_nt(dunits, wgu[k]).astype(BF)
        lane = lax.broadcasted_iota(jnp.int32, (GROUP * slots, LANES), 1)
        high = dgate_value.astype(BF).astype(F32)
        packed = jnp.where(lane == first + k, high, 0.0)
        packed = jnp.where(lane == 32 + first + k, dgate_value - high, packed).astype(BF)
        for i in range(GROUP):
            here = slice(i * slots, (i + 1) * slots)
            xs[b0 + i, at, :D] = share[here]
            xs[b0 + i, at, D:] = packed[here]
            cs[b0 + i, at] = dx[here]
        return carry

    lax.fori_loop(0, local_experts * groups, expert_step, 0)

    def other(k):
        return 2 * (chip ^ k) + 1 - core

    def core_copy(k, src, dst, s, r):
        return pltpu.make_async_remote_copy(
            src_ref=src.at[other(k)],
            dst_ref=dst.at[k],
            send_sem=s.at[k],
            recv_sem=r.at[k],
            device_id=(partner, z),
            device_id_type=MESH,
        )

    def chip_copy(k, src, dst, s, r):
        return pltpu.make_async_remote_copy(
            src_ref=src.at[k],
            dst_ref=dst.at[k],
            send_sem=s.at[k],
            recv_sem=r.at[k],
            device_id=(there(k), z),
            device_id_type=MESH,
        )

    def grads_of(b):
        s = sel[b]
        return jnp.concatenate([mm_tn(s, cs[b]), mm_tn(s, xs[b, :, D:])], axis=1)

    def each(count, body):
        lax.fori_loop(0, count, lambda i, c: (body(i), c)[1], 0)

    def give_grads(i):
        k = chips - 1 - i
        xg[other(k)] = grads_of(other(k)).astype(BF)
        core_copy(k, xg, core_in, core_s, core_r).start()

    def pass_grads(i):
        k = chips - 1 - i
        mine = grads_of(there(k))
        core_copy(k, xg, core_in, core_s, core_r).wait_recv()
        chip_out[k] = (mine + core_in[k].astype(F32)).astype(BF)
        chip_copy(k, chip_out, chip_in, chip_s, chip_r).start()

    def give_mix(i):
        k = chips - 1 - i
        cg[other(k)] = mm_tn(sel[other(k)], xs[other(k), :, :D]).astype(BF)
        core_copy(k, cg, mix_core_in, mcore_s, mcore_r).start()

    def pass_mix(i):
        k = chips - 1 - i
        mine = mm_tn(sel[there(k)], xs[there(k), :, :D])
        core_copy(k, cg, mix_core_in, mcore_s, mcore_r).wait_recv()
        mix_out[k] = (mine + mix_core_in[k].astype(F32)).astype(BF)
        chip_copy(k, mix_out, mix_in, mchip_s, mchip_r).start()

    each(chips, give_grads)
    each(chips - 1, pass_grads)
    each(chips, give_mix)
    each(chips - 1, pass_mix)
    total[...] = grads_of(e)
    core_copy(0, xg, core_in, core_s, core_r).wait_recv()
    total[...] += core_in[0].astype(F32)

    def take_grads(i):
        k = chips - 1 - i
        chip_copy(k, chip_out, chip_in, chip_s, chip_r).wait_recv()
        total[...] += chip_in[k].astype(F32)

    each(chips - 1, take_grads)
    extra = ext[:, D:].astype(F32)
    gates = extra[:, :experts] + extra[:, experts : 2 * experts]
    dgates = total[:, D : D + experts] + total[:, D + experts : D + 2 * experts]
    dlogits = gates * (dgates - jnp.sum(gates * dgates, axis=-1, keepdims=True))
    dlogits = dlogits.astype(BF)
    normed2 = ext[:, :D]
    router_part[...] = mm_tn(dlogits, normed2)
    dnormed2 = total[:, :D] + mm_nt(dlogits, w_router[...])
    scaled2, inverse2 = row_scaling(hidden[...])
    norm2_part[...] = jnp.broadcast_to(
        jnp.sum(dnormed2 * scaled2, axis=0, keepdims=True), norm2_part.shape
    )
    back = cot[...].astype(F32) + norm_backward(dnormed2, scaled2, inverse2, gain2[...])
    dhidden[...] = back
    dhidden_low[...] = back.astype(BF)

    total[:, :D] = hidden[...] + mm_tn(sel[e], xs[e, :, :D])
    core_copy(0, cg, mix_core_in, mcore_s, mcore_r).wait_recv()
    total[:, :D] += mix_core_in[0].astype(F32)

    def take_mix(i):
        k = chips - 1 - i
        chip_copy(k, mix_out, mix_in, mchip_s, mchip_r).wait_recv()
        total[:, :D] += mix_in[k].astype(F32)

    each(chips - 1, take_mix)
    layer_out[...] = total[:, :D].astype(BF)

    def sent_to_core(k):
        core_copy(k, xg, core_in, core_s, core_r).wait_send()
        core_copy(k, cg, mix_core_in, mcore_s, mcore_r).wait_send()

    def sent_to_chip(i):
        chip_copy(i + 1, chip_out, chip_in, chip_s, chip_r).wait_send()
        chip_copy(i + 1, mix_out, mix_in, mchip_s, mchip_r).wait_send()

    each(chips, sent_to_core)
    each(chips - 1, sent_to_chip)


def own_experts(n_exp, ext, cot, cot_all, w_gate_up, w_down, hidden, w_router, gain2, slots):
    rows = ext.shape[0]
    local_experts = w_gate_up.shape[0]
    experts = w_router.shape[1]
    chips = n_exp // 2
    v = pl.BlockSpec(memory_space=VMEM)
    hbm = pl.BlockSpec(memory_space=pl.ANY)
    sem = pltpu.SemaphoreType.DMA
    taken = n_exp * local_experts * slots
    return pl.pallas_call(
        functools.partial(own_experts_kernel, n_exp, local_experts),
        out_shape=(
            jax.ShapeDtypeStruct((rows, D), BF),
            jax.ShapeDtypeStruct((rows, D), F32),
            jax.ShapeDtypeStruct((rows, D), BF),
            jax.ShapeDtypeStruct((experts, D), F32),
            jax.ShapeDtypeStruct((8, D), F32),
        ),
        in_specs=[v, v, hbm, hbm, hbm, v, v, v],
        out_specs=[v] * 5,
        scratch_shapes=[
            pltpu.VMEM((n_exp, rows, XW), BF),
            pltpu.VMEM((n_exp, rows, D), BF),
            pltpu.VMEM(w_gate_up.shape, BF),
            pltpu.VMEM(w_down.shape, BF),
            pltpu.VMEM((n_exp, local_experts * slots, rows), BF),
            pltpu.VMEM((n_exp, local_experts * slots, XW), BF),
            pltpu.VMEM((n_exp, local_experts * slots, D), BF),
            pltpu.VMEM((chips, rows, XW), BF),
            pltpu.VMEM((chips, rows, XW), BF),
            pltpu.VMEM((chips, rows, XW), BF),
            pltpu.VMEM((chips, rows, D), BF),
            pltpu.VMEM((chips, rows, D), BF),
            pltpu.VMEM((chips, rows, D), BF),
            pltpu.VMEM((rows, XW), F32),
            sem((n_exp,)),
            sem((2,)),
        ]
        + [sem((chips,))] * 12,
        compiler_params=pltpu.CompilerParams(
            collective_id=2, has_side_effects=True, vmem_limit_bytes=62 * MIB
        ),
        cost_estimate=pl.CostEstimate(
            flops=2 * taken * 6 * D * FF, bytes_accessed=300 * MIB, transcendentals=0
        ),
    )(ext, cot, cot_all, w_gate_up, w_down, hidden, w_router, gain2)


def expert_grads_kernel(
    blocks,
    groups,
    local_experts,
    ext_all,
    cot_all,
    w_gate_up,
    w_down,
    gate_up_grad,
    down_grad,
    xbuf,
    cbuf,
    kept_x,
    kept_dy,
    kept_active,
    kept_dunits,
    sems,
):
    first = lax.axis_index("exp") * local_experts
    k, g = pl.program_id(0), pl.program_id(1)
    slots = kept_x.shape[0] // blocks
    chunks = blocks // GROUP
    size = GROUP * slots

    def load(c, slot):
        at = pl.ds(g * blocks + c * GROUP, GROUP)
        return (
            pltpu.make_async_copy(ext_all.at[at], xbuf.at[slot], sems.at[0, slot]),
            pltpu.make_async_copy(cot_all.at[at], cbuf.at[slot], sems.at[1, slot]),
        )

    for copy in load(0, 0):
        copy.start()

    def chunk(c, carry):
        slot = lax.rem(c, 2)

        @pl.when(c + 1 < chunks)
        def _():
            for copy in load(c + 1, 1 - slot):
                copy.start()

        for copy in load(c, slot):
            copy.wait()
        wide, upstream = [], []
        for i in range(GROUP):
            s = selection(xbuf[slot, i, :, D:], first + k, 1, slots)
            wide.append(mm(s, xbuf[slot, i]))
            upstream.append(mm(s, cbuf[slot, i]))
        wide = jnp.concatenate(wide, axis=0)
        upstream = jnp.concatenate(upstream, axis=0)
        gate_value = own_gate(wide[:, D:], first + k)
        x = wide[:, :D].astype(BF)
        units = mm(x, w_gate_up[0])
        gate, up = units[:, :FF], units[:, FF:]
        sig = sigmoid(gate)
        silu = gate * sig
        dmade = (gate_value * upstream).astype(BF)
        dactive = mm_nt(dmade, w_down[0])
        dgate = dactive * up * sig * (1.0 + gate * (1.0 - sig))
        at = pl.ds(pl.multiple_of(c * size, size), size)
        kept_x[at] = x
        kept_dy[at] = dmade
        kept_active[at] = (silu * up).astype(BF)
        kept_dunits[at, :FF] = dgate.astype(BF)
        kept_dunits[at, FF:] = (dactive * silu).astype(BF)
        return carry

    lax.fori_loop(0, chunks, chunk, 0)

    def add(out, at, value):
        if groups == 1:
            out[0, at] = value
        else:

            @pl.when(g == 0)
            def _():
                out[0, at] = value

            @pl.when(g > 0)
            def _():
                out[0, at] += value

    tile = 256

    def up_tile(m, carry):
        at = pl.ds(pl.multiple_of(m * tile, tile), tile)
        add(gate_up_grad, at, mm_tn(kept_x[:, at], kept_dunits[...]))
        return carry

    lax.fori_loop(0, D // tile, up_tile, 0)

    def down_tile(m, carry):
        at = pl.ds(pl.multiple_of(m * tile, tile), tile)
        add(down_grad, at, mm_tn(kept_active[:, at], kept_dy[...]))
        return carry

    lax.fori_loop(0, FF // tile, down_tile, 0)


def expert_grads(ext_all, cot_all, w_gate_up, w_down, slots):
    total, rows = ext_all.shape[:2]
    local_experts = w_gate_up.shape[0]
    blocks = min(total, 32)
    groups = total // blocks
    kept = blocks * slots
    hbm = pl.BlockSpec(memory_space=pl.ANY)
    return pl.pallas_call(
        functools.partial(expert_grads_kernel, blocks, groups, local_experts),
        grid=(local_experts, groups),
        out_shape=(
            jax.ShapeDtypeStruct((local_experts, D, 2 * FF), F32),
            jax.ShapeDtypeStruct((local_experts, FF, D), F32),
        ),
        in_specs=[
            hbm,
            hbm,
            pl.BlockSpec((1, D, 2 * FF), lambda k, g: (k, 0, 0)),
            pl.BlockSpec((1, FF, D), lambda k, g: (k, 0, 0)),
        ],
        out_specs=[
            pl.BlockSpec((1, D, 2 * FF), lambda k, g: (k, 0, 0)),
            pl.BlockSpec((1, FF, D), lambda k, g: (k, 0, 0)),
        ],
        scratch_shapes=[
            pltpu.VMEM((2, GROUP, rows, XW), BF),
            pltpu.VMEM((2, GROUP, rows, D), BF),
            pltpu.VMEM((kept, D), BF),
            pltpu.VMEM((kept, D), BF),
            pltpu.VMEM((kept, FF), BF),
            pltpu.VMEM((kept, 2 * FF), BF),
            pltpu.SemaphoreType.DMA((2, 2)),
        ],
        compiler_params=pltpu.CompilerParams(vmem_limit_bytes=60 * MIB),
        cost_estimate=pl.CostEstimate(
            flops=2 * total * slots * local_experts * 6 * D * FF,
            bytes_accessed=200 * MIB,
            transcendentals=0,
        ),
    )(ext_all, cot_all, w_gate_up, w_down)


def attention_backward_kernel(
    n,
    dhidden_low,
    dhidden,
    tokens,
    gain1,
    held,
    queries,
    pairs,
    mixed,
    totals,
    w_query,
    w_pair,
    w_out,
    prefix,
    input_grad,
    query_grad,
    pair_grad,
    out_grad,
    norm1_part,
    dfull,
    dqueries,
    dpairs,
    dpairs_low,
    sent,
    landed,
    ag_rs,
    ag_rr,
    ag_ls,
    ag_lr,
    rs_s,
    rs_r,
):
    e, z = lax.axis_index("exp"), lax.axis_index("tp")
    rows = tokens.shape[0]
    length = rows * n
    kv_local = pairs.shape[1] // LANES
    low = lax.broadcasted_iota(jnp.int32, (rows, LANES), 1) < HD
    scale = HD**-0.5
    greet_line(e, z, n)
    dfull[pl.ds(pl.multiple_of(z * rows, rows), rows)] = dhidden_low[...]
    dpairs[...] = jnp.zeros_like(dpairs)

    def work(d):
        at = pl.ds(pl.multiple_of(d * rows, rows), rows)
        seen = visible_mask(d, rows, length, prefix[0])
        dmixed = mm_nt(dfull[at], w_out[...]).astype(BF)
        stats = totals[at]
        for kv in range(kv_local):
            span = slice(kv * LANES, (kv + 1) * LANES)
            pair = pairs[:, span]
            outs = []
            added = jnp.zeros((length, LANES), F32)
            heads = halves(queries[at, span], low)
            grads = halves(dmixed[:, span], low)
            for h in range(2):
                head = (heads[h] * scale).astype(BF)
                grad = pltpu.roll(grads[h], HD, 1).astype(BF)
                column = 2 * kv + h
                scores = mm_nt(head, pair)
                probs = jnp.where(seen, jnp.exp(scores - stats[:, column : column + 1]), 0.0)
                dprobs = mm_nt(grad, pair)
                inner = jnp.sum(probs * dprobs, axis=-1, keepdims=True)
                dscores = (probs * (dprobs - inner)).astype(BF)
                outs.append(mm(dscores, pair) * scale)
                added += mm_tn(dscores, head) + mm_tn(probs.astype(BF), grad)
            both = jnp.where(low, outs[0], pltpu.roll(outs[1], HD, 1))
            dqueries[at, span] = both.astype(BF)
            dpairs[:, span] += added

    drain = line_gather(e, z, n, rows, dfull, (ag_rs, ag_rr), (ag_ls, ag_lr), work)
    dpairs_low[...] = dpairs[...].astype(BF)

    def part(d):
        at = pl.ds(pl.multiple_of(d * rows, rows), rows)
        return mm_nt(dqueries[at], w_query[...]) + mm_nt(dpairs_low[at], w_pair[...])

    def weights():
        query_grad[...] = mm_tn(held[...], dqueries[...]).astype(BF)
        pair_grad[...] = mm_tn(held[...], dpairs_low[...]).astype(BF)
        out_grad[...] = mm_tn(mixed[...], dfull[...]).astype(BF)

    finish = line_scatter(e, z, n, sent, landed, (rs_s, rs_r), part, weights)
    finish(input_grad)
    dnormed1 = input_grad[...]
    scaled, inverse = row_scaling(tokens[...].astype(F32))
    norm1_part[...] = jnp.broadcast_to(
        jnp.sum(dnormed1 * scaled, axis=0, keepdims=True), norm1_part.shape
    )
    input_grad[...] = dhidden[...] + norm_backward(dnormed1, scaled, inverse, gain1[...])
    drain()


def attention_backward(
    n,
    dhidden_low,
    dhidden,
    tokens,
    gain1,
    held,
    queries,
    pairs,
    mixed,
    totals,
    w_query,
    w_pair,
    w_out,
    prefix,
):
    rows = tokens.shape[0]
    length = rows * n
    qw, pw = w_query.shape[1], w_pair.shape[1]
    v = pl.BlockSpec(memory_space=VMEM)
    sem = pltpu.SemaphoreType.DMA
    return pl.pallas_call(
        functools.partial(attention_backward_kernel, n),
        out_shape=(
            jax.ShapeDtypeStruct((rows, D), F32),
            jax.ShapeDtypeStruct((D, qw), BF),
            jax.ShapeDtypeStruct((D, pw), BF),
            jax.ShapeDtypeStruct((qw, D), BF),
            jax.ShapeDtypeStruct((8, D), F32),
        ),
        in_specs=[v] * 12 + [pl.BlockSpec(memory_space=pltpu.SMEM)],
        out_specs=[v] * 5,
        scratch_shapes=[
            pltpu.VMEM((length, D), BF),
            pltpu.VMEM((length, qw), BF),
            pltpu.VMEM((length, pw), F32),
            pltpu.VMEM((length, pw), BF),
            pltpu.VMEM((2, n, rows, D), BF),
            pltpu.VMEM((2, n, rows, D), BF),
            sem((n,)),
            sem((n,)),
            sem((n,)),
            sem((n,)),
            sem((2, n)),
            sem((2, n)),
        ],
        compiler_params=pltpu.CompilerParams(
            collective_id=3, has_side_effects=True, vmem_limit_bytes=56 * MIB
        ),
        cost_estimate=pl.CostEstimate(
            flops=2 * length * D * 8 * qw, bytes_accessed=300 * MIB, transcendentals=0
        ),
    )(
        dhidden_low,
        dhidden,
        tokens,
        gain1,
        held,
        queries,
        pairs,
        mixed,
        totals,
        w_query,
        w_pair,
        w_out,
        prefix,
    )


def local(
    n_exp,
    n_tp,
    tokens,
    norm1_gain,
    w_query,
    w_key_value,
    w_out,
    norm2_gain,
    w_router,
    w_gate_up,
    w_down,
    routes,
    prefix,
    cotangent,
):
    rows = tokens.shape[0]
    experts = w_router.shape[1]
    slots = slot_rows(rows, routes.shape[1], experts)
    w_pair = w_key_value.reshape(D, -1)
    gain1, gain2 = norm1_gain.reshape(1, D), norm2_gain.reshape(1, D)
    cot_all = lax.all_gather(cotangent, ("exp", "tp"), axis=0, tiled=True)
    cot_all = cot_all.reshape(n_exp * n_tp, rows, D)
    hidden, ext, held, queries, pairs, mixed, totals = attention_forward(
        n_tp, tokens, gain1, w_query, w_pair, w_out, gain2, w_router, routes, prefix
    )
    ext_all = lax.all_gather(ext, ("exp", "tp"), axis=0, tiled=True)
    ext_all = ext_all.reshape(n_exp * n_tp, rows, XW)
    layer_out, dhidden, dhidden_low, router_part, norm2_part = own_experts(
        n_exp,
        ext,
        cotangent,
        cot_all.reshape(n_exp, n_tp, rows, D),
        w_gate_up,
        w_down,
        hidden,
        w_router,
        gain2,
        slots,
    )
    input_grad, query_grad, pair_grad, out_grad, norm1_part = attention_backward(
        n_tp,
        dhidden_low,
        dhidden,
        tokens,
        gain1,
        held,
        queries,
        pairs,
        mixed,
        totals,
        w_query,
        w_pair,
        w_out,
        prefix,
    )
    gate_up_grad, down_grad = expert_grads(ext_all, cot_all, w_gate_up, w_down, slots)
    query_grad, pair_grad, out_grad = (
        lax.psum(query_grad, "exp").astype(F32),
        lax.psum(pair_grad, "exp").astype(F32),
        lax.psum(out_grad, "exp").astype(F32),
    )
    small = jnp.concatenate([router_part, norm1_part[:1], norm2_part[:1]], axis=0)
    small = lax.psum(small, ("exp", "tp"))
    return (
        layer_out,
        input_grad,
        small[experts],
        query_grad,
        pair_grad.reshape(w_key_value.shape),
        out_grad,
        small[experts + 1],
        small[:experts].T,
        gate_up_grad,
        down_grad,
    )


def solution(mesh):
    return jax.shard_map(
        functools.partial(local, mesh.shape["exp"], mesh.shape["tp"]),
        mesh=mesh,
        in_specs=(
            P(("exp", "tp"), None),
            P(),
            P(None, "tp"),
            P(None, "tp", None),
            P("tp", None),
            P(),
            P(),
            P("exp", None, None),
            P("exp", None, None),
            P(("exp", "tp"), None),
            P("exp"),
            P(("exp", "tp"), None),
        ),
        out_specs=(
            P(("exp", "tp"), None),
            P(("exp", "tp"), None),
            P(),
            P(None, "tp"),
            P(None, "tp", None),
            P("tp", None),
            P(),
            P(),
            P("exp", None, None),
            P("exp", None, None),
        ),
        check_vma=False,
    )
```

time: 1300 us -> 851 us (0.65)
  waiting for transfers between devices: 883 us -> 306 us
  Pallas kernels: 0 us -> 494 us
  matrix products: 138 us -> 0 us
  local copies, waits for them, and re-layouts: 102 us -> 19 us
  other arithmetic: 68.5 us -> 7.27 us
  blocking collectives: 47.1 us -> 0 us
  starting transfers between devices: 19.6 us -> 0.16 us
  loops' own time: 13.9 us -> 0 us
    pallas_call x0 -> x4, Pallas kernels: none -> 494 us  [the longest x1 152 us: expert_grads(): pl.pallas_call(functools.partial(expert_grads_kernel, blocks, groups, loc...]
    psum x4 -> x2, waiting for transfers between devices: 594 us -> 181 us  [the longest x1 121 us: local(): small = lax.psum(small, ('exp', 'tp'))]
    all_to_all x4 -> x0, waiting for transfers between devices: 163 us -> none  [the longest x1 51.4 us: local(): lax.all_to_all(dexpert_in, 'exp', split_axis=0, concat_axis=0, tiled=True)]
    dot_general x74 -> x0, matrix products: 138 us -> none  [the longest x16 29.6 us: head_scores(): lax.dot_general(query_head, key_head, (((1,), (1,)), ((), ())), preferred...]
    gather x9 -> x0, local copies, waits for them, and re-layouts: 69 us -> none  [the longest x5 17.2 us: local(): chosen = jnp.take_along_axis(logits, routes, axis=1)]
    psum x1 -> x0, blocking collectives: 47.1 us -> none  [local(): lax.psum((router_grad, norm1_part, norm2_part), ('exp', 'tp'))]
    reduce_scatter x1 -> x0, waiting for transfers between devices: 37 us -> none  [local(): lax.psum_scatter((from_query + from_pair).astype(jnp.bfloat16), 'tp', sca...]
    all_gather x2, waiting for transfers between devices: 88.4 us -> 124 us  [the longest x1 119 us: local(): ext_all = lax.all_gather(ext, ('exp', 'tp'), axis=0, tiled=True)]
  transfers between devices with their start and end apart: 11 -> 4, of which waited for: 11 -> 4; matrix products, arithmetic and copies ran while one was open for 12% -> 2% of each run, Pallas kernels for 0% -> 17%
where the time goes in v1:
time: 851 us; the launch traced here: 842 us
  Pallas kernels  494 us (58%)
  waiting for transfers between devices  306 us (36%)
  local copies, waits for them, and re-layouts  19 us (2%)
  between operations  15 us (2%)
    pallas_call x1, Pallas kernels, expert_grads(): pl.pallas_call(functools.partial(expert_grads_kernel, blocks, groups, loc...  152 us
    pallas_call x1, Pallas kernels, attention_forward(): pl.pallas_call(functools.partial(attention_forward_kernel, n), out_shape=...  146 us
    psum x1, waiting for transfers between devices, local(): small = lax.psum(small, ('exp', 'tp'))  121 us
    all_gather x1, waiting for transfers between devices, local(): ext_all = lax.all_gather(ext, ('exp', 'tp'), axis=0, tiled=True)  119 us
    pallas_call x1, Pallas kernels, own_experts(): pl.pallas_call(functools.partial(own_experts_kernel, n_exp, local_experts...  112 us
    pallas_call x1, Pallas kernels, attention_backward(): pl.pallas_call(functools.partial(attention_backward_kernel, n), out_shape...  83.3 us
    psum x1, waiting for transfers between devices, local(): lax.psum(query_grad, 'exp').astype(F32)  59.8 us
  transfers between devices with their start and end apart: 4, of which 4 were waited for; matrix products, arithmetic and copies ran while one was open for 2% of the time, Pallas kernels for 17%

profile of v1, /device:TPU:8, one launch (start us, length us, event | category | flops | bytes accessed | tf_op | source)
XLA Modules:
  0.0 841.6 jit_solution(3235549024959536786)
XLA Ops:
  7.2 0.0 all-gather.3.cloned.1.call-start
  7.2 0.7 all-gather.3.cloned.1.call-update
  7.9 0.0 all-reduce.4.cloned.1.call-start
  8.0 1.1 copy.27
  9.1 0.0 copy-start
  9.1 1.1 copy.22.w_router
  10.2 0.0 copy-start.1
  10.8 0.8 copy.23.routes
  11.7 0.0 copy-start.2
  11.7 1.0 copy-done.2
  12.7 1.0 copy-done.3
  13.8 1.0 copy-done.4
  14.8 0.7 copy-done.5
  15.5 0.7 copy-done.6
  16.2 146.4 %shard_map.195 = (f32[256,1024]{1,0:T(8,128)}, bf16[256,1152]{1,0:T(8,128)(2,1)}, bf16[1024,1024]{1,0:T(8,128)(2,1)}, bf16[1024,256]{1,0:T(8,128)(2,1)S(1)}, bf1...) custom-call(bf16[256,1024]{1,0:T(8,128)(2,1)S(1)} %copy-done.2, ...), custom_call_target="tpu_custom_call" | custom-call | flops 2147483648 | bytes 314572800 | tf_op jit(solution)/shard_map/pallas_call | solution.py:334
  162.6 0.0 copy-start.7
  162.6 0.8 copy-done.7
  163.4 0.8 copy-done.8
  164.2 0.8 copy-done.9
  165.0 0.8 copy-done.10
  165.8 5.0 all-gather.3.cloned.1.call-done
  170.8 0.0 copy-done.1
  170.9 112.0 %shard_map.196 = (bf16[256,1024]{1,0:T(8,128)(2,1)}, f32[256,1024]{1,0:T(8,128)}, bf16[256,1024]{1,0:T(8,128)(2,1)}, f32[32,1024]{1,0:T(8,128)}, f32[8,1024]{1,0:T(8,128)}) custom-call(bf16[256,1152]{1,0:T(8,128)(2,1)} %get-tuple-element.29.ext, bf16[256,1024]{1,0:T(8,128)(2,1)} %cot.1, bf16[8,4,256,1024]{3,2,1,0:T(8,128)(2,1)} %bitcast.23, ...), custom_call_target="tpu_custom_call" | custom-call | flops 16106127360 | bytes 314572800 | tf_op jit(solution)/shard_map/pallas_call | solution.py:692
  282.9 0.0 copy-done
  282.9 0.0 copy-start.13
  282.9 83.3 %shard_map.197 = (f32[256,1024]{1,0:T(8,128)}, bf16[1024,256]{1,0:T(8,128)(2,1)}, bf16[1024,256]{1,0:T(8,128)(2,1)}, bf16[256,1024]{1,0:T(8,128)(2,1)}, f32[8,1024]{1,0:T(8,128)}) custom-call(bf16[256,1024]{1,0:T(8,128)(2,1)} %get-tuple-element.32.dhidden_low, f32[256,1024]{1,0:T(8,128)} %get-tuple-element.33.dhidden, bf16[256,1024]{1,0:T(8,128)(2,1)} %tokens.3, ...), custom_call_target="tpu_custom_call" | custom-call | flops 4294967296 | bytes 314572800 | tf_op jit(solution)/shard_map/pallas_call | solution.py:987
  366.1 0.8 slice.15
  366.9 0.8 slice.16
  367.7 0.0 copy-done.13
  367.7 0.7 pad_maximum_fusion
  368.3 0.0 all-reduce.4.cloned.1.call-update
  368.4 0.0 all-reduce.6.cloned.1.call-start
  368.4 2.0 reshape.44
  370.4 0.0 all-reduce.6.cloned.1.call-update
  370.4 0.0 all-gather.5.cloned.1.call-start
  370.5 0.5 all-gather.5.cloned.1.call-update
  371.0 121.4 %all-reduce.4.cloned.1.call-done = f32[34,1024]{1,0:T(8,128)} async-done(((f32[34,1024]{1,0:T(8,128)}), f32[34,1024]{1,0:T(8,128)}) %all-reduce.4.cloned.1.call-update) | async-done | bytes 139280 | tf_op jit(solution)/shard_map/psum | solution.py:1098
  492.4 1.4 fusion
  493.8 1.6 slice_bitcast_fusion
  495.4 59.8 %all-reduce.6.cloned.1.call-done = (bf16[1024,256]{1,0:T(8,128)(2,1)}, bf16[1024,2,128]{2,1,0:T(2,128)(2,1)}, bf16[256,1024]{1,0:T(8,128)(2,1)}) async-done(((bf16[1024,256]{1,0:T(8,128)(2,1)}, bf16[1024,2,128]{2,1,0:T(2,128)(2,1)}, bf16[256,1024]{1,0:T(8,128)(2,1)}), (bf16[1024,256]{1,0:T(8,128)(2,1)}, bf16[1024,2,128]{2,1,0:T(2,128)(2,1)}, bf16[256,1024]{1,0:T(8,128)(2,1)})) %all-reduce.6.cloned.1.call-update) | async-done | bytes 1572880 | tf_op jit(solution)/shard_map/psum | solution.py:1093
  555.1 2.1 convert_element_type.7
  557.2 2.1 convert_element_type.8
  559.3 2.4 reshape.45
  561.7 119.0 %all-gather.5.cloned.1.call-done = bf16[8192,1152]{1,0:T(8,128)(2,1)} async-done(((bf16[256,1152]{1,0:T(8,128)(2,1)}), bf16[8192,1152]{1,0:T(8,128)(2,1)}) %all-gather.5.cloned.1.call-update) | async-done | bytes 18874384 | tf_op jit(solution)/shard_map/all_gather | solution.py:1061
  680.7 152.1 %shard_map.198 = (f32[4,1024,1024]{2,1,0:T(8,128)}, f32[4,512,1024]{2,1,0:T(8,128)}) custom-call(bf16[32,256,1152]{2,1,0:T(8,128)(2,1)} %bitcast.22, bf16[32,256,1024]{2,1,0:T(8,128)(2,1)} %bitcast.24, bf16[4,1024,1024]{2,1,0:T(8,128)(2,1)} %w_gate_up.3, bf16[4,512,1024]{2,1,0:T(8,128)(2,1)} %w_down.3), custom_call_target="tpu_custom_call" | custom-call | flops 64424509440 | bytes 209715200 | tf_op jit(solution)/shard_map/pallas_call | solution.py:838
  832.8 0.0 copy-done.12
  832.8 0.8 copy.35
  833.6 1.0 copy.36
  (10 shorter events, 0.0 us)
Async XLA Ops:
  7.2 163.7 %all-gather.3.cloned.1.call-start = ((), (), s32[]{:S(2)}) async-start(), calls=%async_computation | async-start | bytes 17301504 | tf_op jit(solution)/shard_map/all_gather | solution.py:1056
  7.9 484.5 %all-reduce.4.cloned.1.call-start = ((), (), s32[]{:S(2)}) async-start(), calls=%async_computation.1 | async-start | bytes 327680 | tf_op jit(solution)/shard_map/psum | solution.py:1098
  9.1 273.8 %copy-start = (bf16[128,8,2,128]{3,1,2,0:T(8,128)(2,1)}, bf16[128,8,2,128]{3,1,2,0:T(8,128)(2,1)S(1)}, u32[]{:S(2)}) copy-start(bf16[128,8,2,128]{3,1,2,0:T(8,128)(2,1)S(1)} %copy.27) | copy-start | bytes 1572868
  10.2 160.7 %copy-start.1 = (bf16[1024,32]{1,0:T(8,128)(2,1)}, bf16[1024,32]{1,0:T(8,128)(2,1)S(1)}, u32[]{:S(2)}) copy-start(bf16[1024,32]{1,0:T(8,128)(2,1)S(1)} %copy.22.w_router) | copy-start | bytes 196612
  11.7 1.0 copy-start.2
  12.7 1.0 copy-start.3
  13.8 1.0 copy-start.4
  14.8 0.7 copy-start.5
  15.5 0.7 copy-start.6
  162.6 0.8 copy-start.7
  163.4 0.8 copy-start.8
  164.2 0.8 copy-start.9
  165.0 0.8 copy-start.10
  282.9 84.8 %copy-start.13 = (f32[32,1024]{1,0:T(8,128)S(1)}, f32[32,1024]{1,0:T(8,128)}, u32[]{:S(2)}) copy-start(f32[32,1024]{1,0:T(8,128)} %get-tuple-element.40) | copy-start | bytes 393220
  368.4 186.8 %all-reduce.6.cloned.1.call-start = ((), (), s32[]{:S(2)}) async-start(), calls=%async_computation.3 | async-start | bytes 3145728 | tf_op jit(solution)/shard_map/psum | solution.py:1093
  370.4 310.3 %all-gather.5.cloned.1.call-start = ((), (), s32[]{:S(2)}) async-start(), calls=%async_computation.2 | async-start | bytes 19464192 | tf_op jit(solution)/shard_map/all_gather | solution.py:1061
  680.7 152.1 %copy-start.12 = (bf16[256,1024]{1,0:T(8,128)(2,1)S(1)}, bf16[256,1024]{1,0:T(8,128)(2,1)}, u32[]{:S(2)}) copy-start(bf16[256,1024]{1,0:T(8,128)(2,1)} %get-tuple-element.63) | copy-start | bytes 1572868
  680.7 152.9 %copy-start.11 = (f32[256,1024]{1,0:T(8,128)S(1)}, f32[256,1024]{1,0:T(8,128)}, u32[]{:S(2)}) copy-start(f32[256,1024]{1,0:T(8,128)} %get-tuple-element.64) | copy-start | bytes 3145732
Sparse Core Ops, SparseCore 0:
  11.0 159.7 all-gather.2
  368.5 123.8 all-reduce.3
  496.5 58.5 all-reduce.5
  558.2 122.5 all-gather.4

commit v2 on v1

v2 whole, which is shorter than its diff:
```python
import functools

import jax
import jax.numpy as jnp
from jax import lax
from jax.experimental import pallas as pl
from jax.experimental.pallas import tpu as pltpu
from jax.sharding import PartitionSpec as P

D = 1024
H = 16
KVH = 8
HD = 64
FF = 512
LANES = 128
XW = D + LANES
RW = XW + D
GROUP = 4

EPS = 1e-06
MASKED = -1e30
MESH = pl.DeviceIdType.MESH
BF = jnp.bfloat16
F32 = jnp.float32
VMEM = pltpu.VMEM
MIB = 1 << 20


def mm(a, b):
    return jnp.dot(a, b, preferred_element_type=F32)


def mm_nt(a, b):
    return lax.dot_general(a, b, (((1,), (1,)), ((), ())), preferred_element_type=F32)


def mm_tn(a, b):
    return lax.dot_general(a, b, (((0,), (0,)), ((), ())), preferred_element_type=F32)


def row_scaling(values):
    inverse = lax.rsqrt(jnp.mean(values * values, axis=-1, keepdims=True) + EPS)
    return values * inverse, inverse


def norm_backward(gradient, scaled, inverse, gain):
    weighted = gradient * gain
    inner = jnp.mean(weighted * scaled, axis=-1, keepdims=True)
    return inverse * (weighted - scaled * inner)


def block(ref, index, rows):
    return ref.at[pl.ds(pl.multiple_of(index * rows, rows), rows)]


def line_order(n):
    orders = []
    for z in range(n):
        right = list(range(n - 1, z, -1))
        left = list(range(z))
        first, second = (right, left) if len(right) >= len(left) else (left, right)
        order = []
        while first or second:
            if len(first) >= len(second):
                order.append(first.pop(0))
            else:
                order.append(second.pop(0))
        orders.append(order + [z])
    return orders


def lookup(table, z, j):
    value = jnp.int32(table[0][0])
    for a, row in enumerate(table):
        for b, entry in enumerate(row):
            value = jnp.where((z == a) & (j == b), jnp.int32(entry), value)
    return value


def greet(e, z, n, n_exp, line, plane):
    barrier = pltpu.get_barrier_semaphore()
    peers = jnp.int32(0)
    if line:

        @pl.when(z > 0)
        def _():
            pl.semaphore_signal(barrier, inc=1, device_id=(e, z - 1), device_id_type=MESH)

        @pl.when(z < n - 1)
        def _():
            pl.semaphore_signal(barrier, inc=1, device_id=(e, z + 1), device_id_type=MESH)

        peers += jnp.where(z > 0, 1, 0) + jnp.where(z < n - 1, 1, 0)
    if plane:
        chip, core = e // 2, lax.rem(e, 2)
        pl.semaphore_signal(barrier, inc=1, device_id=(e + 1 - 2 * core, z), device_id_type=MESH)

        def one(k, carry):
            there = 2 * (chip ^ k) + core
            pl.semaphore_signal(barrier, inc=1, device_id=(there, z), device_id_type=MESH)
            return carry

        lax.fori_loop(1, n_exp // 2, one, 0)
        peers += n_exp // 2
    return barrier, peers


def each(count, body, start=0):
    lax.fori_loop(start, count, lambda i, c: (body(i), c)[1], 0)


class PlaneGather:
    def __init__(self, e, z, n_exp, own, view, sems):
        self.e, self.z, self.own, self.view = e, z, own, view
        self.chip, self.core, self.chips = e // 2, lax.rem(e, 2), n_exp // 2
        self.push_s, self.push_r, self.pass_s, self.pass_r = sems

    def mine(self, k):
        return 2 * (self.chip ^ k) + self.core

    def other(self, k):
        return 2 * (self.chip ^ k) + 1 - self.core

    def push(self, k):
        return pltpu.make_async_remote_copy(
            src_ref=self.own,
            dst_ref=self.view(self.e),
            send_sem=self.push_s(k),
            recv_sem=self.push_r(k),
            device_id=(self.mine(k), self.z),
            device_id_type=MESH,
        )

    def pushed(self, k):
        there = self.view(self.mine(k))
        return pltpu.make_async_remote_copy(
            src_ref=there,
            dst_ref=there,
            send_sem=self.push_s(k),
            recv_sem=self.push_r(k),
            device_id=(self.mine(k), self.z),
            device_id_type=MESH,
        )

    def hand(self, k, first=False):
        there = self.view(self.mine(k))
        return pltpu.make_async_remote_copy(
            src_ref=self.own if first else there,
            dst_ref=there,
            send_sem=self.pass_s(k),
            recv_sem=self.pass_r(k),
            device_id=(self.other(0), self.z),
            device_id_type=MESH,
        )

    def handed(self, k):
        there = self.view(self.other(k))
        return pltpu.make_async_remote_copy(
            src_ref=there,
            dst_ref=there,
            send_sem=self.pass_s(k),
            recv_sem=self.pass_r(k),
            device_id=(self.other(0), self.z),
            device_id_type=MESH,
        )

    def begin(self):
        each(self.chips, lambda k: self.push(k).start(), 1)
        self.hand(0, True).start()

    def relay(self):
        def one(k):
            self.pushed(k).wait_recv()
            self.hand(k).start()

        each(self.chips, one, 1)

    def arrive(self):
        each(self.chips, lambda k: self.handed(k).wait_recv())

    def drain(self):
        self.hand(0, True).wait_send()

        def one(k):
            self.push(k).wait_send()
            self.hand(k).wait_send()

        each(self.chips, one, 1)


class LineGather:
    def __init__(self, e, z, n, rows, held, right_sems, left_sems):
        self.e, self.z, self.n, self.rows, self.held = e, z, n, rows, held
        self.sems = {1: right_sems, -1: left_sems}
        self.onward = {1: z < n - 1, -1: z > 0}

    def has(self, step, way):
        return self.z >= step if way > 0 else self.z + step < self.n

    def copy(self, step, way, landed=False):
        send, recv = self.sems[way]
        there = block(self.held, self.z - way * step, self.rows)
        return pltpu.make_async_remote_copy(
            src_ref=there,
            dst_ref=there,
            send_sem=send.at[step],
            recv_sem=recv.at[step - 1 if landed else step],
            device_id=(self.e, self.z + way),
            device_id_type=MESH,
        )

    def begin(self):
        for way in (1, -1):

            @pl.when(self.onward[way])
            def _():
                self.copy(0, way).start()

    def step(self, step):
        for way in (1, -1):

            @pl.when(self.has(step, way))
            def _():
                self.copy(step, way, True).wait_recv()

            @pl.when(self.has(step, way) & self.onward[way])
            def _():
                self.copy(step, way).start()

    def work(self, step, body):
        def one(way, carry):
            d = jnp.where(way > 0, self.z - step, self.z + step)

            @pl.when((d >= 0) & (d < self.n) & ((step > 0) | (way > 0)))
            def _():
                body(d)

            return carry

        lax.fori_loop(0, 2, one, 0)

    def drain(self):
        for step in range(self.n - 1):
            for way in (1, -1):

                @pl.when(self.has(step, way) & self.onward[way])
                def _():
                    self.copy(step, way).wait_send()


class LineScatter:
    def __init__(self, e, z, n, sent, landed, sems, part):
        self.e, self.z, self.n, self.sent, self.landed, self.part = e, z, n, sent, landed, part
        self.send, self.recv = sems
        self.table = line_order(n)

    def outgoing(self, d):
        right = d > self.z
        place = jnp.where(right | (d < self.z - 1), d, self.n)
        return pltpu.make_async_remote_copy(
            src_ref=self.sent.at[d],
            dst_ref=self.landed.at[place],
            send_sem=self.send.at[d],
            recv_sem=self.recv.at[place],
            device_id=(self.e, jnp.where(right, self.z + 1, self.z - 1)),
            device_id_type=MESH,
        )

    def incoming(self, place):
        return pltpu.make_async_remote_copy(
            src_ref=self.landed.at[place],
            dst_ref=self.landed.at[place],
            send_sem=self.send.at[0],
            recv_sem=self.recv.at[place],
            device_id=(self.e, jnp.where(self.z > 0, self.z - 1, self.z + 1)),
            device_id_type=MESH,
        )

    def step(self, j):
        d = lookup(self.table, self.z, j)
        value = self.part(d)
        upstream = jnp.where(d > self.z, self.z > 0, self.z < self.n - 1)

        @pl.when(upstream)
        def _():
            self.incoming(d).wait_recv()
            self.sent[d] = (value + self.landed[d].astype(F32)).astype(BF)

        @pl.when(jnp.logical_not(upstream))
        def _():
            self.sent[d] = value.astype(BF)

        self.outgoing(d).start()

    def finish(self, total):
        total[...] = self.part(self.z)

        @pl.when(self.z > 0)
        def _():
            self.incoming(self.z).wait_recv()
            total[...] += self.landed[self.z].astype(F32)

        @pl.when(self.z < self.n - 1)
        def _():
            self.incoming(self.n).wait_recv()
            total[...] += self.landed[self.n].astype(F32)

    def drain(self):
        for d in range(self.n):

            @pl.when(self.z != d)
            def _():
                self.outgoing(d).wait_send()


def visible_mask(d, rows, length, prefix):
    row_ids = d * rows + lax.broadcasted_iota(jnp.int32, (rows, length), 0)
    col_ids = lax.broadcasted_iota(jnp.int32, (rows, length), 1)
    return (col_ids <= row_ids) | (col_ids < prefix)


def halves(pair, low):
    pair = pair.astype(F32)
    zero = jnp.zeros_like(pair)
    return jnp.where(low, pair, zero), jnp.where(low, pltpu.roll(pair, HD, 1), zero)


def attention_forward_kernel(
    n,
    n_exp,
    tokens,
    gain1,
    w_query,
    w_pair,
    w_out,
    gain2,
    w_router,
    routes,
    prefix,
    cot,
    hidden,
    ext,
    cot_plane,
    held,
    queries,
    pairs,
    mixed,
    totals,
    sent,
    landed,
    ag_rs,
    ag_rr,
    ag_ls,
    ag_lr,
    rs_s,
    rs_r,
    push_s,
    push_r,
    pass_s,
    pass_r,
    local_sem,
):
    e, z = lax.axis_index("exp"), lax.axis_index("tp")
    rows = tokens.shape[0]
    length = rows * n
    kv_local = pairs.shape[1] // LANES
    low = lax.broadcasted_iota(jnp.int32, (rows, LANES), 1) < HD
    barrier, peers = greet(e, z, n, n_exp, True, True)
    scaled, _ = row_scaling(tokens[...].astype(F32))
    held[pl.ds(pl.multiple_of(z * rows, rows), rows)] = (scaled * gain1[...]).astype(BF)

    def project(d):
        at = pl.ds(pl.multiple_of(d * rows, rows), rows)
        normed = held[at]
        queries[at] = mm(normed, w_query[...]).astype(BF)
        pairs[at] = mm(normed, w_pair[...]).astype(BF)

    pl.semaphore_wait(barrier, peers)
    line = LineGather(e, z, n, rows, held, (ag_rs, ag_rr), (ag_ls, ag_lr))
    line.begin()
    plane = PlaneGather(
        e,
        z,
        n_exp,
        cot,
        lambda b: cot_plane.at[b],
        [lambda k, s=s: s.at[k] for s in (push_s, push_r, pass_s, pass_r)],
    )
    plane.begin()
    keep = pltpu.make_async_copy(cot, cot_plane.at[e], local_sem)
    keep.start()
    line.work(0, project)

    def gather_step(step):
        line.step(step)
        line.work(step, project)

    each(n, gather_step, 1)

    def part(d):
        at = pl.ds(pl.multiple_of(d * rows, rows), rows)
        seen = visible_mask(d, rows, length, prefix[0])
        lane = lax.broadcasted_iota(jnp.int32, (rows, LANES), 1)
        stats = jnp.zeros((rows, LANES), F32)
        for kv in range(kv_local):
            span = slice(kv * LANES, (kv + 1) * LANES)
            pair = pairs[:, span]
            outs = []
            for h, head in enumerate(halves(queries[at, span], low)):
                scores = mm_nt((head * HD**-0.5).astype(BF), pair)
                scores = jnp.where(seen, scores, MASKED)
                top = jnp.max(scores, axis=-1, keepdims=True)
                grown = jnp.exp(scores - top)
                total = jnp.sum(grown, axis=-1, keepdims=True)
                probs = (grown / total).astype(BF)
                outs.append(mm(probs, pair))
                stats = jnp.where(lane == 2 * kv + h, top + jnp.log(total), stats)
            both = jnp.where(low, pltpu.roll(outs[0], HD, 1), outs[1])
            mixed[at, span] = both.astype(BF)
        totals[at] = stats
        return mm(mixed[at], w_out[...])

    scatter = LineScatter(e, z, n, sent, landed, (rs_s, rs_r), part)
    each(n - 1, scatter.step)
    plane.relay()
    scatter.finish(hidden)
    hid = tokens[...].astype(F32) + hidden[...]
    hidden[...] = hid
    scaled2, _ = row_scaling(hid)
    normed2 = (scaled2 * gain2[...]).astype(BF)
    ext[:, :D] = normed2
    experts = w_router.shape[1]
    logits = mm(normed2, w_router[...])
    lane = lax.broadcasted_iota(jnp.int32, (rows, experts), 1)
    chosen = lane == routes[:, 0:1]
    for k in range(1, routes.shape[1]):
        chosen = chosen | (lane == routes[:, k : k + 1])
    logits = jnp.where(chosen, logits, MASKED)
    grown = jnp.exp(logits - jnp.max(logits, axis=-1, keepdims=True))
    grown = jnp.where(chosen, grown, 0.0)
    gates = grown / jnp.sum(grown, axis=-1, keepdims=True)
    high = gates.astype(BF)
    low_part = (gates - high.astype(F32)).astype(BF)
    mask = jnp.where(chosen, 1.0, 0.0).astype(BF)
    pad = jnp.zeros((rows, LANES - 3 * experts), BF)
    ext[:, D:] = jnp.concatenate([high, low_part, mask, pad], axis=1)
    keep.wait()
    plane.arrive()
    plane.drain()
    line.drain()
    scatter.drain()


def attention_forward(
    n, n_exp, tokens, gain1, w_query, w_pair, w_out, gain2, w_router, routes, prefix, cot
):
    rows = tokens.shape[0]
    length = rows * n
    qw, pw = w_query.shape[1], w_pair.shape[1]
    v = pl.BlockSpec(memory_space=VMEM)
    sem = pltpu.SemaphoreType.DMA
    return pl.pallas_call(
        functools.partial(attention_forward_kernel, n, n_exp),
        out_shape=(
            jax.ShapeDtypeStruct((rows, D), F32),
            jax.ShapeDtypeStruct((rows, XW), BF),
            jax.ShapeDtypeStruct((n_exp, rows, D), BF),
            jax.ShapeDtypeStruct((length, D), BF),
            jax.ShapeDtypeStruct((length, qw), BF),
            jax.ShapeDtypeStruct((length, pw), BF),
            jax.ShapeDtypeStruct((length, qw), BF),
            jax.ShapeDtypeStruct((length, LANES), F32),
        ),
        in_specs=[v] * 8 + [pl.BlockSpec(memory_space=pltpu.SMEM), v],
        out_specs=[v, v, pl.BlockSpec(memory_space=pl.ANY)] + [v] * 5,
        scratch_shapes=[
            pltpu.VMEM((n, rows, D), BF),
            pltpu.VMEM((n + 1, rows, D), BF),
            sem((n,)),
            sem((n,)),
            sem((n,)),
            sem((n,)),
            sem((n,)),
            sem((n + 1,)),
        ]
        + [sem((n_exp // 2,))] * 4
        + [sem],
        compiler_params=pltpu.CompilerParams(
            collective_id=1, has_side_effects=True, vmem_limit_bytes=48 * MIB
        ),
        cost_estimate=pl.CostEstimate(
            flops=2 * length * D * 4 * qw, bytes_accessed=300 * MIB, transcendentals=0
        ),
    )(tokens, gain1, w_query, w_pair, w_out, gain2, w_router, routes, prefix, cot)


def slot_rows(rows, top_k, experts):
    capacity = rows * top_k * 5 // (experts * 4)
    return -(-capacity // 16) * 16


def selection(extra, first, local_experts, slots):
    rows = extra.shape[0]
    pick = lax.broadcasted_iota(jnp.int32, (8, LANES), 1) == (
        64 + first + lax.broadcasted_iota(jnp.int32, (8, LANES), 0)
    )
    named = mm_nt(jnp.where(pick, 1.0, 0.0).astype(BF), extra)
    earlier = lax.broadcasted_iota(jnp.int32, (rows, rows), 0) < lax.broadcasted_iota(
        jnp.int32, (rows, rows), 1
    )
    place = mm(named.astype(BF), jnp.where(earlier, 1.0, 0.0).astype(BF))
    place = jnp.where(named > 0.5, place, -1.0).astype(jnp.int32)
    slot = lax.broadcasted_iota(jnp.int32, (slots, rows), 0)
    parts = [
        jnp.where(slot == place[k : k + 1, :], 1.0, 0.0) for k in range(local_experts)
    ]
    return jnp.concatenate(parts, axis=0).astype(BF)


def own_gate(extra, expert):
    lane = lax.broadcasted_iota(jnp.int32, extra.shape, 1)
    mine = (lane == expert) | (lane == 32 + expert)
    return jnp.sum(jnp.where(mine, extra.astype(F32), 0.0), axis=-1, keepdims=True)


def sigmoid(v):
    return 1.0 / (1.0 + jnp.exp(-v))


def own_experts_kernel(
    n,
    n_exp,
    local_experts,
    ext,
    cot,
    cot_plane,
    w_gate_up,
    w_down,
    hidden,
    w_router,
    gain2,
    layer_out,
    dhidden,
    dhidden_low,
    router_part,
    norm2_part,
    all_rows,
    xg,
    cg,
    wgu,
    wd,
    sel,
    xs,
    cs,
    core_in,
    chip_out,
    chip_in,
    mix_core_in,
    mix_out,
    mix_in,
    total,
    joined,
    cot_sem,
    w_sem,
    out_sem,
    column_s,
    column_r,
    ag_s,
    ag_r,
    fw_s,
    fw_r,
    core_s,
    core_r,
    chip_s,
    chip_r,
    mcore_s,
    mcore_r,
    mchip_s,
    mchip_r,
):
    e, z = lax.axis_index("exp"), lax.axis_index("tp")
    rows = ext.shape[0]
    chips = n_exp // 2
    chip, core = e // 2, lax.rem(e, 2)
    partner = 2 * chip + 1 - core
    slots = sel.shape[1] // local_experts
    first = e * local_experts
    experts = w_router.shape[1]

    loads = [
        pltpu.make_async_copy(w_gate_up, wgu, w_sem.at[0]),
        pltpu.make_async_copy(w_down, wd, w_sem.at[1]),
    ]
    for b in range(n_exp):
        loads.append(pltpu.make_async_copy(cot_plane.at[b], cg.at[b], cot_sem.at[b]))
    for load in loads:
        load.start()

    barrier, peers = greet(e, z, n, n_exp, False, True)
    for k in range(1, n):
        pl.semaphore_signal(barrier, inc=1, device_id=(e, z ^ k), device_id_type=MESH)
    xg[e] = ext[...]
    joined[:, :XW] = ext[...]
    joined[:, XW:] = cot[...]
    pl.semaphore_wait(barrier, peers + n - 1)
    plane = PlaneGather(
        e,
        z,
        n_exp,
        xg.at[e],
        lambda b: xg.at[b],
        [lambda k, s=s: s.at[k] for s in (ag_s, ag_r, fw_s, fw_r)],
    )
    there, other = plane.mine, plane.other
    plane.begin()

    def up_column(k, landed=False):
        return pltpu.make_async_remote_copy(
            src_ref=joined,
            dst_ref=all_rows.at[(z ^ k) if landed else z, e],
            send_sem=column_s.at[k],
            recv_sem=column_r.at[k],
            device_id=(e, z ^ k),
            device_id_type=MESH,
        )

    for k in range(1, n):
        up_column(k).start()
    for load in loads[2:]:
        load.wait()

    def gather(b):
        s = selection(xg[b, :, D:], first, local_experts, slots)
        sel[b] = s
        xs[b] = mm(s, xg[b]).astype(BF)
        cs[b] = mm(s, cg[b]).astype(BF)

    def save(b):
        return (
            pltpu.make_async_copy(xg.at[b], all_rows.at[z, b, :, pl.ds(0, XW)], out_sem.at[0, b]),
            pltpu.make_async_copy(cg.at[b], all_rows.at[z, b, :, pl.ds(XW, D)], out_sem.at[1, b]),
        )

    gather(e)
    plane.relay()
    each(chips, lambda k: gather(there(k)), 1)
    plane.arrive()
    each(chips, lambda k: gather(other(k)))

    def start_save(b):
        for copy in save(b):
            copy.start()

    def end_save(b):
        for copy in save(b):
            copy.wait()

    each(n_exp, start_save)
    for load in loads[:2]:
        load.wait()

    groups = n_exp // GROUP

    def expert_step(step, carry):
        k = step // groups
        b0 = lax.rem(step, groups) * GROUP
        at = pl.ds(pl.multiple_of(k * slots, slots), slots)
        wide = jnp.concatenate([xs[b0 + i, at] for i in range(GROUP)], axis=0)
        gate_value = own_gate(wide[:, D:], first + k)
        units = mm(wide[:, :D], wgu[k])
        gate, up = units[:, :FF], units[:, FF:]
        sig = sigmoid(gate)
        silu = gate * sig
        active = (silu * up).astype(BF)
        made = mm(active, wd[k]).astype(BF).astype(F32)
        upstream = jnp.concatenate([cs[b0 + i, at] for i in range(GROUP)], axis=0).astype(F32)
        dgate_value = jnp.sum(upstream * made, axis=-1, keepdims=True)
        share = (gate_value * made).astype(BF)
        dmade = (gate_value * upstream).astype(BF)
        dactive = mm_nt(dmade, wd[k])
        dgate = dactive * up * sig * (1.0 + gate * (1.0 - sig))
        dunits = jnp.concatenate([dgate, dactive * silu], axis=1).astype(BF)
        dx = mm_nt(dunits, wgu[k]).astype(BF)
        lane = lax.broadcasted_iota(jnp.int32, (GROUP * slots, LANES), 1)
        high = dgate_value.astype(BF).astype(F32)
        packed = jnp.where(lane == first + k, high, 0.0)
        packed = jnp.where(lane == 32 + first + k, dgate_value - high, packed).astype(BF)
        for i in range(GROUP):
            here = slice(i * slots, (i + 1) * slots)
            xs[b0 + i, at, :D] = share[here]
            xs[b0 + i, at, D:] = packed[here]
            cs[b0 + i, at] = dx[here]
        return carry

    lax.fori_loop(0, local_experts * groups, expert_step, 0)

    each(n_exp, end_save)
    plane.drain()

    def core_copy(k, src, dst, s, r):
        return pltpu.make_async_remote_copy(
            src_ref=src.at[other(k)],
            dst_ref=dst.at[k],
            send_sem=s.at[k],
            recv_sem=r.at[k],
            device_id=(partner, z),
            device_id_type=MESH,
        )

    def chip_copy(k, src, dst, s, r):
        return pltpu.make_async_remote_copy(
            src_ref=src.at[k],
            dst_ref=dst.at[k],
            send_sem=s.at[k],
            recv_sem=r.at[k],
            device_id=(there(k), z),
            device_id_type=MESH,
        )

    def grads_of(b):
        s = sel[b]
        return jnp.concatenate([mm_tn(s, cs[b]), mm_tn(s, xs[b, :, D:])], axis=1)

    def give_grads(i):
        k = chips - 1 - i
        xg[other(k)] = grads_of(other(k)).astype(BF)
        core_copy(k, xg, core_in, core_s, core_r).start()

    def pass_grads(i):
        k = chips - 1 - i
        mine = grads_of(there(k))
        core_copy(k, xg, core_in, core_s, core_r).wait_recv()
        chip_out[k] = (mine + core_in[k].astype(F32)).astype(BF)
        chip_copy(k, chip_out, chip_in, chip_s, chip_r).start()

    def give_mix(i):
        k = chips - 1 - i
        cg[other(k)] = mm_tn(sel[other(k)], xs[other(k), :, :D]).astype(BF)
        core_copy(k, cg, mix_core_in, mcore_s, mcore_r).start()

    def pass_mix(i):
        k = chips - 1 - i
        mine = mm_tn(sel[there(k)], xs[there(k), :, :D])
        core_copy(k, cg, mix_core_in, mcore_s, mcore_r).wait_recv()
        mix_out[k] = (mine + mix_core_in[k].astype(F32)).astype(BF)
        chip_copy(k, mix_out, mix_in, mchip_s, mchip_r).start()

    each(chips, give_grads)
    each(chips - 1, pass_grads)
    each(chips, give_mix)
    each(chips - 1, pass_mix)
    total[...] = grads_of(e)
    core_copy(0, xg, core_in, core_s, core_r).wait_recv()
    total[...] += core_in[0].astype(F32)

    def take_grads(i):
        k = chips - 1 - i
        chip_copy(k, chip_out, chip_in, chip_s, chip_r).wait_recv()
        total[...] += chip_in[k].astype(F32)

    each(chips - 1, take_grads)
    extra = ext[:, D:].astype(F32)
    gates = extra[:, :experts] + extra[:, experts : 2 * experts]
    dgates = total[:, D : D + experts] + total[:, D + experts : D + 2 * experts]
    dlogits = gates * (dgates - jnp.sum(gates * dgates, axis=-1, keepdims=True))
    dlogits = dlogits.astype(BF)
    normed2 = ext[:, :D]
    router_part[...] = mm_tn(dlogits, normed2)
    dnormed2 = total[:, :D] + mm_nt(dlogits, w_router[...])
    scaled2, inverse2 = row_scaling(hidden[...])
    norm2_part[...] = jnp.broadcast_to(
        jnp.sum(dnormed2 * scaled2, axis=0, keepdims=True), norm2_part.shape
    )
    back = cot[...].astype(F32) + norm_backward(dnormed2, scaled2, inverse2, gain2[...])
    dhidden[...] = back
    dhidden_low[...] = back.astype(BF)

    total[:, :D] = hidden[...] + mm_tn(sel[e], xs[e, :, :D])
    core_copy(0, cg, mix_core_in, mcore_s, mcore_r).wait_recv()
    total[:, :D] += mix_core_in[0].astype(F32)

    def take_mix(i):
        k = chips - 1 - i
        chip_copy(k, mix_out, mix_in, mchip_s, mchip_r).wait_recv()
        total[:, :D] += mix_in[k].astype(F32)

    each(chips - 1, take_mix)
    layer_out[...] = total[:, :D].astype(BF)

    def sent_to_core(k):
        core_copy(k, xg, core_in, core_s, core_r).wait_send()
        core_copy(k, cg, mix_core_in, mcore_s, mcore_r).wait_send()

    def sent_to_chip(i):
        chip_copy(i + 1, chip_out, chip_in, chip_s, chip_r).wait_send()
        chip_copy(i + 1, mix_out, mix_in, mchip_s, mchip_r).wait_send()

    each(chips, sent_to_core)
    each(chips - 1, sent_to_chip)
    for k in range(1, n):
        up_column(k, True).wait_recv()
        up_column(k).wait_send()


def own_experts(n, n_exp, ext, cot, cot_plane, w_gate_up, w_down, hidden, w_router, gain2, slots):
    rows = ext.shape[0]
    local_experts = w_gate_up.shape[0]
    experts = w_router.shape[1]
    chips = n_exp // 2
    v = pl.BlockSpec(memory_space=VMEM)
    hbm = pl.BlockSpec(memory_space=pl.ANY)
    sem = pltpu.SemaphoreType.DMA
    taken = n_exp * local_experts * slots
    return pl.pallas_call(
        functools.partial(own_experts_kernel, n, n_exp, local_experts),
        out_shape=(
            jax.ShapeDtypeStruct((rows, D), BF),
            jax.ShapeDtypeStruct((rows, D), F32),
            jax.ShapeDtypeStruct((rows, D), BF),
            jax.ShapeDtypeStruct((experts, D), F32),
            jax.ShapeDtypeStruct((8, D), F32),
            jax.ShapeDtypeStruct((n, n_exp, rows, RW), BF),
        ),
        in_specs=[v, v, hbm, hbm, hbm, v, v, v],
        out_specs=[v] * 5 + [hbm],
        scratch_shapes=[
            pltpu.VMEM((n_exp, rows, XW), BF),
            pltpu.VMEM((n_exp, rows, D), BF),
            pltpu.VMEM(w_gate_up.shape, BF),
            pltpu.VMEM(w_down.shape, BF),
            pltpu.VMEM((n_exp, local_experts * slots, rows), BF),
            pltpu.VMEM((n_exp, local_experts * slots, XW), BF),
            pltpu.VMEM((n_exp, local_experts * slots, D), BF),
            pltpu.VMEM((chips, rows, XW), BF),
            pltpu.VMEM((chips, rows, XW), BF),
            pltpu.VMEM((chips, rows, XW), BF),
            pltpu.VMEM((chips, rows, D), BF),
            pltpu.VMEM((chips, rows, D), BF),
            pltpu.VMEM((chips, rows, D), BF),
            pltpu.VMEM((rows, XW), F32),
            pltpu.VMEM((rows, RW), BF),
            sem((n_exp,)),
            sem((2,)),
            sem((2, n_exp)),
            sem((n,)),
            sem((n,)),
        ]
        + [sem((chips,))] * 12,
        compiler_params=pltpu.CompilerParams(
            collective_id=2, has_side_effects=True, vmem_limit_bytes=62 * MIB
        ),
        cost_estimate=pl.CostEstimate(
            flops=2 * taken * 6 * D * FF, bytes_accessed=300 * MIB, transcendentals=0
        ),
    )(ext, cot, cot_plane, w_gate_up, w_down, hidden, w_router, gain2)


def expert_middle(x, gate_value, upstream, w_gate_up, w_down):
    units = mm(x, w_gate_up)
    gate, up = units[:, :FF], units[:, FF:]
    sig = sigmoid(gate)
    silu = gate * sig
    dmade = (gate_value * upstream.astype(F32)).astype(BF)
    dactive = mm_nt(dmade, w_down)
    dgate = dactive * up * sig * (1.0 + gate * (1.0 - sig))
    return dmade, (silu * up).astype(BF), dgate.astype(BF), (dactive * silu).astype(BF)


def expert_grads_kernel(
    blocks,
    groups,
    early,
    local_experts,
    rows_all,
    *refs,
):
    first = lax.axis_index("exp") * local_experts + early
    k, g = pl.program_id(0), pl.program_id(1)
    refs = list(refs)
    w_gate_up, w_down = refs.pop(0), refs.pop(0)
    done = (refs.pop(0), refs.pop(0)) if early else None
    gate_up_grad, down_grad, rbuf, kept_x, kept_dy, kept_active, kept_dunits = refs[:7]
    acc_up, acc_down, sems, out_sems, copy_sems = refs[7:]
    slots = kept_x.shape[0] // blocks
    chunks = blocks // GROUP
    size = GROUP * slots
    last = local_experts - early - 1

    def brought():
        return (
            pltpu.make_async_copy(done[0], acc_up.at[pl.ds(0, early)], copy_sems.at[0]),
            pltpu.make_async_copy(done[1], acc_down.at[pl.ds(0, early)], copy_sems.at[1]),
        )

    def taken():
        return (
            pltpu.make_async_copy(
                acc_up.at[pl.ds(0, early)], gate_up_grad.at[pl.ds(0, early)], copy_sems.at[0]
            ),
            pltpu.make_async_copy(
                acc_down.at[pl.ds(0, early)], down_grad.at[pl.ds(0, early)], copy_sems.at[1]
            ),
        )

    opening = (k == 0) & (g == 0)
    if early:

        @pl.when(opening)
        def _():
            for copy in brought():
                copy.start()

    def load(c, slot):
        at = pl.ds(g * blocks + c * GROUP, GROUP)
        return pltpu.make_async_copy(rows_all.at[at], rbuf.at[slot], sems.at[slot])

    load(0, 0).start()

    def chunk(c, carry):
        slot = lax.rem(c, 2)

        @pl.when(c + 1 < chunks)
        def _():
            load(c + 1, 1 - slot).start()

        load(c, slot).wait()
        if early:

            @pl.when(opening & (c == 2))
            def _():
                for copy in brought():
                    copy.wait()
                for copy in taken():
                    copy.start()

        wide = []
        for i in range(GROUP):
            s = selection(rbuf[slot, i, :, D:XW], first + k, 1, slots)
            wide.append(mm(s, rbuf[slot, i]))
        wide = jnp.concatenate(wide, axis=0)
        x = wide[:, :D].astype(BF)
        made = expert_middle(
            x, own_gate(wide[:, D:XW], first + k), wide[:, XW:], w_gate_up[0], w_down[0]
        )
        at = pl.ds(pl.multiple_of(c * size, size), size)
        kept_x[at] = x
        kept_dy[at] = made[0]
        kept_active[at] = made[1]
        kept_dunits[at, :FF] = made[2]
        kept_dunits[at, FF:] = made[3]
        return carry

    lax.fori_loop(0, chunks, chunk, 0)
    bank = lax.rem(k, 2)
    if early:

        @pl.when(opening)
        def _():
            for copy in taken():
                copy.wait()

    def store(kk):
        b = lax.rem(kk, 2)
        return (
            pltpu.make_async_copy(acc_up.at[b], gate_up_grad.at[early + kk], out_sems.at[0, b]),
            pltpu.make_async_copy(acc_down.at[b], down_grad.at[early + kk], out_sems.at[1, b]),
        )

    @pl.when((g == 0) & (k >= 2))
    def _():
        for copy in store(k - 2):
            copy.wait()

    def add(out, at, value):
        if groups == 1:
            out[bank, at] = value
        else:

            @pl.when(g == 0)
            def _():
                out[bank, at] = value

            @pl.when(g > 0)
            def _():
                out[bank, at] += value

    tile = 256

    def up_tile(m, carry):
        at = pl.ds(pl.multiple_of(m * tile, tile), tile)
        add(acc_up, at, mm_tn(kept_x[:, at], kept_dunits[...]))
        return carry

    lax.fori_loop(0, D // tile, up_tile, 0)

    def down_tile(m, carry):
        at = pl.ds(pl.multiple_of(m * tile, tile), tile)
        add(acc_down, at, mm_tn(kept_active[:, at], kept_dy[...]))
        return carry

    lax.fori_loop(0, FF // tile, down_tile, 0)

    @pl.when(g == groups - 1)
    def _():
        for copy in store(k):
            copy.start()

    @pl.when((g == groups - 1) & (k == last))
    def _():
        for copy in store(k):
            copy.wait()
        if last > 0:
            for copy in store(k - 1):
                copy.wait()


def expert_grads(rows_all, w_gate_up, w_down, done, slots):
    total, rows = rows_all.shape[:2]
    local_experts = w_gate_up.shape[0]
    early = done[0].shape[0] if done else 0
    assert early <= 2
    blocks = min(total, 32)
    groups = total // blocks
    kept = blocks * slots
    hbm = pl.BlockSpec(memory_space=pl.ANY)
    sem = pltpu.SemaphoreType.DMA
    return pl.pallas_call(
        functools.partial(expert_grads_kernel, blocks, groups, early, local_experts),
        grid=(local_experts - early, groups),
        out_shape=(
            jax.ShapeDtypeStruct((local_experts, D, 2 * FF), F32),
            jax.ShapeDtypeStruct((local_experts, FF, D), F32),
        ),
        in_specs=[
            hbm,
            pl.BlockSpec((1, D, 2 * FF), lambda k, g: (k + early, 0, 0)),
            pl.BlockSpec((1, FF, D), lambda k, g: (k + early, 0, 0)),
        ]
        + [hbm] * len(done),
        out_specs=[hbm, hbm],
        scratch_shapes=[
            pltpu.VMEM((2, GROUP, rows, RW), BF),
            pltpu.VMEM((kept, D), BF),
            pltpu.VMEM((kept, D), BF),
            pltpu.VMEM((kept, FF), BF),
            pltpu.VMEM((kept, 2 * FF), BF),
            pltpu.VMEM((2, D, 2 * FF), F32),
            pltpu.VMEM((2, FF, D), F32),
            sem((2,)),
            sem((2, 2)),
            sem((2,)),
        ],
        compiler_params=pltpu.CompilerParams(vmem_limit_bytes=60 * MIB),
        cost_estimate=pl.CostEstimate(
            flops=2 * total * slots * local_experts * 6 * D * FF,
            bytes_accessed=300 * MIB,
            transcendentals=0,
        ),
    )(rows_all, w_gate_up, w_down, *done)


def backward_kernel(n, n_exp, early, local_experts, *refs):
    refs = list(refs)

    def take(count):
        got = refs[:count]
        del refs[:count]
        return got

    dhidden_low, dhidden, tokens, gain1, held, queries, pairs, mixed, totals = take(9)
    w_query, w_pair, w_out, prefix, _ = take(5)
    if early:
        w_gate_up, w_down = take(2)
    input_grad, query_grad, pair_grad, out_grad, norm1, all_rows = take(6)
    if early:
        gate_up_grad, down_grad = take(2)
    dfull, dqueries, dpairs, dpairs_low, sent, landed, line_norms, plane_norms = take(8)
    ag_rs, ag_rr, ag_ls, ag_lr, rs_s, rs_r, push_s, push_r, pass_s, pass_r = take(10)
    nz_s, nz_r, np_s, np_r = take(4)
    if early:
        tokens_in, wgu, wd, acc_up, acc_down, kept_x, kept_c, kept_active, kept_dunits = take(9)
        load_s, w_sem, out_sem = take(3)

    e, z = lax.axis_index("exp"), lax.axis_index("tp")
    rows = tokens.shape[0]
    length = rows * n
    kv_local = pairs.shape[1] // LANES
    low = lax.broadcasted_iota(jnp.int32, (rows, LANES), 1) < HD
    scale = HD**-0.5
    first = e * local_experts

    if early:
        weights = [
            pltpu.make_async_copy(w_gate_up.at[pl.ds(0, early)], wgu, w_sem.at[0]),
            pltpu.make_async_copy(w_down.at[pl.ds(0, early)], wd, w_sem.at[1]),
        ]
        for copy in weights:
            copy.start()

    barrier = pltpu.get_barrier_semaphore()

    def greet_plane(k):
        pl.semaphore_signal(barrier, inc=1, device_id=(e ^ k, z), device_id_type=MESH)

    def greet_line(k):
        pl.semaphore_signal(barrier, inc=1, device_id=(e, z ^ k), device_id_type=MESH)

    each(n_exp, greet_plane, 1)
    each(n, greet_line, 1)
    dfull[pl.ds(pl.multiple_of(z * rows, rows), rows)] = dhidden_low[...]
    dpairs[...] = jnp.zeros_like(dpairs)
    pl.semaphore_wait(barrier, n_exp + n - 2)

    line = LineGather(e, z, n, rows, dfull, (ag_rs, ag_rr), (ag_ls, ag_lr))
    line.begin()

    def plane(i):
        return PlaneGather(
            e,
            z,
            n_exp,
            all_rows.at[z ^ i, e],
            lambda b: all_rows.at[z ^ i, b],
            [lambda k, s=s: s.at[i, k] for s in (push_s, push_r, pass_s, pass_r)],
        )

    plane(1).begin()

    def attend(d):
        at = pl.ds(pl.multiple_of(d * rows, rows), rows)
        seen = visible_mask(d, rows, length, prefix[0])
        dmixed = mm_nt(dfull[at], w_out[...]).astype(BF)
        stats = totals[at]
        for kv in range(kv_local):
            span = slice(kv * LANES, (kv + 1) * LANES)
            pair = pairs[:, span]
            outs = []
            added = jnp.zeros((length, LANES), F32)
            heads = halves(queries[at, span], low)
            grads = halves(dmixed[:, span], low)
            for h in range(2):
                head = (heads[h] * scale).astype(BF)
                grad = pltpu.roll(grads[h], HD, 1).astype(BF)
                stat = 2 * kv + h
                scores = mm_nt(head, pair)
                probs = jnp.where(seen, jnp.exp(scores - stats[:, stat : stat + 1]), 0.0)
                dprobs = mm_nt(grad, pair)
                inner = jnp.sum(probs * dprobs, axis=-1, keepdims=True)
                dscores = (probs * (dprobs - inner)).astype(BF)
                outs.append(mm(dscores, pair) * scale)
                added += mm_tn(dscores, head) + mm_tn(probs.astype(BF), grad)
            both = jnp.where(low, outs[0], pltpu.roll(outs[1], HD, 1))
            dqueries[at, span] = both.astype(BF)
            dpairs[:, span] += added

    def part(d):
        at = pl.ds(pl.multiple_of(d * rows, rows), rows)
        return mm_nt(dqueries[at], w_query[...]) + mm_nt(dpairs_low[at], w_pair[...])

    scatter = LineScatter(e, z, n, sent, landed, (rs_s, rs_r), part)

    def line_norm(k, landed=False):
        return pltpu.make_async_remote_copy(
            src_ref=line_norms.at[z],
            dst_ref=line_norms.at[(z ^ k) if landed else z],
            send_sem=nz_s.at[k],
            recv_sem=nz_r.at[k],
            device_id=(e, z ^ k),
            device_id_type=MESH,
        )

    def plane_norm(k, landed=False):
        return pltpu.make_async_remote_copy(
            src_ref=plane_norms.at[e],
            dst_ref=plane_norms.at[(e ^ k) if landed else e],
            send_sem=np_s.at[k],
            recv_sem=np_r.at[k],
            device_id=(e ^ k, z),
            device_id_type=MESH,
        )

    def event(t):
        @pl.when((t > 0) & (t < n))
        def _():
            line.step(t)

        @pl.when(t < n)
        def _():
            line.work(t, attend)

        @pl.when(t == n)
        def _():
            dpairs_low[...] = dpairs[...].astype(BF)

        @pl.when((t >= n) & (t < 2 * n - 1))
        def _():
            scatter.step(t - n)

        @pl.when(t == 2 * n - 1)
        def _():
            query_grad[...] = mm_tn(held[...], dqueries[...]).astype(BF)
            pair_grad[...] = mm_tn(held[...], dpairs_low[...]).astype(BF)
            out_grad[...] = mm_tn(mixed[...], dfull[...]).astype(BF)

        @pl.when(t == 2 * n)
        def _():
            scatter.finish(input_grad)
            dnormed1 = input_grad[...]
            scaled, inverse = row_scaling(tokens[...].astype(F32))
            total = jnp.sum(dnormed1 * scaled, axis=0, keepdims=True)
            line_norms[z] = jnp.concatenate(
                [total[:, k * LANES : (k + 1) * LANES] for k in range(D // LANES)], axis=0
            )
            each(n, lambda k: line_norm(k).start(), 1)
            back = dhidden[...] + norm_backward(dnormed1, scaled, inverse, gain1[...])
            input_grad[...] = back

        @pl.when(t == 2 * n + 1)
        def _():
            each(n, lambda k: line_norm(k, True).wait_recv(), 1)
            total = line_norms[0]
            for k in range(1, n):
                total = total + line_norms[k]
            plane_norms[e] = total
            each(n_exp, lambda k: plane_norm(k).start(), 1)

    events = 2 * n + 2
    steps = n * (1 + early) if early else 0

    def relay(i):
        each(n_exp // 2, lambda k: plane(i).pushed(k).wait_recv(), 1)

        @pl.when(i + 1 < n)
        def _():
            plane(i + 1).begin()

        each(n_exp // 2, lambda k: plane(i).hand(k).start(), 1)

    if early:
        slots = kept_x.shape[1] // n_exp
        acc_up[...] = jnp.zeros_like(acc_up)
        acc_down[...] = jnp.zeros_like(acc_down)
        for copy in weights:
            copy.wait()

        def one_plane(i, carry):
            @pl.when(i > 0)
            def _():
                plane(i).arrive()

            def load(b):
                return pltpu.make_async_copy(
                    all_rows.at[z ^ i, b], tokens_in.at[b], load_s.at[b]
                )

            each(n_exp, lambda b: load(b).start())

            def pick(b):
                load(b).wait()
                s = selection(tokens_in[b, :, D:XW], first, early, slots)
                got = mm(s, tokens_in[b]).astype(BF)
                at = pl.ds(pl.multiple_of(b * slots, slots), slots)
                for k in range(early):
                    here = got[k * slots : (k + 1) * slots]
                    kept_x[k, at] = here[:, :XW]
                    kept_c[k, at] = here[:, XW:]

            each(n_exp, pick)
            event(i * (1 + early))

            def expert(k):
                gate_value = own_gate(kept_x[k, :, D:], first + k)
                x = kept_x[k, :, :D]
                made = expert_middle(x, gate_value, kept_c[k], wgu[k], wd[k])
                kept_c[k] = made[0]
                kept_active[...] = made[1]
                kept_dunits[:, :FF] = made[2]
                kept_dunits[:, FF:] = made[3]
                acc_up[k] += mm_tn(kept_x[k, :, :D], kept_dunits[...])
                acc_down[k] += mm_tn(kept_active[...], kept_c[k])
                event(i * (1 + early) + 1 + k)

            each(early, expert)

            @pl.when(i + 1 < n)
            def _():
                relay(i + 1)

            return carry

        lax.fori_loop(0, n, one_plane, 0)
        stores = [
            pltpu.make_async_copy(acc_up, gate_up_grad, out_sem.at[0]),
            pltpu.make_async_copy(acc_down, down_grad, out_sem.at[1]),
        ]
        for copy in stores:
            copy.start()
    each(max(events, steps), event, steps)
    if early:
        for copy in stores:
            copy.wait()
    else:

        def one_relay(i):
            relay(i)

        each(n, one_relay, 1)
        each(n, lambda i: plane(i).arrive(), 1)
    each(n_exp, lambda k: plane_norm(k, True).wait_recv(), 1)
    total = plane_norms[0]
    for k in range(1, n_exp):
        total = total + plane_norms[k]
    norm1[...] = total
    each(n, lambda i: plane(i).drain(), 1)
    each(n, lambda k: line_norm(k).wait_send(), 1)
    each(n_exp, lambda k: plane_norm(k).wait_send(), 1)
    line.drain()
    scatter.drain()


def backward(n, n_exp, slots, whole, prefix, all_rows, weights):
    tokens, held = whole[2], whole[4]
    rows = tokens.shape[0]
    length = rows * n
    qw, pw = whole[9].shape[1], whole[10].shape[1]
    local_experts = weights[0].shape[0]
    early = local_experts // 2
    v = pl.BlockSpec(memory_space=VMEM)
    hbm = pl.BlockSpec(memory_space=pl.ANY)
    sem = pltpu.SemaphoreType.DMA
    chips = n_exp // 2
    outs = [
        (jax.ShapeDtypeStruct((rows, D), F32), v),
        (jax.ShapeDtypeStruct((D, qw), BF), v),
        (jax.ShapeDtypeStruct((D, pw), BF), v),
        (jax.ShapeDtypeStruct((qw, D), BF), v),
        (jax.ShapeDtypeStruct((D // LANES, LANES), F32), v),
        (jax.ShapeDtypeStruct((n, n_exp, rows, RW), BF), hbm),
    ]
    scratch = [
        pltpu.VMEM((length, D), BF),
        pltpu.VMEM((length, qw), BF),
        pltpu.VMEM((length, pw), F32),
        pltpu.VMEM((length, pw), BF),
        pltpu.VMEM((n, rows, D), BF),
        pltpu.VMEM((n + 1, rows, D), BF),
        pltpu.VMEM((n, D // LANES, LANES), F32),
        pltpu.VMEM((n_exp, D // LANES, LANES), F32),
        sem((n,)),
        sem((n,)),
        sem((n,)),
        sem((n,)),
        sem((n,)),
        sem((n + 1,)),
    ]
    scratch += [sem((n, chips))] * 4
    scratch += [sem((n,)), sem((n,)), sem((n_exp,)), sem((n_exp,))]
    if early:
        kept = n_exp * slots
        outs += [
            (jax.ShapeDtypeStruct((early, D, 2 * FF), F32), hbm),
            (jax.ShapeDtypeStruct((early, FF, D), F32), hbm),
        ]
        scratch += [
            pltpu.VMEM((n_exp, rows, RW), BF),
            pltpu.VMEM((early, D, 2 * FF), BF),
            pltpu.VMEM((early, FF, D), BF),
            pltpu.VMEM((early, D, 2 * FF), F32),
            pltpu.VMEM((early, FF, D), F32),
            pltpu.VMEM((early, kept, XW), BF),
            pltpu.VMEM((early, kept, D), BF),
            pltpu.VMEM((kept, FF), BF),
            pltpu.VMEM((kept, 2 * FF), BF),
            sem((n_exp,)),
            sem((2,)),
            sem((2,)),
        ]
    return pl.pallas_call(
        functools.partial(backward_kernel, n, n_exp, early, local_experts),
        out_shape=tuple(shape for shape, _ in outs),
        in_specs=[v] * len(whole)
        + [pl.BlockSpec(memory_space=pltpu.SMEM)]
        + [hbm] * (1 + (2 if early else 0)),
        out_specs=tuple(spec for _, spec in outs),
        input_output_aliases={len(whole) + 1: 5},
        scratch_shapes=scratch,
        compiler_params=pltpu.CompilerParams(
            collective_id=3, has_side_effects=True, vmem_limit_bytes=62 * MIB
        ),
        cost_estimate=pl.CostEstimate(
            flops=2 * length * D * 8 * qw, bytes_accessed=300 * MIB, transcendentals=0
        ),
    )(*whole, prefix, all_rows, *(weights if early else ()))


def local(
    n_exp,
    n_tp,
    tokens,
    norm1_gain,
    w_query,
    w_key_value,
    w_out,
    norm2_gain,
    w_router,
    w_gate_up,
    w_down,
    routes,
    prefix,
    cotangent,
):
    rows = tokens.shape[0]
    experts = w_router.shape[1]
    slots = slot_rows(rows, routes.shape[1], experts)
    w_pair = w_key_value.reshape(D, -1)
    gain1, gain2 = norm1_gain.reshape(1, D), norm2_gain.reshape(1, D)
    hidden, ext, cot_plane, held, queries, pairs, mixed, totals = attention_forward(
        n_tp,
        n_exp,
        tokens,
        gain1,
        w_query,
        w_pair,
        w_out,
        gain2,
        w_router,
        routes,
        prefix,
        cotangent,
    )
    layer_out, dhidden, dhidden_low, router_part, norm2_part, all_rows = own_experts(
        n_tp,
        n_exp,
        ext,
        cotangent,
        cot_plane,
        w_gate_up,
        w_down,
        hidden,
        w_router,
        gain2,
        slots,
    )
    small = jnp.concatenate([router_part, norm2_part], axis=0)
    small = lax.psum(small, ("exp", "tp"))
    whole = (dhidden_low, dhidden, tokens, gain1, held, queries, pairs, mixed, totals)
    whole += (w_query, w_pair, w_out)
    made = backward(n_tp, n_exp, slots, whole, prefix, all_rows, (w_gate_up, w_down))
    input_grad, query_grad, pair_grad, out_grad, norm1, all_rows = made[:6]
    gate_up_grad, down_grad = expert_grads(
        all_rows.reshape(n_exp * n_tp, rows, RW), w_gate_up, w_down, made[6:], slots
    )
    query_grad, pair_grad, out_grad = (
        lax.psum(query_grad, "exp").astype(F32),
        lax.psum(pair_grad, "exp").astype(F32),
        lax.psum(out_grad, "exp").astype(F32),
    )
    return (
        layer_out,
        input_grad,
        norm1.reshape(D),
        query_grad,
        pair_grad.reshape(w_key_value.shape),
        out_grad,
        small[experts],
        small[:experts].T,
        gate_up_grad,
        down_grad,
    )


def solution(mesh):
    return jax.shard_map(
        functools.partial(local, mesh.shape["exp"], mesh.shape["tp"]),
        mesh=mesh,
        in_specs=(
            P(("exp", "tp"), None),
            P(),
            P(None, "tp"),
            P(None, "tp", None),
            P("tp", None),
            P(),
            P(),
            P("exp", None, None),
            P("exp", None, None),
            P(("exp", "tp"), None),
            P("exp"),
            P(("exp", "tp"), None),
        ),
        out_specs=(
            P(("exp", "tp"), None),
            P(("exp", "tp"), None),
            P(),
            P(None, "tp"),
            P(None, "tp", None),
            P("tp", None),
            P(),
            P(),
            P("exp", None, None),
            P("exp", None, None),
        ),
        check_vma=False,
    )
```

time: 851 us -> 513 us (0.60)
  waiting for transfers between devices: 306 us -> 0.06 us
  Pallas kernels: 494 us -> 461 us
    all_gather x2 -> x0, waiting for transfers between devices: 124 us -> none  [the longest x1 119 us: local(): ext_all = lax.all_gather(ext, ('exp', 'tp'), axis=0, tiled=True)]
    psum x1, waiting for transfers between devices: 121 us -> 0.02 us  [local(): small = lax.psum(small, ('exp', 'tp'))]
    psum x1, waiting for transfers between devices: 59.8 us -> 0.01 us  [local(): lax.psum(query_grad, 'exp').astype(F32)]
    pallas_call x4, Pallas kernels: 494 us -> 461 us  [the longest x1 188 us: backward(): pl.pallas_call(functools.partial(backward_kernel, n, n_exp, early, local_...]
  transfers between devices with their start and end apart: 4 -> 2, of which waited for: 4 -> 0; matrix products, arithmetic and copies ran while one was open for 2% -> 1% of each run, Pallas kernels for 17% -> 53%
where the time goes in v2:
time: 513 us; the launch traced here: 504 us
  Pallas kernels  461 us (90%)
  local copies, waits for them, and re-layouts  20 us (4%)
  between operations  15.1 us (3%)
  other arithmetic  8.18 us (2%)
    pallas_call x1, Pallas kernels, backward(): pl.pallas_call(functools.partial(backward_kernel, n, n_exp, early, local_...  188 us
    pallas_call x1, Pallas kernels, own_experts(): pl.pallas_call(functools.partial(own_experts_kernel, n, n_exp, local_expe...  111 us
    pallas_call x1, Pallas kernels, expert_grads(): pl.pallas_call(functools.partial(expert_grads_kernel, blocks, groups, ear...  81.7 us
    pallas_call x1, Pallas kernels, attention_forward(): pl.pallas_call(functools.partial(attention_forward_kernel, n, n_exp), out...  80.8 us
    unnamed x38, local copies, waits for them, and re-layouts  15.1 us
  transfers between devices with their start and end apart: 2, of which 0 were waited for; matrix products, arithmetic and copies ran while one was open for 1% of the time, Pallas kernels for 53%

profile of v2, /device:TPU:8, one launch (start us, length us, event | category | flops | bytes accessed | tf_op | source)
XLA Modules:
  0.0 504.2 jit_solution(17751479269988028021)
XLA Ops:
  7.2 0.0 all-reduce.4.cloned.1.call-start
  7.9 0.8 copy.24.routes
  8.7 1.0 copy.23.w_router
  9.7 0.0 copy-start.8
  9.7 1.2 copy.28
  10.9 0.0 copy-start
  11.0 0.0 copy-start.1
  11.0 1.2 copy-done.1
  12.2 0.0 copy-start.2
  12.2 1.0 copy-done.2
  13.2 0.0 copy-start.3
  13.2 1.0 copy-done.3
  14.3 0.0 copy-start.9
  14.3 0.7 copy-done.9
  15.0 1.0 copy-done.10
  16.0 0.7 copy-done.11
  16.7 80.8 %shard_map.195 = (f32[256,1024]{1,0:T(8,128)}, bf16[256,1152]{1,0:T(8,128)(2,1)S(1)}, bf16[8,256,1024]{2,1,0:T(8,128)(2,1)}, bf16[1024,1024]{1,0:T(8,128)(2,1)},...) custom-call(bf16[256,1024]{1,0:T(8,128)(2,1)S(1)} %copy-done.1, ...), custom_call_target="tpu_custom_call" | custom-call | flops 2147483648 | bytes 314572800 | tf_op jit(solution)/shard_map/pallas_call | solution.py:462
  97.5 0.0 copy-start.4
  97.5 0.8 copy-done.4
  98.3 0.8 copy-done.5
  99.1 0.8 copy-done.6
  99.9 0.8 copy-done.7
  100.7 0.8 copy-done.12
  101.5 0.0 copy-done.8
  101.5 110.7 %shard_map.196 = (bf16[256,1024]{1,0:T(8,128)(2,1)}, f32[256,1024]{1,0:T(8,128)}, bf16[256,1024]{1,0:T(8,128)(2,1)}, f32[32,1024]{1,0:T(8,128)}, f32[8,1024]{1,0:T(8,128)}, /*index=5*/bf16[4,8,256,2176]{3,2,1,0:T(8,128)(2,1)}) custom-call(bf16[256,1152]{1,0:T(8,128)(2,1)} %copy-done.12, bf16[256,1024]{1,0:T(8,128)(2,1)} %cot.3, ...), custom_call_target="tpu_custom_call" | custom-call | flops 16106127360 | bytes 314572800 | tf_op jit(solution)/shard_map/pallas_call | solution.py:814
  212.2 0.0 copy-done
  212.2 1.6 pad_maximum_fusion
  213.8 0.0 all-reduce.4.cloned.1.call-update
  213.8 0.0 all-reduce.6.cloned.1.call-start
  213.9 187.7 %shard_map.197 = (f32[256,1024]{1,0:T(8,128)}, bf16[1024,256]{1,0:T(8,128)(2,1)}, bf16[1024,256]{1,0:T(8,128)(2,1)}, bf16[256,1024]{1,0:T(8,128)(2,1)}, f32[8,12...) custom-call(bf16[256,1024]{1,0:T(8,128)(2,1)} %get-tuple-element.38., ...), custom_call_target="tpu_custom_call", output_to_operand_aliasing={{5}: (13, {})} | custom-call | flops 4294967296 | bytes 314572800 | tf_op jit(solution)/shard_map/pallas_call | solution.py:1378
  401.6 2.0 reshape.45
  403.5 0.0 all-reduce.6.cloned.1.call-update
  403.6 0.0 copy-start.14
  403.6 0.0 copy-start.13
  403.6 0.0 copy-start.15
  403.6 81.7 %shard_map.198 = (f32[4,1024,1024]{2,1,0:T(8,128)}, f32[4,512,1024]{2,1,0:T(8,128)}) custom-call(bf16[32,256,2176]{2,1,0:T(8,128)(2,1)} %bitcast.17, bf16[4,1024,1024]{2,1,0:T(8,128)(2,1)} %refs_0_.1, bf16[4,512,1024]{2,1,0:T(8,128)(2,1)} %refs_1_.1, f32[2,1024,1024]{2,1,0:T(8,128)} %get-tuple-element.54.refs_2_, f32[2,512,1024]{2,1,0:T(8,128)} %get-tuple-element.55.refs_3_), custom_call_target="tpu_custom_call" | custom-call | flops 64424509440 | bytes 314572800 | tf_op jit(solution)/shard_map/pallas_call | solution.py:1027
  485.3 0.0 all-reduce.4.cloned.1.call-done
  485.3 1.4 slice.8
  486.6 1.6 slice_bitcast_fusion
  488.2 2.1 convert_element_type.7
  490.3 2.4 reshape.46
  492.7 2.1 convert_element_type.8
  494.8 0.0 copy-done.14
  494.8 0.8 copy.38
  495.6 0.0 copy-done.13
  495.6 1.0 copy.39
  496.6 0.0 copy-done.15
  496.6 0.6 copy.40
  (7 shorter events, 0.0 us)
Async XLA Ops:
  7.2 478.1 %all-reduce.4.cloned.1.call-start = ((), (), s32[]{:S(2)}) async-start(), calls=%async_computation | async-start | bytes 327680 | tf_op jit(solution)/shard_map/psum | solution.py:1445
  9.7 91.8 %copy-start.8 = (bf16[1024,32]{1,0:T(8,128)(2,1)}, bf16[1024,32]{1,0:T(8,128)(2,1)S(1)}, u32[]{:S(2)}) copy-start(bf16[1024,32]{1,0:T(8,128)(2,1)S(1)} %copy.23.w_router) | copy-start | bytes 196612
  10.9 201.2 %copy-start = (bf16[128,8,2,128]{3,1,2,0:T(8,128)(2,1)}, bf16[128,8,2,128]{3,1,2,0:T(8,128)(2,1)S(1)}, u32[]{:S(2)}) copy-start(bf16[128,8,2,128]{3,1,2,0:T(8,128)(2,1)S(1)} %copy.28) | copy-start | bytes 1572868
  11.0 1.2 copy-start.1
  12.2 1.0 copy-start.2
  13.2 1.0 copy-start.3
  14.3 0.7 copy-start.9
  15.0 1.0 copy-start.10
  16.0 0.7 copy-start.11
  97.5 0.8 copy-start.4
  98.3 0.8 copy-start.5
  99.1 0.8 copy-start.6
  99.9 0.8 copy-start.7
  100.7 0.8 copy-start.12
  213.8 274.4 %all-reduce.6.cloned.1.call-start = ((), (), s32[]{:S(2)}) async-start(), calls=%async_computation.1 | async-start | bytes 3145728 | tf_op jit(solution)/shard_map/psum | solution.py:1454
  403.6 91.2 %copy-start.14 = (bf16[256,1024]{1,0:T(8,128)(2,1)S(1)}, bf16[256,1024]{1,0:T(8,128)(2,1)}, u32[]{:S(2)}) copy-start(bf16[256,1024]{1,0:T(8,128)(2,1)} %get-tuple-element.71) | copy-start | bytes 1572868
  403.6 92.0 %copy-start.13 = (f32[256,1024]{1,0:T(8,128)S(1)}, f32[256,1024]{1,0:T(8,128)}, u32[]{:S(2)}) copy-start(f32[256,1024]{1,0:T(8,128)} %get-tuple-element.72) | copy-start | bytes 3145732
  403.6 93.0 %copy-start.15 = (f32[8,128]{1,0:T(8,128)S(1)}, f32[8,128]{1,0:T(8,128)}, u32[]{:S(2)}) copy-start(f32[8,128]{1,0:T(8,128)} %get-tuple-element.47) | copy-start | bytes 12292
Sparse Core Ops, SparseCore 0:
  213.9 161.0 all-reduce.3
  403.7 58.8 all-reduce.5

commit v3 on v2

--- a/solution.py
+++ b/solution.py
@@ -114,6 +114,8 @@
         self.e, self.z, self.own, self.view = e, z, own, view
         self.chip, self.core, self.chips = e // 2, lax.rem(e, 2), n_exp // 2
         self.push_s, self.push_r, self.pass_s, self.pass_r = sems
+        self.square = self.chips == 4
+        self.pushes = 3 if self.square else self.chips
 
     def mine(self, k):
         return 2 * (self.chip ^ k) + self.core
@@ -121,71 +123,66 @@
     def other(self, k):
         return 2 * (self.chip ^ k) + 1 - self.core
 
-    def push(self, k):
+    def copy(self, src, dst, sems, at, device):
         return pltpu.make_async_remote_copy(
-            src_ref=self.own,
-            dst_ref=self.view(self.e),
-            send_sem=self.push_s(k),
-            recv_sem=self.push_r(k),
-            device_id=(self.mine(k), self.z),
+            src_ref=src,
+            dst_ref=dst,
+            send_sem=sems[0](at),
+            recv_sem=sems[1](at),
+            device_id=(device, self.z),
             device_id_type=MESH,
         )
 
-    def pushed(self, k):
-        there = self.view(self.mine(k))
-        return pltpu.make_async_remote_copy(
-            src_ref=there,
-            dst_ref=there,
-            send_sem=self.push_s(k),
-            recv_sem=self.push_r(k),
-            device_id=(self.mine(k), self.z),
-            device_id_type=MESH,
-        )
-
-    def hand(self, k, first=False):
-        there = self.view(self.mine(k))
-        return pltpu.make_async_remote_copy(
-            src_ref=self.own if first else there,
-            dst_ref=there,
-            send_sem=self.pass_s(k),
-            recv_sem=self.pass_r(k),
-            device_id=(self.other(0), self.z),
-            device_id_type=MESH,
-        )
-
-    def handed(self, k):
-        there = self.view(self.other(k))
-        return pltpu.make_async_remote_copy(
-            src_ref=there,
-            dst_ref=there,
-            send_sem=self.pass_s(k),
-            recv_sem=self.pass_r(k),
-            device_id=(self.other(0), self.z),
-            device_id_type=MESH,
-        )
+    def push(self, k, landed=False):
+        src = self.view(self.mine(k)) if landed else self.own
+        dst = src if landed else self.view(self.e)
+        return self.copy(src, dst, (self.push_s, self.push_r), k, self.mine(k))
+
+    def hand(self, k, first=False, landed=False):
+        there = self.view(self.other(k) if landed else self.mine(k))
+        src = self.own if first else there
+        return self.copy(src, there, (self.pass_s, self.pass_r), k, self.other(0))
+
+    def across(self, half, landed=False):
+        whole = self.view(self.mine(3 if landed else 1 + half))
+        rows = whole.shape[0] // 2
+        there = whole.at[pl.ds(half * rows, rows)]
+        sems = (self.push_s, self.push_r)
+        return self.copy(there, there, sems, 3 * half, self.mine(2 - half))
 
     def begin(self):
-        each(self.chips, lambda k: self.push(k).start(), 1)
+        each(self.pushes, lambda k: self.push(k).start(), 1)
         self.hand(0, True).start()
 
-    def relay(self):
+    def turn(self):
         def one(k):
-            self.pushed(k).wait_recv()
+            self.push(k, True).wait_recv()
             self.hand(k).start()
 
-        each(self.chips, one, 1)
-
-    def arrive(self):
-        each(self.chips, lambda k: self.handed(k).wait_recv())
+        if self.square:
+            for half in range(2):
+                self.push(1 + half, True).wait_recv()
+                self.across(half).start()
+                self.hand(1 + half).start()
+        else:
+            each(self.chips, one, 1)
+
+    def turn_across(self):
+        if self.square:
+            for half in range(2):
+                self.across(half, True).wait_recv()
+            self.hand(3).start()
+
+    def arrive(self, k):
+        self.hand(k, landed=True).wait_recv()
 
     def drain(self):
         self.hand(0, True).wait_send()
-
-        def one(k):
-            self.push(k).wait_send()
-            self.hand(k).wait_send()
-
-        each(self.chips, one, 1)
+        each(self.pushes, lambda k: self.push(k).wait_send(), 1)
+        each(self.chips, lambda k: self.hand(k).wait_send(), 1)
+        if self.square:
+            for half in range(2):
+                self.across(half).wait_send()
 
 
 class LineGather:
@@ -422,7 +419,8 @@
 
     scatter = LineScatter(e, z, n, sent, landed, (rs_s, rs_r), part)
     each(n - 1, scatter.step)
-    plane.relay()
+    plane.turn()
+    plane.turn_across()
     scatter.finish(hidden)
     hid = tokens[...].astype(F32) + hidden[...]
     hidden[...] = hid
@@ -445,7 +443,7 @@
     pad = jnp.zeros((rows, LANES - 3 * experts), BF)
     ext[:, D:] = jnp.concatenate([high, low_part, mask, pad], axis=1)
     keep.wait()
-    plane.arrive()
+    each(n_exp // 2, plane.arrive)
     plane.drain()
     line.drain()
     scatter.drain()
@@ -612,7 +610,15 @@
         [lambda k, s=s: s.at[k] for s in (ag_s, ag_r, fw_s, fw_r)],
     )
     there, other = plane.mine, plane.other
-    plane.begin()
+
+    def place(p):
+        if chips != 4:
+            return p
+        return jnp.where(p == 0, 0, jnp.where(p == 1, 3, p - 1))
+
+    pair = GROUP // 2
+    each(pair, lambda p: plane.push(place(p)).start(), 1)
+    plane.hand(0, True).start()
 
     def up_column(k, landed=False):
         return pltpu.make_async_remote_copy(
@@ -641,31 +647,23 @@
             pltpu.make_async_copy(cg.at[b], all_rows.at[z, b, :, pl.ds(XW, D)], out_sem.at[1, b]),
         )
 
-    gather(e)
-    plane.relay()
-    each(chips, lambda k: gather(there(k)), 1)
-    plane.arrive()
-    each(chips, lambda k: gather(other(k)))
-
-    def start_save(b):
-        for copy in save(b):
-            copy.start()
-
-    def end_save(b):
-        for copy in save(b):
-            copy.wait()
-
-    each(n_exp, start_save)
-    for load in loads[:2]:
-        load.wait()
-
-    groups = n_exp // GROUP
-
-    def expert_step(step, carry):
-        k = step // groups
-        b0 = lax.rem(step, groups) * GROUP
+    def save(b):
+        return (
+            pltpu.make_async_copy(
+                xg.at[b], all_rows.at[z, b, :, pl.ds(0, XW)], out_sem.at[0, b]
+            ),
+            pltpu.make_async_copy(
+                cg.at[b], all_rows.at[z, b, :, pl.ds(XW, D)], out_sem.at[1, b]
+            ),
+        )
+
+    def members(g):
+        return [f(place(pair * g + i)) for i in range(pair) for f in (there, other)]
+
+    def expert_step(g, k):
+        blocks = members(g)
         at = pl.ds(pl.multiple_of(k * slots, slots), slots)
-        wide = jnp.concatenate([xs[b0 + i, at] for i in range(GROUP)], axis=0)
+        wide = jnp.concatenate([xs[b, at] for b in blocks], axis=0)
         gate_value = own_gate(wide[:, D:], first + k)
         units = mm(wide[:, :D], wgu[k])
         gate, up = units[:, :FF], units[:, FF:]
@@ -673,7 +671,7 @@
         silu = gate * sig
         active = (silu * up).astype(BF)
         made = mm(active, wd[k]).astype(BF).astype(F32)
-        upstream = jnp.concatenate([cs[b0 + i, at] for i in range(GROUP)], axis=0).astype(F32)
+        upstream = jnp.concatenate([cs[b, at] for b in blocks], axis=0).astype(F32)
         dgate_value = jnp.sum(upstream * made, axis=-1, keepdims=True)
         share = (gate_value * made).astype(BF)
         dmade = (gate_value * upstream).astype(BF)
@@ -685,17 +683,11 @@
         high = dgate_value.astype(BF).astype(F32)
         packed = jnp.where(lane == first + k, high, 0.0)
         packed = jnp.where(lane == 32 + first + k, dgate_value - high, packed).astype(BF)
-        for i in range(GROUP):
+        for i, b in enumerate(blocks):
             here = slice(i * slots, (i + 1) * slots)
-            xs[b0 + i, at, :D] = share[here]
-            xs[b0 + i, at, D:] = packed[here]
-            cs[b0 + i, at] = dx[here]
-        return carry
-
-    lax.fori_loop(0, local_experts * groups, expert_step, 0)
-
-    each(n_exp, end_save)
-    plane.drain()
+            xs[b, at, :D] = share[here]
+            xs[b, at, D:] = packed[here]
+            cs[b, at] = dx[here]
 
     def core_copy(k, src, dst, s, r):
         return pltpu.make_async_remote_copy(
@@ -721,34 +713,92 @@
         s = sel[b]
         return jnp.concatenate([mm_tn(s, cs[b]), mm_tn(s, xs[b, :, D:])], axis=1)
 
-    def give_grads(i):
-        k = chips - 1 - i
-        xg[other(k)] = grads_of(other(k)).astype(BF)
-        core_copy(k, xg, core_in, core_s, core_r).start()
-
-    def pass_grads(i):
-        k = chips - 1 - i
-        mine = grads_of(there(k))
-        core_copy(k, xg, core_in, core_s, core_r).wait_recv()
-        chip_out[k] = (mine + core_in[k].astype(F32)).astype(BF)
-        chip_copy(k, chip_out, chip_in, chip_s, chip_r).start()
-
-    def give_mix(i):
-        k = chips - 1 - i
-        cg[other(k)] = mm_tn(sel[other(k)], xs[other(k), :, :D]).astype(BF)
-        core_copy(k, cg, mix_core_in, mcore_s, mcore_r).start()
-
-    def pass_mix(i):
-        k = chips - 1 - i
-        mine = mm_tn(sel[there(k)], xs[there(k), :, :D])
-        core_copy(k, cg, mix_core_in, mcore_s, mcore_r).wait_recv()
-        mix_out[k] = (mine + mix_core_in[k].astype(F32)).astype(BF)
-        chip_copy(k, mix_out, mix_in, mchip_s, mchip_r).start()
-
-    each(chips, give_grads)
-    each(chips - 1, pass_grads)
-    each(chips, give_mix)
-    each(chips - 1, pass_mix)
+    def mix_of(b):
+        return mm_tn(sel[b], xs[b, :, :D])
+
+    def pass_on(g, of, kept, came, out, into, sems):
+        core_sems, chip_sems = sems
+
+        def give(i):
+            k = place(pair * g + i)
+            kept[other(k)] = of(other(k)).astype(BF)
+            core_copy(k, kept, came, *core_sems).start()
+
+        def send(i):
+            k = place(pair * g + i)
+
+            @pl.when(k > 0)
+            def _():
+                mine = of(there(k))
+                core_copy(k, kept, came, *core_sems).wait_recv()
+                out[k] = (mine + came[k].astype(F32)).astype(BF)
+                chip_copy(k, out, into, *chip_sems).start()
+
+        each(pair, give)
+        each(pair, send)
+
+    def group_step(g):
+        @pl.when(g == 0)
+        def _():
+            gather(e)
+
+        def turn(i):
+            k = place(pair * g + i)
+
+            @pl.when(k > 0)
+            def _():
+                plane.push(k, True).wait_recv()
+                plane.hand(k).start()
+
+        each(pair, turn)
+
+        @pl.when(g == 0)
+        def _():
+            each(chips, lambda p: plane.push(place(p)).start(), pair)
+
+        def pick(i):
+            k = place(pair * g + i)
+
+            @pl.when(k > 0)
+            def _():
+                gather(there(k))
+
+        def pick_other(i):
+            k = place(pair * g + i)
+            plane.arrive(k)
+            gather(other(k))
+
+        each(pair, pick)
+        each(pair, pick_other)
+
+        def start_save(i):
+            for b in (there(place(pair * g + i)), other(place(pair * g + i))):
+                for copy in save(b):
+                    copy.start()
+
+        def end_save(i):
+            for b in (there(place(pair * g + i)), other(place(pair * g + i))):
+                for copy in save(b):
+                    copy.wait()
+
+        each(pair, start_save)
+
+        @pl.when(g == 0)
+        def _():
+            for load in loads[:2]:
+                load.wait()
+
+        each(local_experts, lambda k: expert_step(g, k))
+        each(pair, end_save)
+        grad_sems = ((core_s, core_r), (chip_s, chip_r))
+        mix_sems = ((mcore_s, mcore_r), (mchip_s, mchip_r))
+        pass_on(g, grads_of, xg, core_in, chip_out, chip_in, grad_sems)
+        pass_on(g, mix_of, cg, mix_core_in, mix_out, mix_in, mix_sems)
+
+    each(n_exp // GROUP, group_step)
+    plane.hand(0, True).wait_send()
+    each(chips, lambda k: plane.push(k).wait_send(), 1)
+    each(chips, lambda k: plane.hand(k).wait_send(), 1)
     total[...] = grads_of(e)
     core_copy(0, xg, core_in, core_s, core_r).wait_recv()
     total[...] += core_in[0].astype(F32)
@@ -775,7 +825,7 @@
     dhidden[...] = back
     dhidden_low[...] = back.astype(BF)
 
-    total[:, :D] = hidden[...] + mm_tn(sel[e], xs[e, :, :D])
+    total[:, :D] = hidden[...] + mix_of(e)
     core_copy(0, cg, mix_core_in, mcore_s, mcore_r).wait_recv()
     total[:, :D] += mix_core_in[0].astype(F32)
 
@@ -847,7 +897,7 @@
         ]
         + [sem((chips,))] * 12,
         compiler_params=pltpu.CompilerParams(
-            collective_id=2, has_side_effects=True, vmem_limit_bytes=62 * MIB
+            collective_id=2, has_side_effects=True, vmem_limit_bytes=63 * MIB
         ),
         cost_estimate=pl.CostEstimate(
             flops=2 * taken * 6 * D * FF, bytes_accessed=300 * MIB, transcendentals=0
@@ -1227,14 +1277,12 @@
     events = 2 * n + 2
     steps = n * (1 + early) if early else 0
 
-    def relay(i):
-        each(n_exp // 2, lambda k: plane(i).pushed(k).wait_recv(), 1)
+    def turn(i):
+        plane(i).turn()
 
         @pl.when(i + 1 < n)
         def _():
             plane(i + 1).begin()
-
-        each(n_exp // 2, lambda k: plane(i).hand(k).start(), 1)
 
     if early:
         slots = kept_x.shape[1] // n_exp
@@ -1246,7 +1294,7 @@
         def one_plane(i, carry):
             @pl.when(i > 0)
             def _():
-                plane(i).arrive()
+                each(n_exp // 2, plane(i).arrive)
 
             def load(b):
                 return pltpu.make_async_copy(
@@ -1280,11 +1328,15 @@
                 acc_down[k] += mm_tn(kept_active[...], kept_c[k])
                 event(i * (1 + early) + 1 + k)
 
+                @pl.when((k == 0) & (i + 1 < n))
+                def _():
+                    turn(i + 1)
+
             each(early, expert)
 
             @pl.when(i + 1 < n)
             def _():
-                relay(i + 1)
+                plane(i + 1).turn_across()
 
             return carry
 
@@ -1301,11 +1353,12 @@
             copy.wait()
     else:
 
-        def one_relay(i):
-            relay(i)
-
-        each(n, one_relay, 1)
-        each(n, lambda i: plane(i).arrive(), 1)
+        def one_plane(i):
+            turn(i)
+            plane(i).turn_across()
+
+        each(n, one_plane, 1)
+        each(n, lambda i: each(n_exp // 2, plane(i).arrive), 1)
     each(n_exp, lambda k: plane_norm(k, True).wait_recv(), 1)
     total = plane_norms[0]
     for k in range(1, n_exp):

time: 513 us -> 477 us (0.930); the launches traced: 504 us -> 474 us
  Pallas kernels: 461 us -> 430 us
    pallas_call x1, Pallas kernels: 188 us -> 165 us  [backward(): pl.pallas_call(functools.partial(backward_kernel, n, n_exp, early, local_...]
    pallas_call x1, Pallas kernels: 111 us -> 100 us  [own_experts(): pl.pallas_call(functools.partial(own_experts_kernel, n, n_exp, local_expe...]
  transfers between devices with their start and end apart: 2 -> 2, of which waited for: 0 -> 0; matrix products, arithmetic and copies ran while one was open for 1% -> 1% of each run, Pallas kernels for 53% -> 52%
where the time goes in v3:
time: 477 us; the launch traced here: 474 us
  Pallas kernels  430 us (90%)
  local copies, waits for them, and re-layouts  20 us (4%)
  between operations  15.1 us (3%)
  other arithmetic  8.18 us (2%)
    pallas_call x1, Pallas kernels, backward(): pl.pallas_call(functools.partial(backward_kernel, n, n_exp, early, local_...  165 us
    pallas_call x1, Pallas kernels, own_experts(): pl.pallas_call(functools.partial(own_experts_kernel, n, n_exp, local_expe...  100 us
    pallas_call x1, Pallas kernels, attention_forward(): pl.pallas_call(functools.partial(attention_forward_kernel, n, n_exp), out...  83.7 us
    pallas_call x1, Pallas kernels, expert_grads(): pl.pallas_call(functools.partial(expert_grads_kernel, blocks, groups, ear...  81.4 us
    unnamed x38, local copies, waits for them, and re-layouts  15.1 us
  transfers between devices with their start and end apart: 2, of which 0 were waited for; matrix products, arithmetic and copies ran while one was open for 1% of the time, Pallas kernels for 52%

profile of v3, /device:TPU:8, one launch (start us, length us, event | category | flops | bytes accessed | tf_op | source)
XLA Modules:
  0.0 473.6 jit_solution(8134869798279216306)
XLA Ops:
  7.2 0.0 all-reduce.4.cloned.1.call-start
  7.9 0.8 copy.24.routes
  8.7 1.0 copy.23.w_router
  9.7 0.0 copy-start.8
  9.7 1.2 copy.28
  10.9 0.0 copy-start
  11.0 0.0 copy-start.1
  11.0 1.2 copy-done.1
  12.2 0.0 copy-start.2
  12.2 1.0 copy-done.2
  13.2 0.0 copy-start.3
  13.2 1.0 copy-done.3
  14.3 0.0 copy-start.9
  14.3 0.7 copy-done.9
  15.0 1.0 copy-done.10
  16.0 0.7 copy-done.11
  16.7 83.7 %shard_map.195 = (f32[256,1024]{1,0:T(8,128)}, bf16[256,1152]{1,0:T(8,128)(2,1)S(1)}, bf16[8,256,1024]{2,1,0:T(8,128)(2,1)}, bf16[1024,1024]{1,0:T(8,128)(2,1)},...) custom-call(bf16[256,1024]{1,0:T(8,128)(2,1)S(1)} %copy-done.1, ...), custom_call_target="tpu_custom_call" | custom-call | flops 2147483648 | bytes 314572800 | tf_op jit(solution)/shard_map/pallas_call | solution.py:460
  100.4 0.0 copy-start.4
  100.4 0.8 copy-done.4
  101.2 0.8 copy-done.5
  102.0 0.8 copy-done.6
  102.8 0.8 copy-done.7
  103.6 0.8 copy-done.12
  104.4 0.0 copy-done.8
  104.4 100.4 %shard_map.196 = (bf16[256,1024]{1,0:T(8,128)(2,1)}, f32[256,1024]{1,0:T(8,128)}, bf16[256,1024]{1,0:T(8,128)(2,1)}, f32[32,1024]{1,0:T(8,128)}, f32[8,1024]{1,0:T(8,128)}, /*index=5*/bf16[4,8,256,2176]{3,2,1,0:T(8,128)(2,1)}) custom-call(bf16[256,1152]{1,0:T(8,128)(2,1)} %copy-done.12, bf16[256,1024]{1,0:T(8,128)(2,1)} %cot.3, ...), custom_call_target="tpu_custom_call" | custom-call | flops 16106127360 | bytes 314572800 | tf_op jit(solution)/shard_map/pallas_call | solution.py:864
  204.8 0.0 copy-done
  204.8 1.6 pad_maximum_fusion
  206.5 0.0 all-reduce.4.cloned.1.call-update
  206.5 0.0 all-reduce.6.cloned.1.call-start
  206.5 164.7 %shard_map.197 = (f32[256,1024]{1,0:T(8,128)}, bf16[1024,256]{1,0:T(8,128)(2,1)}, bf16[1024,256]{1,0:T(8,128)(2,1)}, bf16[256,1024]{1,0:T(8,128)(2,1)}, f32[8,12...) custom-call(bf16[256,1024]{1,0:T(8,128)(2,1)} %get-tuple-element.38., ...), custom_call_target="tpu_custom_call", output_to_operand_aliasing={{5}: (13, {})} | custom-call | flops 4294967296 | bytes 314572800 | tf_op jit(solution)/shard_map/pallas_call | solution.py:1431
  371.2 2.0 reshape.45
  373.2 0.0 all-reduce.6.cloned.1.call-update
  373.2 0.0 copy-start.14
  373.2 0.0 copy-start.13
  373.2 0.0 copy-start.15
  373.2 81.4 %shard_map.198 = (f32[4,1024,1024]{2,1,0:T(8,128)}, f32[4,512,1024]{2,1,0:T(8,128)}) custom-call(bf16[32,256,2176]{2,1,0:T(8,128)(2,1)} %bitcast.17, bf16[4,1024,1024]{2,1,0:T(8,128)(2,1)} %refs_0_.1, bf16[4,512,1024]{2,1,0:T(8,128)(2,1)} %refs_1_.1, f32[2,1024,1024]{2,1,0:T(8,128)} %get-tuple-element.54.refs_2_, f32[2,512,1024]{2,1,0:T(8,128)} %get-tuple-element.55.refs_3_), custom_call_target="tpu_custom_call" | custom-call | flops 64424509440 | bytes 314572800 | tf_op jit(solution)/shard_map/pallas_call | solution.py:1077
  454.6 0.0 all-reduce.4.cloned.1.call-done
  454.7 1.4 slice.8
  456.0 1.6 slice_bitcast_fusion
  457.6 2.1 convert_element_type.7
  459.7 2.4 reshape.46
  462.0 2.1 convert_element_type.8
  464.2 0.0 copy-done.14
  464.2 0.8 copy.38
  465.0 0.0 copy-done.13
  465.0 1.0 copy.39
  465.9 0.0 copy-done.15
  465.9 0.6 copy.40
  (7 shorter events, 0.0 us)
Async XLA Ops:
  7.2 447.5 %all-reduce.4.cloned.1.call-start = ((), (), s32[]{:S(2)}) async-start(), calls=%async_computation | async-start | bytes 327680 | tf_op jit(solution)/shard_map/psum | solution.py:1498
  9.7 94.7 %copy-start.8 = (bf16[1024,32]{1,0:T(8,128)(2,1)}, bf16[1024,32]{1,0:T(8,128)(2,1)S(1)}, u32[]{:S(2)}) copy-start(bf16[1024,32]{1,0:T(8,128)(2,1)S(1)} %copy.23.w_router) | copy-start | bytes 196612
  10.9 193.9 %copy-start = (bf16[128,8,2,128]{3,1,2,0:T(8,128)(2,1)}, bf16[128,8,2,128]{3,1,2,0:T(8,128)(2,1)S(1)}, u32[]{:S(2)}) copy-start(bf16[128,8,2,128]{3,1,2,0:T(8,128)(2,1)S(1)} %copy.28) | copy-start | bytes 1572868
  11.0 1.2 copy-start.1
  12.2 1.0 copy-start.2
  13.2 1.0 copy-start.3
  14.3 0.7 copy-start.9
  15.0 1.0 copy-start.10
  16.0 0.7 copy-start.11
  100.4 0.8 copy-start.4
  101.2 0.8 copy-start.5
  102.0 0.8 copy-start.6
  102.8 0.8 copy-start.7
  103.6 0.8 copy-start.12
  206.5 251.1 %all-reduce.6.cloned.1.call-start = ((), (), s32[]{:S(2)}) async-start(), calls=%async_computation.1 | async-start | bytes 3145728 | tf_op jit(solution)/shard_map/psum | solution.py:1507
  373.2 91.0 %copy-start.14 = (bf16[256,1024]{1,0:T(8,128)(2,1)S(1)}, bf16[256,1024]{1,0:T(8,128)(2,1)}, u32[]{:S(2)}) copy-start(bf16[256,1024]{1,0:T(8,128)(2,1)} %get-tuple-element.71) | copy-start | bytes 1572868
  373.2 91.8 %copy-start.13 = (f32[256,1024]{1,0:T(8,128)S(1)}, f32[256,1024]{1,0:T(8,128)}, u32[]{:S(2)}) copy-start(f32[256,1024]{1,0:T(8,128)} %get-tuple-element.72) | copy-start | bytes 3145732
  373.2 92.7 %copy-start.15 = (f32[8,128]{1,0:T(8,128)S(1)}, f32[8,128]{1,0:T(8,128)}, u32[]{:S(2)}) copy-start(f32[8,128]{1,0:T(8,128)} %get-tuple-element.47) | copy-start | bytes 12292
Sparse Core Ops, SparseCore 0:
  206.6 127.2 all-reduce.3
  373.3 61.5 all-reduce.5

commit v4 on v3

--- a/solution.py
+++ b/solution.py
@@ -322,47 +322,43 @@
     return jnp.where(low, pair, zero), jnp.where(low, pltpu.roll(pair, HD, 1), zero)
 
 
-def attention_forward_kernel(
-    n,
-    n_exp,
-    tokens,
-    gain1,
-    w_query,
-    w_pair,
-    w_out,
-    gain2,
-    w_router,
-    routes,
-    prefix,
-    cot,
-    hidden,
-    ext,
-    cot_plane,
-    held,
-    queries,
-    pairs,
-    mixed,
-    totals,
-    sent,
-    landed,
-    ag_rs,
-    ag_rr,
-    ag_ls,
-    ag_lr,
-    rs_s,
-    rs_r,
-    push_s,
-    push_r,
-    pass_s,
-    pass_r,
-    local_sem,
-):
+def attention_forward_kernel(n, n_exp, *refs):
+    tokens_in, w_query_in, w_pair, w_out_in, cot, gain1, gain2, w_router, routes, prefix = refs[:10]
+    hidden_out, ext_out, cot_plane, held_out, queries_out, pairs_out, mixed_out, totals_out = refs[
+        10:18
+    ]
+    tokens, w_query, w_out, hidden, ext, held, queries, pairs, mixed, totals = refs[18:28]
+    sent, landed, ag_rs, ag_rr, ag_ls, ag_lr, rs_s, rs_r = refs[28:36]
+    push_s, push_r, pass_s, pass_r, local_sem, in_sem, out_sem = refs[36:]
     e, z = lax.axis_index("exp"), lax.axis_index("tp")
     rows = tokens.shape[0]
     length = rows * n
     kv_local = pairs.shape[1] // LANES
     low = lax.broadcasted_iota(jnp.int32, (rows, LANES), 1) < HD
+    ins = [
+        pltpu.make_async_copy(a, b, in_sem.at[i])
+        for i, (a, b) in enumerate(
+            ((tokens_in, tokens), (w_query_in, w_query), (w_out_in, w_out))
+        )
+    ]
+    outs = [
+        pltpu.make_async_copy(a, b, out_sem.at[i])
+        for i, (a, b) in enumerate(
+            (
+                (held, held_out),
+                (queries, queries_out),
+                (pairs, pairs_out),
+                (mixed, mixed_out),
+                (totals, totals_out),
+                (hidden, hidden_out),
+                (ext, ext_out),
+            )
+        )
+    ]
+    for copy in ins:
+        copy.start()
     barrier, peers = greet(e, z, n, n_exp, True, True)
+    ins[0].wait()
     scaled, _ = row_scaling(tokens[...].astype(F32))
     held[pl.ds(pl.multiple_of(z * rows, rows), rows)] = (scaled * gain1[...]).astype(BF)
 
@@ -384,8 +380,8 @@
         [lambda k, s=s: s.at[k] for s in (push_s, push_r, pass_s, pass_r)],
     )
     plane.begin()
-    keep = pltpu.make_async_copy(cot, cot_plane.at[e], local_sem)
-    keep.start()
+    ins[1].wait()
+    ins[2].wait()
     line.work(0, project)
 
     def gather_step(step):
@@ -393,6 +389,8 @@
         line.work(step, project)
 
     each(n, gather_step, 1)
+    for copy in outs[:3]:
+        copy.start()
 
     def part(d):
         at = pl.ds(pl.multiple_of(d * rows, rows), rows)
@@ -422,13 +420,15 @@
     plane.turn()
     plane.turn_across()
     scatter.finish(hidden)
+    for copy in outs[3:5]:
+        copy.start()
     hid = tokens[...].astype(F32) + hidden[...]
     hidden[...] = hid
     scaled2, _ = row_scaling(hid)
     normed2 = (scaled2 * gain2[...]).astype(BF)
     ext[:, :D] = normed2
-    experts = w_router.shape[1]
-    logits = mm(normed2, w_router[...])
+    experts = w_router.shape[0]
+    logits = mm_nt(normed2, w_router[...])
     lane = lax.broadcasted_iota(jnp.int32, (rows, experts), 1)
     chosen = lane == routes[:, 0:1]
     for k in range(1, routes.shape[1]):
@@ -442,36 +442,49 @@
     mask = jnp.where(chosen, 1.0, 0.0).astype(BF)
     pad = jnp.zeros((rows, LANES - 3 * experts), BF)
     ext[:, D:] = jnp.concatenate([high, low_part, mask, pad], axis=1)
-    keep.wait()
+    for copy in outs[5:]:
+        copy.start()
     each(n_exp // 2, plane.arrive)
     plane.drain()
     line.drain()
     scatter.drain()
-
-
-def attention_forward(
-    n, n_exp, tokens, gain1, w_query, w_pair, w_out, gain2, w_router, routes, prefix, cot
-):
+    for copy in outs:
+        copy.wait()
+
+
+def attention_forward(n, n_exp, in_hbm, in_vmem, prefix):
+    tokens, w_query, w_pair, w_out, cot = in_hbm
     rows = tokens.shape[0]
     length = rows * n
     qw, pw = w_query.shape[1], w_pair.shape[1]
     v = pl.BlockSpec(memory_space=VMEM)
+    hbm = pl.BlockSpec(memory_space=pl.ANY)
     sem = pltpu.SemaphoreType.DMA
+    made = (
+        ((rows, D), F32),
+        ((rows, XW), BF),
+        ((length, D), BF),
+        ((length, qw), BF),
+        ((length, pw), BF),
+        ((length, qw), BF),
+        ((length, LANES), F32),
+    )
+    shapes = [jax.ShapeDtypeStruct(*m) for m in made]
+    shapes.insert(2, jax.ShapeDtypeStruct((n_exp, rows, D), BF))
     return pl.pallas_call(
         functools.partial(attention_forward_kernel, n, n_exp),
-        out_shape=(
-            jax.ShapeDtypeStruct((rows, D), F32),
-            jax.ShapeDtypeStruct((rows, XW), BF),
-            jax.ShapeDtypeStruct((n_exp, rows, D), BF),
-            jax.ShapeDtypeStruct((length, D), BF),
-            jax.ShapeDtypeStruct((length, qw), BF),
-            jax.ShapeDtypeStruct((length, pw), BF),
-            jax.ShapeDtypeStruct((length, qw), BF),
-            jax.ShapeDtypeStruct((length, LANES), F32),
-        ),
-        in_specs=[v] * 8 + [pl.BlockSpec(memory_space=pltpu.SMEM), v],
-        out_specs=[v, v, pl.BlockSpec(memory_space=pl.ANY)] + [v] * 5,
+        out_shape=tuple(shapes),
+        in_specs=[hbm, hbm, v, hbm, hbm]
+        + [v] * len(in_vmem)
+        + [pl.BlockSpec(memory_space=pltpu.SMEM)],
+        out_specs=[hbm] * 8,
         scratch_shapes=[
+            pltpu.VMEM(tokens.shape, BF),
+            pltpu.VMEM(w_query.shape, BF),
+            pltpu.VMEM(w_out.shape, BF),
+        ]
+        + [pltpu.VMEM(*m) for m in made]
+        + [
             pltpu.VMEM((n, rows, D), BF),
             pltpu.VMEM((n + 1, rows, D), BF),
             sem((n,)),
@@ -482,14 +495,14 @@
             sem((n + 1,)),
         ]
         + [sem((n_exp // 2,))] * 4
-        + [sem],
+        + [sem, sem((3,)), sem((7,))],
         compiler_params=pltpu.CompilerParams(
-            collective_id=1, has_side_effects=True, vmem_limit_bytes=48 * MIB
+            collective_id=1, has_side_effects=True, vmem_limit_bytes=60 * MIB
         ),
         cost_estimate=pl.CostEstimate(
             flops=2 * length * D * 4 * qw, bytes_accessed=300 * MIB, transcendentals=0
         ),
-    )(tokens, gain1, w_query, w_pair, w_out, gain2, w_router, routes, prefix, cot)
+    )(*in_hbm, *in_vmem, prefix)
 
 
 def slot_rows(rows, top_k, experts):
@@ -519,6 +532,12 @@
     lane = lax.broadcasted_iota(jnp.int32, extra.shape, 1)
     mine = (lane == expert) | (lane == 32 + expert)
     return jnp.sum(jnp.where(mine, extra.astype(F32), 0.0), axis=-1, keepdims=True)
+
+
+def folded(row):
+    return jnp.concatenate(
+        [row[:, k * LANES : (k + 1) * LANES] for k in range(D // LANES)], axis=0
+    )
 
 
 def sigmoid(v):
@@ -583,16 +602,20 @@
     partner = 2 * chip + 1 - core
     slots = sel.shape[1] // local_experts
     first = e * local_experts
-    experts = w_router.shape[1]
+    experts = w_router.shape[0]
 
     loads = [
         pltpu.make_async_copy(w_gate_up, wgu, w_sem.at[0]),
         pltpu.make_async_copy(w_down, wd, w_sem.at[1]),
     ]
-    for b in range(n_exp):
-        loads.append(pltpu.make_async_copy(cot_plane.at[b], cg.at[b], cot_sem.at[b]))
     for load in loads:
         load.start()
+
+    def cot_load(k):
+        return pltpu.make_async_copy(cot_plane.at[e ^ k], cg.at[e ^ k], cot_sem.at[k])
+
+    each(n_exp, lambda k: cot_load(k).start(), 1)
+    cg[e] = cot[...]
 
     barrier, peers = greet(e, z, n, n_exp, False, True)
     for k in range(1, n):
@@ -630,10 +653,30 @@
             device_id_type=MESH,
         )
 
+    relayed = n == 4
+    inner = (z == 1) | (z == 2)
+    far = n - 1
+
+    def column_on():
+        at = all_rows.at[z ^ 2, e]
+        return pltpu.make_async_remote_copy(
+            src_ref=at,
+            dst_ref=at,
+            send_sem=column_s.at[0],
+            recv_sem=column_r.at[far],
+            device_id=(e, z ^ 1),
+            device_id_type=MESH,
+        )
+
     for k in range(1, n):
-        up_column(k).start()
-    for load in loads[2:]:
-        load.wait()
+        if k == far and relayed:
+
+            @pl.when(inner)
+            def _():
+                up_column(far).start()
+        else:
+            up_column(k).start()
+    each(n_exp, lambda k: cot_load(k).wait(), 1)
 
     def gather(b):
         s = selection(xg[b, :, D:], first, local_experts, slots)
@@ -788,7 +831,20 @@
             for load in loads[:2]:
                 load.wait()
 
-        each(local_experts, lambda k: expert_step(g, k))
+        def column_step(k):
+            if relayed:
+
+                @pl.when((g == 1) & (k == local_experts // 2))
+                def _():
+                    up_column(2, True).wait_recv()
+
+                    @pl.when(inner)
+                    def _():
+                        column_on().start()
+
+            expert_step(g, k)
+
+        each(local_experts, column_step)
         each(pair, end_save)
         grad_sems = ((core_s, core_r), (chip_s, chip_r))
         mix_sems = ((mcore_s, mcore_r), (mchip_s, mchip_r))
@@ -815,12 +871,12 @@
     dlogits = gates * (dgates - jnp.sum(gates * dgates, axis=-1, keepdims=True))
     dlogits = dlogits.astype(BF)
     normed2 = ext[:, :D]
-    router_part[...] = mm_tn(dlogits, normed2)
-    dnormed2 = total[:, :D] + mm_nt(dlogits, w_router[...])
+    routed = mm_tn(dlogits, normed2)
+    for k in range(D // LANES):
+        router_part[k * experts : (k + 1) * experts] = routed[:, k * LANES : (k + 1) * LANES]
+    dnormed2 = total[:, :D] + mm(dlogits, w_router[...])
     scaled2, inverse2 = row_scaling(hidden[...])
-    norm2_part[...] = jnp.broadcast_to(
-        jnp.sum(dnormed2 * scaled2, axis=0, keepdims=True), norm2_part.shape
-    )
+    norm2_part[...] = folded(jnp.sum(dnormed2 * scaled2, axis=0, keepdims=True))
     back = cot[...].astype(F32) + norm_backward(dnormed2, scaled2, inverse2, gain2[...])
     dhidden[...] = back
     dhidden_low[...] = back.astype(BF)
@@ -848,14 +904,22 @@
     each(chips, sent_to_core)
     each(chips - 1, sent_to_chip)
     for k in range(1, n):
-        up_column(k, True).wait_recv()
-        up_column(k).wait_send()
+        if not (relayed and k == 2):
+            up_column(k, True).wait_recv()
+        if relayed and k == far:
+
+            @pl.when(inner)
+            def _():
+                up_column(far).wait_send()
+                column_on().wait_send()
+        else:
+            up_column(k).wait_send()
 
 
 def own_experts(n, n_exp, ext, cot, cot_plane, w_gate_up, w_down, hidden, w_router, gain2, slots):
     rows = ext.shape[0]
     local_experts = w_gate_up.shape[0]
-    experts = w_router.shape[1]
+    experts = w_router.shape[0]
     chips = n_exp // 2
     v = pl.BlockSpec(memory_space=VMEM)
     hbm = pl.BlockSpec(memory_space=pl.ANY)
@@ -867,8 +931,8 @@
             jax.ShapeDtypeStruct((rows, D), BF),
             jax.ShapeDtypeStruct((rows, D), F32),
             jax.ShapeDtypeStruct((rows, D), BF),
-            jax.ShapeDtypeStruct((experts, D), F32),
-            jax.ShapeDtypeStruct((8, D), F32),
+            jax.ShapeDtypeStruct((experts * (D // LANES), LANES), F32),
+            jax.ShapeDtypeStruct((D // LANES, LANES), F32),
             jax.ShapeDtypeStruct((n, n_exp, rows, RW), BF),
         ),
         in_specs=[v, v, hbm, hbm, hbm, v, v, v],
@@ -929,8 +993,11 @@
     refs = list(refs)
     w_gate_up, w_down = refs.pop(0), refs.pop(0)
     done = (refs.pop(0), refs.pop(0)) if early else None
-    gate_up_grad, down_grad, rbuf, kept_x, kept_dy, kept_active, kept_dunits = refs[:7]
-    acc_up, acc_down, sems, out_sems, copy_sems = refs[7:]
+    summed, routed, got, layer, gate_up_grad, down_grad = refs[:6]
+    query_grad, pair_grad, out_grad, router_grad, input_grad, layer_out = refs[6:12]
+    refs = refs[12:]
+    rbuf, kept_x, kept_dy, kept_active, kept_dunits = refs[:5]
+    acc_up, acc_down, sems, out_sems, copy_sems = refs[5:]
     slots = kept_x.shape[0] // blocks
     chunks = blocks // GROUP
     size = GROUP * slots
@@ -1050,6 +1117,19 @@
 
     lax.fori_loop(0, FF // tile, down_tile, 0)
 
+    @pl.when(opening)
+    def _():
+        qw, pw = query_grad.shape[1], LANES
+        query_grad[...] = summed[:, :qw].astype(F32)
+        for j in range(pair_grad.shape[1]):
+            pair_grad[:, j] = summed[:, qw + j * pw : qw + (j + 1) * pw].astype(F32)
+        out_grad[...] = summed[:, qw + pair_grad.shape[1] * pw :].astype(F32).T
+        experts = router_grad.shape[0]
+        for j in range(D // LANES):
+            router_grad[:, j * LANES : (j + 1) * LANES] = routed[j * experts : (j + 1) * experts]
+        input_grad[...] = got[...]
+        layer_out[...] = layer[...]
+
     @pl.when(g == groups - 1)
     def _():
         for copy in store(k):
@@ -1064,7 +1144,7 @@
                 copy.wait()
 
 
-def expert_grads(rows_all, w_gate_up, w_down, done, slots):
+def expert_grads(rows_all, w_gate_up, w_down, done, rest, slots, experts):
     total, rows = rows_all.shape[:2]
     local_experts = w_gate_up.shape[0]
     early = done[0].shape[0] if done else 0
@@ -1073,21 +1153,30 @@
     groups = total // blocks
     kept = blocks * slots
     hbm = pl.BlockSpec(memory_space=pl.ANY)
+    v = pl.BlockSpec(memory_space=VMEM)
     sem = pltpu.SemaphoreType.DMA
+    width = rest[0].shape[1] // 3
     return pl.pallas_call(
         functools.partial(expert_grads_kernel, blocks, groups, early, local_experts),
         grid=(local_experts - early, groups),
         out_shape=(
             jax.ShapeDtypeStruct((local_experts, D, 2 * FF), F32),
             jax.ShapeDtypeStruct((local_experts, FF, D), F32),
+            jax.ShapeDtypeStruct((D, width), F32),
+            jax.ShapeDtypeStruct((D, width // LANES, LANES), F32),
+            jax.ShapeDtypeStruct((width, D), F32),
+            jax.ShapeDtypeStruct((experts, D), F32),
+            jax.ShapeDtypeStruct(rest[2].shape, F32),
+            jax.ShapeDtypeStruct(rest[3].shape, BF),
         ),
         in_specs=[
             hbm,
             pl.BlockSpec((1, D, 2 * FF), lambda k, g: (k + early, 0, 0)),
             pl.BlockSpec((1, FF, D), lambda k, g: (k + early, 0, 0)),
         ]
-        + [hbm] * len(done),
-        out_specs=[hbm, hbm],
+        + [hbm] * len(done)
+        + [v] * 4,
+        out_specs=[hbm, hbm] + [v] * 6,
         scratch_shapes=[
             pltpu.VMEM((2, GROUP, rows, RW), BF),
             pltpu.VMEM((kept, D), BF),
@@ -1106,7 +1195,7 @@
             bytes_accessed=300 * MIB,
             transcendentals=0,
         ),
-    )(rows_all, w_gate_up, w_down, *done)
+    )(rows_all, w_gate_up, w_down, *done, *rest)
 
 
 def backward_kernel(n, n_exp, early, local_experts, *refs):
@@ -1118,15 +1207,17 @@
         return got
 
     dhidden_low, dhidden, tokens, gain1, held, queries, pairs, mixed, totals = take(9)
-    w_query, w_pair, w_out, prefix, _ = take(5)
+    w_query, w_pair, w_out, router_part, norm2_part, prefix, _ = take(7)
     if early:
         w_gate_up, w_down = take(2)
-    input_grad, query_grad, pair_grad, out_grad, norm1, all_rows = take(6)
+    input_grad, summed, router, norms, all_rows = take(5)
     if early:
         gate_up_grad, down_grad = take(2)
     dfull, dqueries, dpairs, dpairs_low, sent, landed, line_norms, plane_norms = take(8)
+    w_sum, w_core, w_chip_out, w_chip_in, r_in, r_line = take(6)
     ag_rs, ag_rr, ag_ls, ag_lr, rs_s, rs_r, push_s, push_r, pass_s, pass_r = take(10)
-    nz_s, nz_r, np_s, np_r = take(4)
+    nz_s, nz_r, np_s, np_r, r1_s, r1_r, r2_s, r2_r, r3_s, r3_r = take(10)
+    wc_s, wc_r, wx_s, wx_r, wg_ps, wg_pr, wg_hs, wg_hr = take(8)
     if early:
         tokens_in, wgu, wd, acc_up, acc_down, kept_x, kept_c, kept_active, kept_dunits = take(9)
         load_s, w_sem, out_sem = take(3)
@@ -1175,6 +1266,82 @@
         )
 
     plane(1).begin()
+
+    part_rows = r_in.shape[1]
+    share = D // n_exp
+
+    def routers(b):
+        return router.at[pl.ds(pl.multiple_of(b * part_rows, part_rows), part_rows)]
+
+    def router_give(k, landed=False):
+        src = router_part.at[pl.ds(pl.multiple_of((e ^ k) * part_rows, part_rows), part_rows)]
+        return pltpu.make_async_remote_copy(
+            src_ref=src,
+            dst_ref=r_in.at[(e ^ k) if landed else e],
+            send_sem=r1_s.at[k],
+            recv_sem=r1_r.at[k],
+            device_id=(e ^ k, z),
+            device_id_type=MESH,
+        )
+
+    def router_line(k, landed=False):
+        return pltpu.make_async_remote_copy(
+            src_ref=r_line.at[z],
+            dst_ref=r_line.at[(z ^ k) if landed else z],
+            send_sem=r2_s.at[k],
+            recv_sem=r2_r.at[k],
+            device_id=(e, z ^ k),
+            device_id_type=MESH,
+        )
+
+    def router_gather(k, landed=False):
+        return pltpu.make_async_remote_copy(
+            src_ref=routers(e),
+            dst_ref=routers((e ^ k) if landed else e),
+            send_sem=r3_s.at[k],
+            recv_sem=r3_r.at[k],
+            device_id=(e ^ k, z),
+            device_id_type=MESH,
+        )
+
+    r_in[e] = router_part[pl.ds(pl.multiple_of(e * part_rows, part_rows), part_rows)]
+    each(n_exp, lambda k: router_give(k).start(), 1)
+
+    def shares(ref, b):
+        return ref.at[pl.ds(pl.multiple_of(b * share, share), share)]
+
+    w_gather = PlaneGather(
+        e,
+        z,
+        n_exp,
+        shares(summed, e),
+        lambda b: shares(summed, b),
+        [lambda k, s=s: s.at[k] for s in (wg_ps, wg_pr, wg_hs, wg_hr)],
+    )
+    mine, other = w_gather.mine, w_gather.other
+
+    def w_give(k):
+        return pltpu.make_async_remote_copy(
+            src_ref=shares(w_sum, other(k)),
+            dst_ref=w_core.at[k],
+            send_sem=wc_s.at[k],
+            recv_sem=wc_r.at[k],
+            device_id=(other(0), z),
+            device_id_type=MESH,
+        )
+
+    def w_cross(k):
+        return pltpu.make_async_remote_copy(
+            src_ref=w_chip_out.at[k],
+            dst_ref=w_chip_in.at[k],
+            send_sem=wx_s.at[k],
+            recv_sem=wx_r.at[k],
+            device_id=(mine(k), z),
+            device_id_type=MESH,
+        )
+
+    def own_share(b):
+        return w_sum[pl.ds(pl.multiple_of(b * share, share), share)].astype(F32)
 
     def attend(d):
         at = pl.ds(pl.multiple_of(d * rows, rows), rows)
@@ -1246,26 +1413,60 @@
         def _():
             scatter.step(t - n)
 
+        @pl.when(t == n)
+        def _():
+            qw, pw = dqueries.shape[1], dpairs_low.shape[1]
+            w_sum[:, :qw] = mm_tn(held[...], dqueries[...]).astype(BF)
+            w_sum[:, qw : qw + pw] = mm_tn(held[...], dpairs_low[...]).astype(BF)
+            w_sum[:, qw + pw :] = mm_tn(dfull[...], mixed[...]).astype(BF)
+            each(n_exp // 2, lambda k: w_give(k).start())
+            each(n_exp, lambda k: router_give(k, True).wait_recv(), 1)
+            total = r_in[0]
+            for k in range(1, n_exp):
+                total = total + r_in[k]
+            r_line[z] = total
+            each(n, lambda k: router_line(k).start(), 1)
+
+        @pl.when(t == n + 1)
+        def _():
+            def cross(k):
+                w_give(k).wait_recv()
+                w_chip_out[k] = (own_share(mine(k)) + w_core[k].astype(F32)).astype(BF)
+                w_cross(k).start()
+
+            each(n_exp // 2, cross, 1)
+
+        @pl.when(t == n + 2)
+        def _():
+            w_give(0).wait_recv()
+            at = pl.ds(pl.multiple_of(e * share, share), share)
+            total = own_share(e) + w_core[0].astype(F32)
+            for k in range(1, n_exp // 2):
+                w_cross(k).wait_recv()
+                total = total + w_chip_in[k].astype(F32)
+            summed[at] = total.astype(BF)
+            w_gather.begin()
+            each(n, lambda k: router_line(k, True).wait_recv(), 1)
+            total = r_line[0]
+            for k in range(1, n):
+                total = total + r_line[k]
+            router[pl.ds(pl.multiple_of(e * part_rows, part_rows), part_rows)] = total
+            each(n_exp, lambda k: router_gather(k).start(), 1)
+
         @pl.when(t == 2 * n - 1)
-        def _():
-            query_grad[...] = mm_tn(held[...], dqueries[...]).astype(BF)
-            pair_grad[...] = mm_tn(held[...], dpairs_low[...]).astype(BF)
-            out_grad[...] = mm_tn(mixed[...], dfull[...]).astype(BF)
-
-        @pl.when(t == 2 * n)
         def _():
             scatter.finish(input_grad)
             dnormed1 = input_grad[...]
             scaled, inverse = row_scaling(tokens[...].astype(F32))
-            total = jnp.sum(dnormed1 * scaled, axis=0, keepdims=True)
-            line_norms[z] = jnp.concatenate(
-                [total[:, k * LANES : (k + 1) * LANES] for k in range(D // LANES)], axis=0
-            )
+            half = D // LANES
+            line_norms[z, :half] = folded(jnp.sum(dnormed1 * scaled, axis=0, keepdims=True))
+            line_norms[z, half:] = norm2_part[...]
             each(n, lambda k: line_norm(k).start(), 1)
             back = dhidden[...] + norm_backward(dnormed1, scaled, inverse, gain1[...])
             input_grad[...] = back
-
-        @pl.when(t == 2 * n + 1)
+            w_gather.turn()
+
+        @pl.when(t == 2 * n)
         def _():
             each(n, lambda k: line_norm(k, True).wait_recv(), 1)
             total = line_norms[0]
@@ -1273,16 +1474,33 @@
                 total = total + line_norms[k]
             plane_norms[e] = total
             each(n_exp, lambda k: plane_norm(k).start(), 1)
-
-    events = 2 * n + 2
+            w_gather.turn_across()
+
+    events = 2 * n + 1
     steps = n * (1 + early) if early else 0
 
-    def turn(i):
-        plane(i).turn()
-
-        @pl.when(i + 1 < n)
-        def _():
-            plane(i + 1).begin()
+    if n == 4 and early == 2:
+        acts = {
+            (0, 1): [("begin", 2)],
+            (0, 2): [("turn", 1)],
+            (0, 4): [("turn_across", 1), ("begin", 3)],
+            (1, 0): [("turn", 2)],
+            (1, 2): [("turn_across", 2), ("turn", 3)],
+            (1, 4): [("turn_across", 3)],
+        }
+    else:
+        acts = {}
+        for i in range(1, n):
+            acts[i - 1, 2] = [("turn", i)] + ([("begin", i + 1)] if i + 1 < n else [])
+            acts[i - 1, 2 * early] = acts.get((i - 1, 2 * early), []) + [("turn_across", i)]
+
+    def act(i, point):
+        for (step, at), moves in acts.items():
+
+            @pl.when((i == step) & (point == at))
+            def _():
+                for name, which in moves:
+                    getattr(plane(which), name)()
 
     if early:
         slots = kept_x.shape[1] // n_exp
@@ -1297,24 +1515,31 @@
                 each(n_exp // 2, plane(i).arrive)
 
             def load(b):
+                slot = lax.rem(b, GROUP)
                 return pltpu.make_async_copy(
-                    all_rows.at[z ^ i, b], tokens_in.at[b], load_s.at[b]
+                    all_rows.at[z ^ i, b], tokens_in.at[slot], load_s.at[slot]
                 )
 
-            each(n_exp, lambda b: load(b).start())
+            each(GROUP, lambda b: load(b).start())
 
             def pick(b):
                 load(b).wait()
-                s = selection(tokens_in[b, :, D:XW], first, early, slots)
-                got = mm(s, tokens_in[b]).astype(BF)
+                slot = lax.rem(b, GROUP)
+                s = selection(tokens_in[slot, :, D:XW], first, early, slots)
+                got = mm(s, tokens_in[slot]).astype(BF)
                 at = pl.ds(pl.multiple_of(b * slots, slots), slots)
                 for k in range(early):
                     here = got[k * slots : (k + 1) * slots]
                     kept_x[k, at] = here[:, :XW]
                     kept_c[k, at] = here[:, XW:]
 
+                @pl.when(b + GROUP < n_exp)
+                def _():
+                    load(b + GROUP).start()
+
             each(n_exp, pick)
             event(i * (1 + early))
+            act(i, 0)
 
             def expert(k):
                 gate_value = own_gate(kept_x[k, :, D:], first + k)
@@ -1326,17 +1551,11 @@
                 kept_dunits[:, FF:] = made[3]
                 acc_up[k] += mm_tn(kept_x[k, :, :D], kept_dunits[...])
                 acc_down[k] += mm_tn(kept_active[...], kept_c[k])
+                act(i, 2 * k + 1)
                 event(i * (1 + early) + 1 + k)
-
-                @pl.when((k == 0) & (i + 1 < n))
-                def _():
-                    turn(i + 1)
+                act(i, 2 * k + 2)
 
             each(early, expert)
-
-            @pl.when(i + 1 < n)
-            def _():
-                plane(i + 1).turn_across()
 
             return carry
 
@@ -1354,7 +1573,12 @@
     else:
 
         def one_plane(i):
-            turn(i)
+            plane(i).turn()
+
+            @pl.when(i + 1 < n)
+            def _():
+                plane(i + 1).begin()
+
             plane(i).turn_across()
 
         each(n, one_plane, 1)
@@ -1363,10 +1587,18 @@
     total = plane_norms[0]
     for k in range(1, n_exp):
         total = total + plane_norms[k]
-    norm1[...] = total
+    norms[...] = total
+    each(n_exp // 2, w_gather.arrive)
+    each(n_exp, lambda k: router_gather(k, True).wait_recv(), 1)
     each(n, lambda i: plane(i).drain(), 1)
     each(n, lambda k: line_norm(k).wait_send(), 1)
     each(n_exp, lambda k: plane_norm(k).wait_send(), 1)
+    each(n_exp, lambda k: router_give(k).wait_send(), 1)
+    each(n, lambda k: router_line(k).wait_send(), 1)
+    each(n_exp, lambda k: router_gather(k).wait_send(), 1)
+    each(n_exp // 2, lambda k: w_give(k).wait_send())
+    each(n_exp // 2, lambda k: w_cross(k).wait_send(), 1)
+    w_gather.drain()
     line.drain()
     scatter.drain()
 
@@ -1382,12 +1614,15 @@
     hbm = pl.BlockSpec(memory_space=pl.ANY)
     sem = pltpu.SemaphoreType.DMA
     chips = n_exp // 2
+    width = 2 * qw + pw
+    share = D // n_exp
+    folds = D // LANES
+    routed = whole[12].shape[0]
     outs = [
         (jax.ShapeDtypeStruct((rows, D), F32), v),
-        (jax.ShapeDtypeStruct((D, qw), BF), v),
-        (jax.ShapeDtypeStruct((D, pw), BF), v),
-        (jax.ShapeDtypeStruct((qw, D), BF), v),
-        (jax.ShapeDtypeStruct((D // LANES, LANES), F32), v),
+        (jax.ShapeDtypeStruct((D, width), BF), v),
+        (jax.ShapeDtypeStruct((routed, LANES), F32), v),
+        (jax.ShapeDtypeStruct((2 * folds, LANES), F32), v),
         (jax.ShapeDtypeStruct((n, n_exp, rows, RW), BF), hbm),
     ]
     scratch = [
@@ -1397,8 +1632,14 @@
         pltpu.VMEM((length, pw), BF),
         pltpu.VMEM((n, rows, D), BF),
         pltpu.VMEM((n + 1, rows, D), BF),
-        pltpu.VMEM((n, D // LANES, LANES), F32),
-        pltpu.VMEM((n_exp, D // LANES, LANES), F32),
+        pltpu.VMEM((n, 2 * folds, LANES), F32),
+        pltpu.VMEM((n_exp, 2 * folds, LANES), F32),
+        pltpu.VMEM((D, width), BF),
+        pltpu.VMEM((chips, share, width), BF),
+        pltpu.VMEM((chips, share, width), BF),
+        pltpu.VMEM((chips, share, width), BF),
+        pltpu.VMEM((n_exp, routed // n_exp, LANES), F32),
+        pltpu.VMEM((n, routed // n_exp, LANES), F32),
         sem((n,)),
         sem((n,)),
         sem((n,)),
@@ -1407,7 +1648,8 @@
         sem((n + 1,)),
     ]
     scratch += [sem((n, chips))] * 4
-    scratch += [sem((n,)), sem((n,)), sem((n_exp,)), sem((n_exp,))]
+    scratch += [sem((n,))] * 2 + [sem((n_exp,))] * 4 + [sem((n,))] * 2 + [sem((n_exp,))] * 2
+    scratch += [sem((chips,))] * 8
     if early:
         kept = n_exp * slots
         outs += [
@@ -1415,7 +1657,7 @@
             (jax.ShapeDtypeStruct((early, FF, D), F32), hbm),
         ]
         scratch += [
-            pltpu.VMEM((n_exp, rows, RW), BF),
+            pltpu.VMEM((GROUP, rows, RW), BF),
             pltpu.VMEM((early, D, 2 * FF), BF),
             pltpu.VMEM((early, FF, D), BF),
             pltpu.VMEM((early, D, 2 * FF), F32),
@@ -1424,7 +1666,7 @@
             pltpu.VMEM((early, kept, D), BF),
             pltpu.VMEM((kept, FF), BF),
             pltpu.VMEM((kept, 2 * FF), BF),
-            sem((n_exp,)),
+            sem((GROUP,)),
             sem((2,)),
             sem((2,)),
         ]
@@ -1435,7 +1677,7 @@
         + [pl.BlockSpec(memory_space=pltpu.SMEM)]
         + [hbm] * (1 + (2 if early else 0)),
         out_specs=tuple(spec for _, spec in outs),
-        input_output_aliases={len(whole) + 1: 5},
+        input_output_aliases={len(whole) + 1: 4},
         scratch_shapes=scratch,
         compiler_params=pltpu.CompilerParams(
             collective_id=3, has_side_effects=True, vmem_limit_bytes=62 * MIB
@@ -1467,21 +1709,15 @@
     slots = slot_rows(rows, routes.shape[1], experts)
     w_pair = w_key_value.reshape(D, -1)
     gain1, gain2 = norm1_gain.reshape(1, D), norm2_gain.reshape(1, D)
+    router_t = w_router.T
     hidden, ext, cot_plane, held, queries, pairs, mixed, totals = attention_forward(
         n_tp,
         n_exp,
-        tokens,
-        gain1,
-        w_query,
-        w_pair,
-        w_out,
-        gain2,
-        w_router,
-        routes,
+        (tokens, w_query, w_pair, w_out, cotangent),
+        (gain1, gain2, router_t, routes),
         prefix,
-        cotangent,
     )
-    layer_out, dhidden, dhidden_low, router_part, norm2_part, all_rows = own_experts(
+    layer, dhidden, dhidden_low, router_part, norm2_part, all_rows = own_experts(
         n_tp,
         n_exp,
         ext,
@@ -1490,33 +1726,35 @@
         w_gate_up,
         w_down,
         hidden,
-        w_router,
+        router_t,
         gain2,
         slots,
     )
-    small = jnp.concatenate([router_part, norm2_part], axis=0)
-    small = lax.psum(small, ("exp", "tp"))
     whole = (dhidden_low, dhidden, tokens, gain1, held, queries, pairs, mixed, totals)
-    whole += (w_query, w_pair, w_out)
+    whole += (w_query, w_pair, w_out, router_part, norm2_part)
     made = backward(n_tp, n_exp, slots, whole, prefix, all_rows, (w_gate_up, w_down))
-    input_grad, query_grad, pair_grad, out_grad, norm1, all_rows = made[:6]
-    gate_up_grad, down_grad = expert_grads(
-        all_rows.reshape(n_exp * n_tp, rows, RW), w_gate_up, w_down, made[6:], slots
+    got, summed, routed, norms, all_rows = made[:5]
+    gate_up_grad, down_grad, query_grad, pair_grad, out_grad, router_grad, input_grad, layer_out = (
+        expert_grads(
+            all_rows.reshape(n_exp * n_tp, rows, RW),
+            w_gate_up,
+            w_down,
+            made[5:],
+            (summed, routed, got, layer),
+            slots,
+            experts,
+        )
     )
-    query_grad, pair_grad, out_grad = (
-        lax.psum(query_grad, "exp").astype(F32),
-        lax.psum(pair_grad, "exp").astype(F32),
-        lax.psum(out_grad, "exp").astype(F32),
-    )
+    norms = norms.reshape(2, D)
     return (
         layer_out,
         input_grad,
-        norm1.reshape(D),
+        norms[0],
         query_grad,
-        pair_grad.reshape(w_key_value.shape),
+        pair_grad,
         out_grad,
-        small[experts],
-        small[:experts].T,
+        norms[1],
+        router_grad.T,
         gate_up_grad,
         down_grad,
     )

time: 477 us -> 453 us (0.950)
  local copies, waits for them, and re-layouts: 20 us -> 4.01 us
  between operations: 15.1 us -> 1.57 us
  Pallas kernels: 430 us -> 441 us
  other arithmetic: 8.18 us -> 0 us
    pallas_call x1, Pallas kernels: 165 us -> 182 us  [backward(): pl.pallas_call(functools.partial(backward_kernel, n, n_exp, early, local_...]
    pallas_call x1, Pallas kernels: 100 us -> 86.9 us  [own_experts(): pl.pallas_call(functools.partial(own_experts_kernel, n, n_exp, local_expe...]
    unnamed x38 -> x4, local copies, waits for them, and re-layouts: 15.1 us -> 3.41 us
    pallas_call x1, Pallas kernels: 81.4 us -> 87.8 us  [expert_grads(): pl.pallas_call(functools.partial(expert_grads_kernel, blocks, groups, ear...]
  transfers between devices with their start and end apart: 2 -> 0, of which waited for: 0 -> 0; matrix products, arithmetic and copies ran while one was open for 1% -> 0% of each run, Pallas kernels for 52% -> 0%
where the time goes in v4:
time: 453 us; the launch traced here: 447 us
  Pallas kernels  441 us (97%)
    pallas_call x1, Pallas kernels, backward(): pl.pallas_call(functools.partial(backward_kernel, n, n_exp, early, local_...  182 us
    pallas_call x1, Pallas kernels, expert_grads(): pl.pallas_call(functools.partial(expert_grads_kernel, blocks, groups, ear...  87.8 us
    pallas_call x1, Pallas kernels, own_experts(): pl.pallas_call(functools.partial(own_experts_kernel, n, n_exp, local_expe...  86.9 us
    pallas_call x1, Pallas kernels, attention_forward(): pl.pallas_call(functools.partial(attention_forward_kernel, n, n_exp), out...  84.4 us

profile of v4, /device:TPU:8, one launch (start us, length us, event | category | flops | bytes accessed | tf_op | source)
XLA Modules:
  0.0 446.7 jit_solution(17560234601775930128)
XLA Ops:
  1.3 1.5 copy.23.refs_8_
  2.8 1.9 copy.26
  4.7 84.4 %shard_map.195 = (f32[256,1024]{1,0:T(8,128)}, bf16[256,1152]{1,0:T(8,128)(2,1)}, bf16[8,256,1024]{2,1,0:T(8,128)(2,1)}, bf16[1024,1024]{1,0:T(8,128)(2,1)}, bf1...) custom-call(bf16[256,1024]{1,0:T(8,128)(2,1)} %refs_2_.1, ...), custom_call_target="tpu_custom_call" | custom-call | flops 2147483648 | bytes 314572800 | tf_op jit(solution)/shard_map/pallas_call | solution.py:474
  89.1 86.9 %shard_map.196 = (bf16[256,1024]{1,0:T(8,128)(2,1)}, f32[256,1024]{1,0:T(8,128)}, bf16[256,1024]{1,0:T(8,128)(2,1)}, f32[256,128]{1,0:T(8,128)}, f32[8,128]{1,0:T(8,128)}, /*index=5*/bf16[4,8,256,2176]{3,2,1,0:T(8,128)(2,1)}) custom-call(bf16[256,1152]{1,0:T(8,128)(2,1)} %get-tuple-element.39.ext, bf16[256,1024]{1,0:T(8,128)(2,1)} %cot.1, ...), custom_call_target="tpu_custom_call" | custom-call | flops 16106127360 | bytes 314572800 | tf_op jit(solution)/shard_map/pallas_call | solution.py:928
  176.0 182.1 %shard_map.197 = (f32[256,1024]{1,0:T(8,128)}, bf16[1024,768]{1,0:T(8,128)(2,1)}, f32[256,128]{1,0:T(8,128)}, f32[16,128]{1,0:T(8,128)}, bf16[4,8,256,2176]{3,2,...) custom-call(bf16[256,1024]{1,0:T(8,128)(2,1)} %get-tuple-element.42.refs_0_, ...), custom_call_target="tpu_custom_call", output_to_operand_aliasing={{4}: (15, {})} | custom-call | flops 4294967296 | bytes 314572800 | tf_op jit(solution)/shard_map/pallas_call | solution.py:1673
  358.0 0.0 copy-start
  358.1 87.8 %shard_map.198 = (f32[4,1024,1024]{2,1,0:T(8,128)}, f32[4,512,1024]{2,1,0:T(8,128)}, f32[1024,256]{1,0:T(8,128)}, f32[1024,2,128]{2,1,0:T(2,128)}, f32[256,1024]...) custom-call(bf16[32,256,2176]{2,1,0:T(8,128)(2,1)} %bitcast.13, ...), custom_call_target="tpu_custom_call" | custom-call | flops 64424509440 | bytes 314572800 | tf_op jit(solution)/shard_map/pallas_call | solution.py:1159
  445.9 0.0 copy-done
  445.9 0.6 slice_bitcast_fusion
Async XLA Ops:
  358.0 87.8 %copy-start = (f32[16,128]{1,0:T(8,128)S(1)}, f32[16,128]{1,0:T(8,128)}, u32[]{:S(2)}) copy-start(f32[16,128]{1,0:T(8,128)} %get-tuple-element.61) | copy-start | bytes 24580

commit v5 on v4

--- a/solution.py
+++ b/solution.py
@@ -153,6 +153,16 @@
     def begin(self):
         each(self.pushes, lambda k: self.push(k).start(), 1)
         self.hand(0, True).start()
+
+    def begin_part(self, part, parts):
+        rows = self.own.shape[0] // parts
+        at = pl.ds(part * rows, rows)
+        for k in (1, 2):
+            sems = (self.push_s, self.push_r)
+            own, there = self.own.at[at], self.view(self.e).at[at]
+            self.copy(own, there, sems, k, self.mine(k)).start()
+        if part == 0:
+            self.hand(0, True).start()
 
     def turn(self):
         def one(k):
@@ -980,56 +990,78 @@
     return dmade, (silu * up).astype(BF), dgate.astype(BF), (dactive * silu).astype(BF)
 
 
-def expert_grads_kernel(
-    blocks,
-    groups,
-    early,
-    local_experts,
-    rows_all,
-    *refs,
-):
+def expert_grads_kernel(n, n_exp, chunks, groups, early, local_experts, rows_all, *refs):
+    z = lax.axis_index("tp")
     first = lax.axis_index("exp") * local_experts + early
     k, g = pl.program_id(0), pl.program_id(1)
     refs = list(refs)
-    w_gate_up, w_down = refs.pop(0), refs.pop(0)
-    done = (refs.pop(0), refs.pop(0)) if early else None
-    summed, routed, got, layer, gate_up_grad, down_grad = refs[:6]
-    query_grad, pair_grad, out_grad, router_grad, input_grad, layer_out = refs[6:12]
-    refs = refs[12:]
-    rbuf, kept_x, kept_dy, kept_active, kept_dunits = refs[:5]
-    acc_up, acc_down, sems, out_sems, copy_sems = refs[5:]
-    slots = kept_x.shape[0] // blocks
-    chunks = blocks // GROUP
+
+    def take(count):
+        got = refs[:count]
+        del refs[:count]
+        return got
+
+    w_gate_up, w_down = take(2)
+    if early:
+        up_done, down_done = take(2)
+    ends_in = take(4)
+    gate_up_grad, down_grad, pair_grad, query_grad, out_grad, router_grad = take(6)
+    input_grad, layer_out = take(2)
+    rbuf, kept_x, kept_dy, kept_active, kept_dunits, acc_up, acc_down = take(7)
+    summed, routed, got, layer, query_v, out_v, router_v = take(7)
+    sems, out_sems, copy_sems, end_in_sems, end_out_sems = take(5)
+    slots = kept_x.shape[0] // (chunks * GROUP)
     size = GROUP * slots
     last = local_experts - early - 1
+    per_plane = n_exp // GROUP
+    opening = (k == 0) & (g == 0)
 
     def brought():
         return (
-            pltpu.make_async_copy(done[0], acc_up.at[pl.ds(0, early)], copy_sems.at[0]),
-            pltpu.make_async_copy(done[1], acc_down.at[pl.ds(0, early)], copy_sems.at[1]),
+            pltpu.make_async_copy(up_done, acc_up.at[pl.ds(0, early)], copy_sems.at[0]),
+            pltpu.make_async_copy(down_done, acc_down.at[pl.ds(0, early)], copy_sems.at[1]),
         )
 
     def taken():
+        at = pl.ds(0, early)
         return (
-            pltpu.make_async_copy(
-                acc_up.at[pl.ds(0, early)], gate_up_grad.at[pl.ds(0, early)], copy_sems.at[0]
-            ),
-            pltpu.make_async_copy(
-                acc_down.at[pl.ds(0, early)], down_grad.at[pl.ds(0, early)], copy_sems.at[1]
-            ),
-        )
-
-    opening = (k == 0) & (g == 0)
-    if early:
-
-        @pl.when(opening)
-        def _():
+            pltpu.make_async_copy(acc_up.at[at], gate_up_grad.at[at], copy_sems.at[0]),
+            pltpu.make_async_copy(acc_down.at[at], down_grad.at[at], copy_sems.at[1]),
+        )
+
+    def ends_came():
+        return [
+            pltpu.make_async_copy(a, b, end_in_sems.at[i])
+            for i, (a, b) in enumerate(zip(ends_in, (summed, routed, got, layer)))
+        ]
+
+    def ends_go():
+        pairs = (
+            (query_v, query_grad),
+            (out_v, out_grad),
+            (router_v, router_grad),
+            (got, input_grad),
+            (layer, layer_out),
+        )
+        return [
+            pltpu.make_async_copy(a, b, end_out_sems.at[i]) for i, (a, b) in enumerate(pairs)
+        ]
+
+    @pl.when(opening)
+    def _():
+        if early:
             for copy in brought():
                 copy.start()
+        for copy in ends_came():
+            copy.start()
 
     def load(c, slot):
-        at = pl.ds(g * blocks + c * GROUP, GROUP)
-        return pltpu.make_async_copy(rows_all.at[at], rbuf.at[slot], sems.at[slot])
+        at = g * chunks + c
+        plane = z ^ (at // per_plane)
+        b = lax.rem(at, per_plane) * GROUP
+        return pltpu.make_async_copy(
+            rows_all.at[plane, pl.ds(b, GROUP)], rbuf.at[slot], sems.at[slot]
+        )
 
     load(0, 0).start()
 
@@ -1069,12 +1101,25 @@
 
     lax.fori_loop(0, chunks, chunk, 0)
     bank = lax.rem(k, 2)
-    if early:
-
-        @pl.when(opening)
-        def _():
+
+    @pl.when(opening)
+    def _():
+        if early:
             for copy in taken():
                 copy.wait()
+        for copy in ends_came():
+            copy.wait()
+        qw, kv = query_v.shape[1], pair_grad.shape[1]
+        query_v[...] = summed[:, :qw].astype(F32)
+        for j in range(kv):
+            at = qw + j * LANES
+            pair_grad[:, j] = summed[:, at : at + LANES].astype(F32)
+        out_v[...] = summed[:, qw + kv * LANES :].astype(F32).T
+        experts = router_v.shape[0]
+        for j in range(D // LANES):
+            router_v[:, j * LANES : (j + 1) * LANES] = routed[j * experts : (j + 1) * experts]
+        for copy in ends_go():
+            copy.start()
 
     def store(kk):
         b = lax.rem(kk, 2)
@@ -1103,32 +1148,17 @@
 
     tile = 256
 
-    def up_tile(m, carry):
+    def up_tile(m):
         at = pl.ds(pl.multiple_of(m * tile, tile), tile)
         add(acc_up, at, mm_tn(kept_x[:, at], kept_dunits[...]))
-        return carry
-
-    lax.fori_loop(0, D // tile, up_tile, 0)
-
-    def down_tile(m, carry):
+
+    each(D // tile, up_tile)
+
+    def down_tile(m):
         at = pl.ds(pl.multiple_of(m * tile, tile), tile)
         add(acc_down, at, mm_tn(kept_active[:, at], kept_dy[...]))
-        return carry
-
-    lax.fori_loop(0, FF // tile, down_tile, 0)
-
-    @pl.when(opening)
-    def _():
-        qw, pw = query_grad.shape[1], LANES
-        query_grad[...] = summed[:, :qw].astype(F32)
-        for j in range(pair_grad.shape[1]):
-            pair_grad[:, j] = summed[:, qw + j * pw : qw + (j + 1) * pw].astype(F32)
-        out_grad[...] = summed[:, qw + pair_grad.shape[1] * pw :].astype(F32).T
-        experts = router_grad.shape[0]
-        for j in range(D // LANES):
-            router_grad[:, j * LANES : (j + 1) * LANES] = routed[j * experts : (j + 1) * experts]
-        input_grad[...] = got[...]
-        layer_out[...] = layer[...]
+
+    each(FF // tile, down_tile)
 
     @pl.when(g == groups - 1)
     def _():
@@ -1142,28 +1172,33 @@
         if last > 0:
             for copy in store(k - 1):
                 copy.wait()
+        for copy in ends_go():
+            copy.wait()
 
 
 def expert_grads(rows_all, w_gate_up, w_down, done, rest, slots, experts):
-    total, rows = rows_all.shape[:2]
+    n, n_exp, rows = rows_all.shape[:3]
     local_experts = w_gate_up.shape[0]
     early = done[0].shape[0] if done else 0
     assert early <= 2
-    blocks = min(total, 32)
-    groups = total // blocks
-    kept = blocks * slots
+    total = n * n_exp // GROUP
+    chunks = min(total, 8)
+    groups = total // chunks
+    kept = chunks * GROUP * slots
     hbm = pl.BlockSpec(memory_space=pl.ANY)
     v = pl.BlockSpec(memory_space=VMEM)
     sem = pltpu.SemaphoreType.DMA
     width = rest[0].shape[1] // 3
     return pl.pallas_call(
-        functools.partial(expert_grads_kernel, blocks, groups, early, local_experts),
+        functools.partial(
+            expert_grads_kernel, n, n_exp, chunks, groups, early, local_experts
+        ),
         grid=(local_experts - early, groups),
         out_shape=(
             jax.ShapeDtypeStruct((local_experts, D, 2 * FF), F32),
             jax.ShapeDtypeStruct((local_experts, FF, D), F32),
+            jax.ShapeDtypeStruct((D, width // LANES, LANES), F32),
             jax.ShapeDtypeStruct((D, width), F32),
-            jax.ShapeDtypeStruct((D, width // LANES, LANES), F32),
             jax.ShapeDtypeStruct((width, D), F32),
             jax.ShapeDtypeStruct((experts, D), F32),
             jax.ShapeDtypeStruct(rest[2].shape, F32),
@@ -1174,9 +1209,8 @@
             pl.BlockSpec((1, D, 2 * FF), lambda k, g: (k + early, 0, 0)),
             pl.BlockSpec((1, FF, D), lambda k, g: (k + early, 0, 0)),
         ]
-        + [hbm] * len(done)
-        + [v] * 4,
-        out_specs=[hbm, hbm] + [v] * 6,
+        + [hbm] * (len(done) + 4),
+        out_specs=[hbm, hbm, v] + [hbm] * 5,
         scratch_shapes=[
             pltpu.VMEM((2, GROUP, rows, RW), BF),
             pltpu.VMEM((kept, D), BF),
@@ -1185,13 +1219,21 @@
             pltpu.VMEM((kept, 2 * FF), BF),
             pltpu.VMEM((2, D, 2 * FF), F32),
             pltpu.VMEM((2, FF, D), F32),
+        ]
+        + [pltpu.VMEM(a.shape, a.dtype) for a in rest]
+        + [
+            pltpu.VMEM((D, width), F32),
+            pltpu.VMEM((width, D), F32),
+            pltpu.VMEM((experts, D), F32),
             sem((2,)),
             sem((2, 2)),
             sem((2,)),
+            sem((4,)),
+            sem((5,)),
         ],
         compiler_params=pltpu.CompilerParams(vmem_limit_bytes=60 * MIB),
         cost_estimate=pl.CostEstimate(
-            flops=2 * total * slots * local_experts * 6 * D * FF,
+            flops=2 * total * GROUP * slots * local_experts * 6 * D * FF,
             bytes_accessed=300 * MIB,
             transcendentals=0,
         ),
@@ -1250,6 +1292,9 @@
     each(n, greet_line, 1)
     dfull[pl.ds(pl.multiple_of(z * rows, rows), rows)] = dhidden_low[...]
     dpairs[...] = jnp.zeros_like(dpairs)
+    if early:
+        acc_up[...] = jnp.zeros_like(acc_up)
+        acc_down[...] = jnp.zeros_like(acc_down)
     pl.semaphore_wait(barrier, n_exp + n - 2)
 
     line = LineGather(e, z, n, rows, dfull, (ag_rs, ag_rr), (ag_ls, ag_lr))
@@ -1265,7 +1310,11 @@
             [lambda k, s=s: s.at[i, k] for s in (push_s, push_r, pass_s, pass_r)],
         )
 
-    plane(1).begin()
+    if n == 4 and early == 2:
+        plane(1).begin_part(0, 4)
+        plane(1).begin_part(1, 4)
+    else:
+        plane(1).begin()
 
     part_rows = r_in.shape[1]
     share = D // n_exp
@@ -1481,12 +1530,18 @@
 
     if n == 4 and early == 2:
         acts = {
-            (0, 1): [("begin", 2)],
-            (0, 2): [("turn", 1)],
-            (0, 4): [("turn_across", 1), ("begin", 3)],
-            (1, 0): [("turn", 2)],
-            (1, 2): [("turn_across", 2), ("turn", 3)],
-            (1, 4): [("turn_across", 3)],
+            (0, 0): [("begin_part", 1, 2, 4)],
+            (0, 1): [("begin_part", 1, 3, 4)],
+            (0, 2): [("begin_part", 2, 0, 4)],
+            (0, 3): [("turn", 1), ("begin_part", 2, 1, 4)],
+            (0, 4): [("begin_part", 2, 2, 4), ("turn_across", 1)],
+            (1, 0): [("begin_part", 2, 3, 4)],
+            (1, 1): [("begin_part", 3, 0, 4)],
+            (1, 2): [("begin_part", 3, 1, 4)],
+            (1, 3): [("turn", 2), ("begin_part", 3, 2, 4)],
+            (1, 4): [("begin_part", 3, 3, 4), ("turn_across", 2)],
+            (2, 2): [("turn", 3)],
+            (2, 4): [("turn_across", 3)],
         }
     else:
         acts = {}
@@ -1499,13 +1554,11 @@
 
             @pl.when((i == step) & (point == at))
             def _():
-                for name, which in moves:
-                    getattr(plane(which), name)()
+                for name, which, *more in moves:
+                    getattr(plane(which), name)(*more)
 
     if early:
         slots = kept_x.shape[1] // n_exp
-        acc_up[...] = jnp.zeros_like(acc_up)
-        acc_down[...] = jnp.zeros_like(acc_down)
         for copy in weights:
             copy.wait()
 
@@ -1734,9 +1787,9 @@
     whole += (w_query, w_pair, w_out, router_part, norm2_part)
     made = backward(n_tp, n_exp, slots, whole, prefix, all_rows, (w_gate_up, w_down))
     got, summed, routed, norms, all_rows = made[:5]
-    gate_up_grad, down_grad, query_grad, pair_grad, out_grad, router_grad, input_grad, layer_out = (
+    gate_up_grad, down_grad, pair_grad, query_grad, out_grad, router_grad, input_grad, layer_out = (
         expert_grads(
-            all_rows.reshape(n_exp * n_tp, rows, RW),
+            all_rows,
             w_gate_up,
             w_down,
             made[5:],

time: 453 us -> 452 us (level); the launches traced: 447 us -> 452 us
  Pallas kernels: 441 us -> 446 us
    pallas_call x1, Pallas kernels: 182 us -> 191 us  [backward(): pl.pallas_call(functools.partial(backward_kernel, n, n_exp, early, local_...]
where the time goes in v5:
time: 452 us
  Pallas kernels  446 us (99%)
    pallas_call x1, Pallas kernels, backward(): pl.pallas_call(functools.partial(backward_kernel, n, n_exp, early, local_...  191 us
    pallas_call x1, Pallas kernels, own_experts(): pl.pallas_call(functools.partial(own_experts_kernel, n, n_exp, local_expe...  86.9 us
    pallas_call x1, Pallas kernels, attention_forward(): pl.pallas_call(functools.partial(attention_forward_kernel, n, n_exp), out...  84.4 us
    pallas_call x1, Pallas kernels, expert_grads(): pl.pallas_call(functools.partial(expert_grads_kernel, n, n_exp, chunks, g...  83.7 us

profile of v5, /device:TPU:8, one launch (start us, length us, event | category | flops | bytes accessed | tf_op | source)
XLA Modules:
  0.0 451.7 jit_solution(12518686667257626368)
XLA Ops:
  1.3 1.5 copy.23.refs_8_
  2.8 1.9 copy.26
  4.7 84.4 %shard_map.195 = (f32[256,1024]{1,0:T(8,128)}, bf16[256,1152]{1,0:T(8,128)(2,1)}, bf16[8,256,1024]{2,1,0:T(8,128)(2,1)}, bf16[1024,1024]{1,0:T(8,128)(2,1)}, bf1...) custom-call(bf16[256,1024]{1,0:T(8,128)(2,1)} %refs_2_.1, ...), custom_call_target="tpu_custom_call" | custom-call | flops 2147483648 | bytes 314572800 | tf_op jit(solution)/shard_map/pallas_call | solution.py:484
  89.1 86.9 %shard_map.196 = (bf16[256,1024]{1,0:T(8,128)(2,1)}, f32[256,1024]{1,0:T(8,128)}, bf16[256,1024]{1,0:T(8,128)(2,1)}, f32[256,128]{1,0:T(8,128)}, f32[8,128]{1,0:T(8,128)}, /*index=5*/bf16[4,8,256,2176]{3,2,1,0:T(8,128)(2,1)}) custom-call(bf16[256,1152]{1,0:T(8,128)(2,1)} %get-tuple-element.39.ext, bf16[256,1024]{1,0:T(8,128)(2,1)} %cot.1, ...), custom_call_target="tpu_custom_call" | custom-call | flops 16106127360 | bytes 314572800 | tf_op jit(solution)/shard_map/pallas_call | solution.py:938
  176.0 191.1 %shard_map.197 = (f32[256,1024]{1,0:T(8,128)}, bf16[1024,768]{1,0:T(8,128)(2,1)}, f32[256,128]{1,0:T(8,128)}, f32[16,128]{1,0:T(8,128)}, bf16[4,8,256,2176]{3,2,...) custom-call(bf16[256,1024]{1,0:T(8,128)(2,1)} %get-tuple-element.42.refs_0_, ...), custom_call_target="tpu_custom_call", output_to_operand_aliasing={{4}: (15, {})} | custom-call | flops 4294967296 | bytes 314572800 | tf_op jit(solution)/shard_map/pallas_call | solution.py:1726
  367.1 0.0 copy-start
  367.1 83.7 %shard_map.198 = (f32[4,1024,1024]{2,1,0:T(8,128)}, f32[4,512,1024]{2,1,0:T(8,128)}, f32[1024,2,128]{2,1,0:T(2,128)}, f32[1024,256]{1,0:T(8,128)}, f32[256,1024]...) custom-call(bf16[4,8,256,2176]{3,2,1,0:T(8,128)(2,1)} %get-tuple-element.52.rows_all, ...), custom_call_target="tpu_custom_call" | custom-call | flops 64424509440 | bytes 314572800 | tf_op jit(solution)/shard_map/pallas_call | solution.py:1192
  450.8 0.0 copy-done
  450.8 0.6 slice_bitcast_fusion
Async XLA Ops:
  367.1 83.7 %copy-start = (f32[16,128]{1,0:T(8,128)S(1)}, f32[16,128]{1,0:T(8,128)}, u32[]{:S(2)}) copy-start(f32[16,128]{1,0:T(8,128)} %get-tuple-element.61) | copy-start | bytes 24580

commit v6 on v5

--- a/solution.py
+++ b/solution.py
@@ -439,10 +439,14 @@
     ext[:, :D] = normed2
     experts = w_router.shape[0]
     logits = mm_nt(normed2, w_router[...])
-    lane = lax.broadcasted_iota(jnp.int32, (rows, experts), 1)
-    chosen = lane == routes[:, 0:1]
-    for k in range(1, routes.shape[1]):
-        chosen = chosen | (lane == routes[:, k : k + 1])
+    place = lax.broadcasted_iota(jnp.int32, (experts, rows), 0)
+    named = place == routes[0:1, :]
+    for k in range(1, routes.shape[0]):
+        named = named | (place == routes[k : k + 1, :])
+    square = (experts, experts)
+    same = lax.broadcasted_iota(jnp.int32, square, 0) == lax.broadcasted_iota(jnp.int32, square, 1)
+    named = jnp.where(named, 1.0, 0.0).astype(BF)
+    chosen = mm_tn(named, jnp.where(same, 1.0, 0.0).astype(BF)) > 0.5
     logits = jnp.where(chosen, logits, MASKED)
     grown = jnp.exp(logits - jnp.max(logits, axis=-1, keepdims=True))
     grown = jnp.where(chosen, grown, 0.0)
@@ -1530,29 +1534,26 @@
 
     if n == 4 and early == 2:
         acts = {
-            (0, 0): [("begin_part", 1, 2, 4)],
-            (0, 1): [("begin_part", 1, 3, 4)],
-            (0, 2): [("begin_part", 2, 0, 4)],
-            (0, 3): [("turn", 1), ("begin_part", 2, 1, 4)],
-            (0, 4): [("begin_part", 2, 2, 4), ("turn_across", 1)],
-            (1, 0): [("begin_part", 2, 3, 4)],
-            (1, 1): [("begin_part", 3, 0, 4)],
-            (1, 2): [("begin_part", 3, 1, 4)],
-            (1, 3): [("turn", 2), ("begin_part", 3, 2, 4)],
-            (1, 4): [("begin_part", 3, 3, 4), ("turn_across", 2)],
-            (2, 2): [("turn", 3)],
-            (2, 4): [("turn_across", 3)],
+            0: [("begin_part", 1, 2, 4), ("begin_part", 1, 3, 4)],
+            1: [("begin_part", 2, 0, 4), ("turn", 1), ("begin_part", 2, 1, 4)],
+            2: [("begin_part", 2, 2, 4), ("turn_across", 1)],
+            3: [("begin_part", 2, 3, 4), ("begin_part", 3, 0, 4)],
+            4: [("begin_part", 3, 1, 4), ("turn", 2), ("begin_part", 3, 2, 4)],
+            5: [("begin_part", 3, 3, 4), ("turn_across", 2)],
+            7: [("turn", 3)],
+            8: [("turn_across", 3)],
         }
     else:
         acts = {}
         for i in range(1, n):
-            acts[i - 1, 2] = [("turn", i)] + ([("begin", i + 1)] if i + 1 < n else [])
-            acts[i - 1, 2 * early] = acts.get((i - 1, 2 * early), []) + [("turn_across", i)]
-
-    def act(i, point):
-        for (step, at), moves in acts.items():
-
-            @pl.when((i == step) & (point == at))
+            at = (i - 1) * (1 + early) + 1
+            acts[at] = [("turn", i)] + ([("begin", i + 1)] if i + 1 < n else [])
+            acts[at + early - 1] = acts.get(at + early - 1, []) + [("turn_across", i)]
+
+    def act(t):
+        for at, moves in acts.items():
+
+            @pl.when(t == at)
             def _():
                 for name, which, *more in moves:
                     getattr(plane(which), name)(*more)
@@ -1562,7 +1563,7 @@
         for copy in weights:
             copy.wait()
 
-        def one_plane(i, carry):
+        def pick_plane(i):
             @pl.when(i > 0)
             def _():
                 each(n_exp // 2, plane(i).arrive)
@@ -1591,35 +1592,41 @@
                     load(b + GROUP).start()
 
             each(n_exp, pick)
-            event(i * (1 + early))
-            act(i, 0)
-
-            def expert(k):
-                gate_value = own_gate(kept_x[k, :, D:], first + k)
-                x = kept_x[k, :, :D]
-                made = expert_middle(x, gate_value, kept_c[k], wgu[k], wd[k])
-                kept_c[k] = made[0]
-                kept_active[...] = made[1]
-                kept_dunits[:, :FF] = made[2]
-                kept_dunits[:, FF:] = made[3]
-                acc_up[k] += mm_tn(kept_x[k, :, :D], kept_dunits[...])
-                acc_down[k] += mm_tn(kept_active[...], kept_c[k])
-                act(i, 2 * k + 1)
-                event(i * (1 + early) + 1 + k)
-                act(i, 2 * k + 2)
-
-            each(early, expert)
-
-            return carry
-
-        lax.fori_loop(0, n, one_plane, 0)
+
+        def expert(k):
+            gate_value = own_gate(kept_x[k, :, D:], first + k)
+            x = kept_x[k, :, :D]
+            made = expert_middle(x, gate_value, kept_c[k], wgu[k], wd[k])
+            kept_c[k] = made[0]
+            kept_active[...] = made[1]
+            kept_dunits[:, :FF] = made[2]
+            kept_dunits[:, FF:] = made[3]
+            acc_up[k] += mm_tn(kept_x[k, :, :D], kept_dunits[...])
+            acc_down[k] += mm_tn(kept_active[...], kept_c[k])
+
+        def one_step(t):
+            i, r = t // (1 + early), lax.rem(t, 1 + early)
+
+            @pl.when(r == 0)
+            def _():
+                pick_plane(i)
+
+            @pl.when(r > 0)
+            def _():
+                expert(r - 1)
+
+            event(t)
+            act(t)
+
+        each(steps, one_step)
         stores = [
             pltpu.make_async_copy(acc_up, gate_up_grad, out_sem.at[0]),
             pltpu.make_async_copy(acc_down, down_grad, out_sem.at[1]),
         ]
         for copy in stores:
             copy.start()
-    each(max(events, steps), event, steps)
+    if steps < events:
+        each(events, event, steps)
     if early:
         for copy in stores:
             copy.wait()
@@ -1767,7 +1774,7 @@
         n_tp,
         n_exp,
         (tokens, w_query, w_pair, w_out, cotangent),
-        (gain1, gain2, router_t, routes),
+        (gain1, gain2, router_t, routes.T),
         prefix,
     )
     layer, dhidden, dhidden_low, router_part, norm2_part, all_rows = own_experts(

time: 452 us -> 436 us (0.965)
  Pallas kernels: 446 us -> 432 us
    pallas_call x1, Pallas kernels: 191 us -> 177 us  [backward(): pl.pallas_call(functools.partial(backward_kernel, n, n_exp, early, local_...]
where the time goes in v6:
time: 436 us
  Pallas kernels  432 us (99%)
    pallas_call x1, Pallas kernels, backward(): pl.pallas_call(functools.partial(backward_kernel, n, n_exp, early, local_...  177 us
    pallas_call x1, Pallas kernels, own_experts(): pl.pallas_call(functools.partial(own_experts_kernel, n, n_exp, local_expe...  87.1 us
    pallas_call x1, Pallas kernels, attention_forward(): pl.pallas_call(functools.partial(attention_forward_kernel, n, n_exp), out...  84.1 us
    pallas_call x1, Pallas kernels, expert_grads(): pl.pallas_call(functools.partial(expert_grads_kernel, n, n_exp, chunks, g...  83.7 us

profile of v6, /device:TPU:8, one launch (start us, length us, event | category | flops | bytes accessed | tf_op | source)
XLA Modules:
  0.0 435.8 jit_solution(8206484016423443523)
XLA Ops:
  1.3 1.9 copy.25
  3.2 84.1 %shard_map.195 = (f32[256,1024]{1,0:T(8,128)}, bf16[256,1152]{1,0:T(8,128)(2,1)}, bf16[8,256,1024]{2,1,0:T(8,128)(2,1)}, bf16[1024,1024]{1,0:T(8,128)(2,1)}, bf1...) custom-call(bf16[256,1024]{1,0:T(8,128)(2,1)} %refs_2_.1, ...), custom_call_target="tpu_custom_call" | custom-call | flops 2147483648 | bytes 314572800 | tf_op jit(solution)/shard_map/pallas_call | solution.py:488
  87.3 87.1 %shard_map.196 = (bf16[256,1024]{1,0:T(8,128)(2,1)}, f32[256,1024]{1,0:T(8,128)}, bf16[256,1024]{1,0:T(8,128)(2,1)}, f32[256,128]{1,0:T(8,128)}, f32[8,128]{1,0:T(8,128)}, /*index=5*/bf16[4,8,256,2176]{3,2,1,0:T(8,128)(2,1)}) custom-call(bf16[256,1152]{1,0:T(8,128)(2,1)} %get-tuple-element.39.ext, bf16[256,1024]{1,0:T(8,128)(2,1)} %cot.1, ...), custom_call_target="tpu_custom_call" | custom-call | flops 16106127360 | bytes 314572800 | tf_op jit(solution)/shard_map/pallas_call | solution.py:942
  174.5 177.0 %shard_map.197 = (f32[256,1024]{1,0:T(8,128)}, bf16[1024,768]{1,0:T(8,128)(2,1)}, f32[256,128]{1,0:T(8,128)}, f32[16,128]{1,0:T(8,128)}, bf16[4,8,256,2176]{3,2,...) custom-call(bf16[256,1024]{1,0:T(8,128)(2,1)} %get-tuple-element.42.refs_0_, ...), custom_call_target="tpu_custom_call", output_to_operand_aliasing={{4}: (15, {})} | custom-call | flops 4294967296 | bytes 314572800 | tf_op jit(solution)/shard_map/pallas_call | solution.py:1733
  351.4 0.0 copy-start
  351.4 83.7 %shard_map.198 = (f32[4,1024,1024]{2,1,0:T(8,128)}, f32[4,512,1024]{2,1,0:T(8,128)}, f32[1024,2,128]{2,1,0:T(2,128)}, f32[1024,256]{1,0:T(8,128)}, f32[256,1024]...) custom-call(bf16[4,8,256,2176]{3,2,1,0:T(8,128)(2,1)} %get-tuple-element.52.rows_all, ...), custom_call_target="tpu_custom_call" | custom-call | flops 64424509440 | bytes 314572800 | tf_op jit(solution)/shard_map/pallas_call | solution.py:1196
  435.2 0.0 copy-done
  435.2 0.6 slice_bitcast_fusion
Async XLA Ops:
  351.4 83.7 %copy-start = (f32[16,128]{1,0:T(8,128)S(1)}, f32[16,128]{1,0:T(8,128)}, u32[]{:S(2)}) copy-start(f32[16,128]{1,0:T(8,128)} %get-tuple-element.61) | copy-start | bytes 24580
